TPU v7x, 32 devices: a whole 2x2x4 slice. The times are simulated.
32 devices in a mesh: prow: 4 (over y, core), pcol: 8 (over z, x).
Axes of the slice: x: 2, y: 2, z: 4, core: 2. Of those that a mesh axis runs over, the one named last changes fastest.
Arguments:
- rhs: float32 [16, 8, 128, 512], P(None, 'pcol'), may hold values from -6 to 6
- coupling: bfloat16 [16, 8, 32, 4, 128, 128], P(None, 'pcol', None, 'prow'), may hold values from -0.0625 to 0.0625
- pattern: int32 [16, 8, 32, 4], P(None, 'pcol', None, 'prow'), may hold values 0 or 1
- inverse: bfloat16 [4, 4, 8, 8, 4, 128, 128], P(None, None, 'pcol', None, 'prow'), may hold values from -1 to 3
- trail_coupling: bfloat16 [32, 8, 32, 4, 128, 128], P(None, 'pcol', None, 'prow'), may hold values from -0.0625 to 0.0625
- trail_rhs: float32 [32, 8, 128, 512], P('prow', 'pcol'), may hold values from -6 to 6
Outputs:
- solution: bfloat16 [32, 4, 128, 512], P(None, 'prow')
- trail_out: float32 [32, 8, 128, 512], P('prow', 'pcol')
Inputs may be any that keep to these rules, and one draw needn't show every extreme that they name: `pattern`: each entry is 1 where the coupling tile is present and 0 where it is empty.
All inputs are finite; a program needn't handle non-finite values. No bound on the sum of `pattern` on one device may be relied on, other than what follows from the above.
Results may differ from a plain program's by a relative error of at most 0.004.
Values may be sent and summed in bfloat16 or wider, within the bound.
No kernel may reach another device: no remote copies, remote signals or barrier semaphores. Data moves between devices by JAX's collectives and lax.ppermute only.
A program may use at most 128 MiB of HBM per device.

v0:
```python
import jax
import jax.numpy as jnp
from jax import lax
from jax.sharding import PartitionSpec as P


def tile_product(factor, solved_rows):
    return jnp.einsum("acrs,csn->arn", factor, solved_rows, preferred_element_type=jnp.float32)


def body(rhs, coupling, pattern, inverse, trail_coupling, trail_rhs):
    panels = inverse.shape[0]
    row_count = inverse.shape[1]
    col_count = inverse.shape[3]
    window_rhs = rhs[:, 0]
    factor = coupling[:, 0, :, 0] * pattern[:, 0, :, 0, None, None].astype(jnp.bfloat16)
    trail_factor = trail_coupling[:, 0, :, 0]
    tile_size = window_rhs.shape[1]
    width = window_rhs.shape[2]
    solved = []
    for panel_index in range(panels):
        row_lower = panel_index * row_count
        row_upper = row_lower + row_count
        col_lower = panel_index * col_count
        reduced = window_rhs[row_lower:row_upper]
        if panel_index > 0:
            partial_value = tile_product(
                factor[row_lower:row_upper, :col_lower], jnp.concatenate(solved, 0)
            )
            reduced = reduced - lax.psum(partial_value, "prow")
        term_rows = jnp.einsum(
            "acrs,arn->csn",
            inverse[panel_index, :, 0, :, 0].astype(jnp.float32),
            reduced,
            precision=lax.Precision.HIGHEST,
        )
        flat_terms = term_rows.reshape(col_count * tile_size, width)
        share = lax.psum_scatter(flat_terms, "pcol", scatter_dimension=0, tiled=True).astype(
            jnp.bfloat16
        )
        current = lax.all_gather(share, "pcol", axis=0, tiled=True).reshape(
            col_count, tile_size, width
        )
        solved.append(current)
    known_tiles = jnp.concatenate(solved, 0)
    trail_sum = lax.psum_scatter(
        tile_product(trail_factor, known_tiles), "prow", scatter_dimension=0, tiled=True
    )
    trail_out = trail_rhs - trail_sum[:, None]
    return (known_tiles[:, None], trail_out)


def solution(mesh):
    placed = (
        P(None, "pcol", None, None),
        P(None, "pcol", None, "prow", None, None),
        P(None, "pcol", None, "prow"),
        P(None, None, "pcol", None, "prow", None, None),
        P(None, "pcol", None, "prow", None, None),
        P("prow", "pcol", None, None),
    )
    return jax.shard_map(
        body,
        mesh=mesh,
        in_specs=placed,
        out_specs=(P(None, "prow", None, None), P("prow", "pcol", None, None)),
        check_vma=False,
    )
```

profile of v0, /device:TPU:0, one launch (start us, length us, event | category | flops | bytes accessed | tf_op | source)
XLA Modules:
  0.0 701.8 jit_solution(4984877532847176495)
XLA Ops:
  7.2 0.0 reduce-scatter.6.cloned.1.call-start
  7.2 3.9 fusion.39
  11.2 1.6 copy.19
  12.8 4.4 convolution_bitcast_fusion
  17.2 0.0 reduce-scatter.6.cloned.1.call-update
  17.2 0.0 all-gather.5.cloned.1.call-start
  17.3 70.8 %reduce-scatter.6.cloned.1.call-done = f32[128,512]{1,0:T(8,128)} async-done(((f32[1024,512]{1,0:T(8,128)}), f32[128,512]{1,0:T(8,128)}) %reduce-scatter.6.cloned.1.call-update) | async-done | bytes 262160 | tf_op jit(solution)/shard_map/reduce_scatter | solution.py:38
  88.1 1.6 convert_element_type.27
  89.7 0.0 all-gather.5.cloned.1.call-update
  89.7 0.0 all-reduce.4.cloned.1.call-start
  89.8 40.1 %all-gather.5.cloned.1.call-done = bf16[1024,512]{1,0:T(8,128)(2,1)} async-done(((bf16[128,512]{1,0:T(8,128)(2,1)}), bf16[1024,512]{1,0:T(8,128)(2,1)}) %all-gather.5.cloned.1.call-update) | async-done | bytes 1048592 | tf_op jit(solution)/shard_map/all_gather | solution.py:41
  130.0 3.3 fusion.20
  133.2 0.0 all-reduce.4.cloned.1.call-update
  133.2 0.0 reduce-scatter.8.cloned.1.call-start
  133.3 1.6 copy.39
  134.9 33.3 %all-reduce.4.cloned.1.call-done = f32[4,128,512]{2,1,0:T(8,128)} async-done(((f32[4,128,512]{2,1,0:T(8,128)}), f32[4,128,512]{2,1,0:T(8,128)}) %all-reduce.4.cloned.1.call-update) | async-done | bytes 1048592 | tf_op jit(solution)/shard_map/psum | solution.py:30
  168.2 4.7 fusion.27
  173.0 0.0 reduce-scatter.8.cloned.1.call-update
  173.0 0.0 all-gather.7.cloned.1.call-start
  173.1 68.1 %reduce-scatter.8.cloned.1.call-done = f32[128,512]{1,0:T(8,128)} async-done(((f32[1024,512]{1,0:T(8,128)}), f32[128,512]{1,0:T(8,128)}) %reduce-scatter.8.cloned.1.call-update) | async-done | bytes 262160 | tf_op jit(solution)/shard_map/reduce_scatter | solution.py:38
  241.2 1.6 convert_element_type.30
  242.8 0.0 all-gather.7.cloned.1.call-update
  242.8 0.0 all-reduce.6.cloned.1.call-start
  242.9 40.3 %all-gather.7.cloned.1.call-done = bf16[1024,512]{1,0:T(8,128)(2,1)} async-done(((bf16[128,512]{1,0:T(8,128)(2,1)}), bf16[1024,512]{1,0:T(8,128)(2,1)}) %all-gather.7.cloned.1.call-update) | async-done | bytes 1048592 | tf_op jit(solution)/shard_map/all_gather | solution.py:41
  283.1 4.4 fusion.21
  287.6 0.0 all-reduce.6.cloned.1.call-update
  287.6 0.0 reduce-scatter.10.cloned.1.call-start
  287.7 0.7 copy.40
  288.3 34.3 %all-reduce.6.cloned.1.call-done = f32[4,128,512]{2,1,0:T(8,128)} async-done(((f32[4,128,512]{2,1,0:T(8,128)}), f32[4,128,512]{2,1,0:T(8,128)}) %all-reduce.6.cloned.1.call-update) | async-done | bytes 1048592 | tf_op jit(solution)/shard_map/psum | solution.py:30
  322.6 4.7 fusion.25
  327.4 0.0 reduce-scatter.10.cloned.1.call-update
  327.4 0.0 all-gather.9.cloned.1.call-start
  327.4 68.2 %reduce-scatter.10.cloned.1.call-done = f32[128,512]{1,0:T(8,128)} async-done(((f32[1024,512]{1,0:T(8,128)}), f32[128,512]{1,0:T(8,128)}) %reduce-scatter.10.cloned.1.call-update) | async-done | bytes 262160 | tf_op jit(solution)/shard_map/reduce_scatter | solution.py:38
  395.6 1.6 convert_element_type.31
  397.2 0.0 all-gather.9.cloned.1.call-update
  397.3 0.0 all-reduce.8.cloned.1.call-start
  397.3 40.2 %all-gather.9.cloned.1.call-done = bf16[1024,512]{1,0:T(8,128)(2,1)} async-done(((bf16[128,512]{1,0:T(8,128)(2,1)}), bf16[1024,512]{1,0:T(8,128)(2,1)}) %all-gather.9.cloned.1.call-update) | async-done | bytes 1048592 | tf_op jit(solution)/shard_map/all_gather | solution.py:41
  437.5 0.0 copy-done.2
  437.5 5.3 fusion.22
  442.8 0.0 all-reduce.8.cloned.1.call-update
  442.8 0.2 reduce-scatter.12.cloned.1.call-start
  443.1 0.7 copy.41
  443.7 34.0 %all-reduce.8.cloned.1.call-done = f32[4,128,512]{2,1,0:T(8,128)} async-done(((f32[4,128,512]{2,1,0:T(8,128)}), f32[4,128,512]{2,1,0:T(8,128)}) %all-reduce.8.cloned.1.call-update) | async-done | bytes 1048592 | tf_op jit(solution)/shard_map/psum | solution.py:30
  477.8 4.7 fusion.23
  482.5 0.0 reduce-scatter.12.cloned.1.call-update
  482.5 0.0 all-gather.11.cloned.1.call-start
  482.6 68.1 %reduce-scatter.12.cloned.1.call-done = f32[128,512]{1,0:T(8,128)} async-done(((f32[1024,512]{1,0:T(8,128)}), f32[128,512]{1,0:T(8,128)}) %reduce-scatter.12.cloned.1.call-update) | async-done | bytes 262160 | tf_op jit(solution)/shard_map/reduce_scatter | solution.py:38
  550.7 1.6 convert_element_type.32
  552.4 0.0 all-gather.11.cloned.1.call-update
  552.4 0.0 reduce-scatter.14.cloned.1.call-start
  552.4 0.7 copy.24
  553.1 1.6 copy.25
  554.7 2.0 copy.26
  556.7 0.0 copy-start.1
  556.8 36.2 %all-gather.11.cloned.1.call-done = bf16[1024,512]{1,0:T(8,128)(2,1)} async-done(((bf16[128,512]{1,0:T(8,128)(2,1)}), bf16[1024,512]{1,0:T(8,128)(2,1)}) %all-gather.11.cloned.1.call-update) | async-done | bytes 1048592 | tf_op jit(solution)/shard_map/all_gather | solution.py:41
  592.9 2.3 copy.27
  595.2 23.1 %fusion.9 = f32[32,128,512]{1,2,0:T(8,128)} fusion(bf16[32,1,32,1,128,128]{5,4,3,2,1,0:T(8,128)(2,1)} %param.10, bf16[8,128,512]{1,2,0:T(8,128)(2,1)} %copy.27, bf16[8,128,512]{1,2,0:T(8,128)(2,1)S(1)} %copy.26, bf16[8,128,512]{1,2,0:T(8,128)(2,1)S(1)} %copy.25, bf16[8,128,512]{1,2,0:T(8,128)(2,1)S(1)} %copy.24), kind=kOutput, calls=%fused_computation.11 | convolution fusion | flops 17196646400 | bytes 46137344 | tf_op jit(solution)/shard_map/acrs,csn->arn/dot_general | solution.py:8
  618.3 0.0 reduce-scatter.14.cloned.1.call-update
  618.3 1.9 copy.28
  620.2 3.7 fusion.35
  624.0 6.8 copy.29
  630.8 58.1 %reduce-scatter.14.cloned.1.call-done = f32[8,128,512]{1,2,0:T(8,128)} async-done(((f32[32,128,512]{1,2,0:T(8,128)}), f32[8,128,512]{1,2,0:T(8,128)}) %reduce-scatter.14.cloned.1.call-update) | async-done | bytes 2097168 | tf_op jit(solution)/shard_map/reduce_scatter | solution.py:46
  689.0 3.1 bitcast_subtract_fusion
  692.1 2.9 copy.30
  (10 shorter events, 0.0 us)
Async XLA Ops:
  7.2 80.9 %reduce-scatter.6.cloned.1.call-start = ((), (), s32[]{:S(2)}) async-start(), calls=%async_computation.5 | async-start | bytes 2359296 | tf_op jit(solution)/shard_map/reduce_scatter | solution.py:38
  11.1 78.6 %copy-start.4 = (s32[16,1,32,1]{2,3,1,0:T(1,128)S(1)}, s32[16,1,32,1]{2,3,1,0:T(1,128)}, u32[]{:S(2)}) copy-start(s32[16,1,32,1]{2,3,1,0:T(1,128)} %param.8) | copy-start | bytes 6148
  17.2 112.7 %all-gather.5.cloned.1.call-start = ((), (), s32[]{:S(2)}) async-start(), calls=%async_computation.6 | async-start | bytes 1179648 | tf_op jit(solution)/shard_map/all_gather | solution.py:41
  89.7 78.5 %all-reduce.4.cloned.1.call-start = ((), (), s32[]{:S(2)}) async-start(), calls=%async_computation.7 | async-start | bytes 2097152 | tf_op jit(solution)/shard_map/psum | solution.py:30
  133.2 108.0 %reduce-scatter.8.cloned.1.call-start = ((), (), s32[]{:S(2)}) async-start(), calls=%async_computation.8 | async-start | bytes 2359296 | tf_op jit(solution)/shard_map/reduce_scatter | solution.py:38
  173.0 110.1 %all-gather.7.cloned.1.call-start = ((), (), s32[]{:S(2)}) async-start(), calls=%async_computation.9 | async-start | bytes 1179648 | tf_op jit(solution)/shard_map/all_gather | solution.py:41
  242.8 79.8 %all-reduce.6.cloned.1.call-start = ((), (), s32[]{:S(2)}) async-start(), calls=%async_computation.10 | async-start | bytes 2097152 | tf_op jit(solution)/shard_map/psum | solution.py:30
  287.6 108.0 %reduce-scatter.10.cloned.1.call-start = ((), (), s32[]{:S(2)}) async-start(), calls=%async_computation.11 | async-start | bytes 2359296 | tf_op jit(solution)/shard_map/reduce_scatter | solution.py:38
  288.3 149.2 %copy-start.2 = (bf16[1024,512]{1,0:T(8,128)(2,1)S(1)}, bf16[1024,512]{1,0:T(8,128)(2,1)}, u32[]{:S(2)}) copy-start(bf16[1024,512]{1,0:T(8,128)(2,1)} %all-gather.5.cloned.1.call-done) | copy-start | bytes 3145732
  327.4 110.1 %all-gather.9.cloned.1.call-start = ((), (), s32[]{:S(2)}) async-start(), calls=%async_computation.12 | async-start | bytes 1179648 | tf_op jit(solution)/shard_map/all_gather | solution.py:41
  397.3 80.5 %all-reduce.8.cloned.1.call-start = ((), (), s32[]{:S(2)}) async-start(), calls=%async_computation.13 | async-start | bytes 2097152 | tf_op jit(solution)/shard_map/psum | solution.py:30
  442.8 107.9 %reduce-scatter.12.cloned.1.call-start = ((), (), s32[]{:S(2)}) async-start(), calls=%async_computation.14 | async-start | bytes 2359296 | tf_op jit(solution)/shard_map/reduce_scatter | solution.py:38
  443.7 108.7 %copy-start.3 = (bf16[1024,512]{1,0:T(8,128)(2,1)S(1)}, bf16[1024,512]{1,0:T(8,128)(2,1)}, u32[]{:S(2)}) copy-start(bf16[1024,512]{1,0:T(8,128)(2,1)} %all-gather.5.cloned.1.call-done) | copy-start | bytes 3145732
  482.5 110.4 %all-gather.11.cloned.1.call-start = ((), (), s32[]{:S(2)}) async-start(), calls=%async_computation.15 | async-start | bytes 1179648 | tf_op jit(solution)/shard_map/all_gather | solution.py:41
  552.4 136.6 %reduce-scatter.14.cloned.1.call-start = ((), (), s32[]{:S(2)}) async-start(), calls=%async_computation.16 | async-start | bytes 10485760 | tf_op jit(solution)/shard_map/reduce_scatter | solution.py:46
  554.7 63.6 %copy-start = (bf16[8,128,512]{1,2,0:T(8,128)(2,1)}, bf16[8,128,512]{1,2,0:T(8,128)(2,1)S(1)}, u32[]{:S(2)}) copy-start(bf16[8,128,512]{1,2,0:T(8,128)(2,1)S(1)} %copy.25) | copy-start | bytes 3145732
  556.7 61.6 %copy-start.1 = (bf16[8,128,512]{1,2,0:T(8,128)(2,1)}, bf16[8,128,512]{1,2,0:T(8,128)(2,1)S(1)}, u32[]{:S(2)}) copy-start(bf16[8,128,512]{1,2,0:T(8,128)(2,1)S(1)} %copy.26) | copy-start | bytes 3145732
Sparse Core Ops, SparseCore 0:
  17.3 70.6 reduce-scatter.5
  90.8 39.1 all-gather.4
  133.4 34.8 all-reduce.3
  173.1 68.0 reduce-scatter.7
  244.0 39.1 all-gather.6
  287.7 34.8 all-reduce.5
  327.5 68.0 reduce-scatter.9
  398.3 39.1 all-gather.8
  442.9 34.7 all-reduce.7
  482.7 68.0 reduce-scatter.11
  553.7 39.2 all-gather.10
  618.4 70.4 reduce-scatter.13
where the time goes:
time: 703 us; the launch traced here: 702 us
  waiting for transfers between devices  592 us (84%)
  matrix products  54.7 us (8%)
  local copies, waits for them, and re-layouts  26.7 us (4%)
  between operations  14.3 us (2%)
  other arithmetic  13.4 us (2%)
    reduce_scatter x4, waiting for transfers between devices, body(): lax.psum_scatter(flat_terms, 'pcol', scatter_dimension=0, tiled=True)  275 us
    all_gather x4, waiting for transfers between devices, body(): lax.all_gather(share, 'pcol', axis=0, tiled=True)  157 us
    psum x3, waiting for transfers between devices, body(): reduced = reduced - lax.psum(partial_value, 'prow')  102 us
    reduce_scatter x1, waiting for transfers between devices, body(): lax.psum_scatter(tile_product(trail_factor, known_tiles), 'prow', scatter...  58.1 us
    dot_general x4, matrix products, tile_product(): jnp.einsum('acrs,csn->arn', factor, solved_rows, preferred_element_type=j...  36.1 us
    dot_general x4, matrix products, body(): jnp.einsum('acrs,arn->csn', inverse[panel_index, :, 0, :, 0].astype(jnp.f...  18.6 us
    unnamed x17, local copies, waits for them, and re-layouts  14.6 us
  transfers between devices with their start and end apart: 12, of which 12 were waited for; matrix products, arithmetic and copies ran while one was open for 3% of the time, Pallas kernels for 0%

commit v1 on v0

v1 whole, which is shorter than its diff:
```python
import functools

import jax
import jax.numpy as jnp
from jax import lax
from jax.experimental import pallas as pl
from jax.experimental.pallas import tpu as pltpu
from jax.sharding import PartitionSpec as P

SPLITS = 2
LAG = 5
F32 = jnp.float32
BF16 = jnp.bfloat16
CODE = jnp.int16
EXTRA = 16
TOP = 32000.0
MIB = 1024 * 1024
HBM = pl.BlockSpec(memory_space=pltpu.HBM)
SMEM = pl.BlockSpec(memory_space=pltpu.SMEM)
VMEM = pl.BlockSpec(memory_space=pltpu.VMEM)
ANY = pl.BlockSpec(memory_space=pl.ANY)


def swap(value, axis, count, mask):
    return lax.ppermute(value, axis, [(s, s ^ mask) for s in range(count)])


def shape(dims, dtype):
    return jax.ShapeDtypeStruct(tuple(dims), dtype)


def whole(array):
    return pl.BlockSpec(array.shape, lambda *_: (0,) * array.ndim)


def cost(flops, size):
    return pl.CostEstimate(flops=int(flops), bytes_accessed=int(size), transcendentals=0)


def flat_rows(value):
    return value.reshape(-1, value.shape[-1])


def exponent_of(value):
    top = jnp.max(jnp.max(jnp.abs(value), axis=0, keepdims=True), axis=1, keepdims=True)
    return jnp.ceil(jnp.log2(jnp.maximum(top, 1e-30)))


def encode(value, exponent):
    return jnp.round(value * (TOP * jnp.exp2(-exponent))).astype(jnp.int32).astype(CODE)


def put_exponent(ref, count, exponent):
    ref[count : count + EXTRA] = jnp.broadcast_to(exponent, (EXTRA, ref.shape[1])).astype(jnp.int32).astype(CODE)


def decode(ref):
    count = ref.shape[0] - EXTRA
    tail = ref[count : count + EXTRA].astype(jnp.int32).astype(F32)
    factor = jnp.exp2(tail[:1, :1]) * (1.0 / TOP)
    return ref[:count].astype(jnp.int32).astype(F32) * factor


def tile_matrix(block, scale=None):
    lines = []
    for a in range(block.shape[0]):
        tiles = [block[a, c] for c in range(block.shape[1])]
        if scale is not None:
            tiles = [t * scale(a, c) for c, t in enumerate(tiles)]
        lines.append(jnp.concatenate(tiles, axis=1))
    return jnp.concatenate(lines, axis=0)


def coupling_kernel(panel, inner, refs):
    own_ref, pattern_ref, coupling_ref = refs[:3]
    xs, pieces = refs[3 : 2 + panel], refs[2 + panel : 2 + panel + inner]
    u_ref, newest_ref, blocks, sems = refs[-4:]
    me = own_ref[0]
    row_count, col_count, tile, _ = blocks.shape[1:]
    copies = []
    for e in range(panel):
        source = coupling_ref.at[pl.ds(panel * row_count, row_count), 0, pl.ds(e * col_count, col_count), 0]
        copies.append(pltpu.make_async_copy(source, blocks.at[e], sems.at[e]))
        copies[e].start()
    for d in range(inner):
        newest_ref[:, me ^ d] = pieces[d][...]
    total = None
    for e in range(panel):
        copies[e].wait()
        x = xs[e][...] if e < panel - 1 else flat_rows(newest_ref[...])

        def scale(a, c, e=e):
            m = pattern_ref[panel * row_count + a, e * col_count + c].astype(F32)
            return jnp.full((tile, tile), m, F32).astype(BF16)

        part = jnp.dot(tile_matrix(blocks.at[e], scale), x, preferred_element_type=F32)
        total = part if total is None else total + part
    u_ref[...] = total


def merge_kernel(coded, refs):
    value_ref, arrived, sum_ref, out_ref = refs[0], refs[1:-2], refs[-2], refs[-1]
    total = value_ref[...]
    for r in arrived:
        total = total + (decode(r) if coded else r[...])
    sum_ref[...] = total
    count = total.shape[0]
    exponent = exponent_of(total)
    out_ref[:count] = encode(total, exponent)
    put_exponent(out_ref, count, exponent)


def inverse_kernel(panel, half, updates, inner, refs):
    own_ref, rhs_ref, inverse_ref = refs[:3]
    rest, (rhs_block, block, sems) = refs[3:-3], refs[-3:]
    row_count, _, width = rhs_block.shape
    source = rhs_ref.at[pl.ds(panel * row_count, row_count), 0, :, pl.ds(half * width, width)]
    get_rhs = pltpu.make_async_copy(source, rhs_block, sems.at[0])
    get_rhs.start()
    get_block = pltpu.make_async_copy(inverse_ref.at[panel, :, 0, :, 0], block, sems.at[1])
    get_block.start()
    get_rhs.wait()
    y = flat_rows(rhs_block[...])
    if updates:
        y = y - rest[0][...]
        for r in rest[1:updates]:
            y = y - decode(r)
        rest = rest[updates:]
    kept_ref, sent, terms_ref = rest[0], rest[1:-1], rest[-1]
    me = own_ref[0]
    high = y.astype(BF16)
    low = (y - high.astype(F32)).astype(BF16)
    get_block.wait()
    out = lax.dot_general(
        tile_matrix(block),
        jnp.concatenate([high, low], axis=1),
        (((0,), (0,)), ((), ())),
        preferred_element_type=F32,
    )
    terms = out[:, :width] + out[:, width:]
    exponent = exponent_of(terms)
    terms_ref[...] = terms.reshape(terms_ref.shape)
    outer, _, rows, _ = terms_ref.shape
    for o in range(outer):
        kept_ref[o] = terms_ref[o, me]
        for d, ref in enumerate(sent):
            ref[o * rows : (o + 1) * rows] = encode(terms_ref[o, me ^ (d + 1)], exponent)
    for ref in sent:
        put_exponent(ref, outer * rows, exponent)


def fold_kernel(inner, outer, refs):
    own_ref, kept_ref, arrived = refs[0], refs[1], refs[2 : 1 + inner]
    mine_ref, sent, total_ref = refs[-1 - outer], refs[-outer:-1], refs[-1]
    me = own_ref[0]
    total = flat_rows(kept_ref[...])
    for r in arrived:
        total = total + decode(r)
    exponent = exponent_of(total)
    total_ref[...] = total.reshape(total_ref.shape)
    rows = total_ref.shape[1]
    mine_ref[...] = total_ref[me]
    for d, ref in enumerate(sent):
        ref[:rows] = encode(total_ref[me ^ (d + 1)], exponent)
        put_exponent(ref, rows, exponent)


def finish_kernel(refs):
    total = refs[0][...]
    for r in refs[1:-1]:
        total = total + decode(r)
    refs[-1][...] = total.astype(BF16)


def order_kernel(refs):
    me, out_ref = refs[0][0], refs[-1]
    for d, piece in enumerate(refs[1:-1]):
        out_ref[me ^ d] = piece[...]


def order_last_kernel(refs):
    me, out_ref = refs[0][0], refs[-1]
    for d, piece in enumerate(refs[1:-1]):
        out_ref[:, me ^ d] = piece[...]


def trail_kernel(groups, add, refs):
    blocks, rest, out_ref = refs[1 : 1 + groups], refs[1 + groups : -1], refs[-1]
    count = (len(rest) - int(add)) // groups
    total = flat_rows(rest[-1][...]) if add else None
    for g in range(groups):
        xs = [rest[g * count + i][...] for i in range(count)]
        x = jnp.concatenate(xs, axis=1) if count > 1 else xs[0]
        part = jnp.dot(tile_matrix(blocks[g]), x, preferred_element_type=F32)
        total = part if total is None else total + part
    out_ref[...] = total.astype(out_ref.dtype).reshape(out_ref.shape)


def add_kernel(refs):
    total = refs[0][...]
    for r in refs[1:-1]:
        total = total + r[...].astype(F32)
    refs[-1][...] = total.astype(refs[-1].dtype)


def join_kernel(count, refs):
    out_ref = refs[-1]
    halves = refs[:count]
    width = halves[0].shape[-1]
    for i, r in enumerate(halves):
        out_ref[:, i * width : (i + 1) * width] = r[...]


def subtract_kernel(count, refs):
    total = refs[0][...]
    for r in refs[1:count]:
        total = total - r[...].astype(F32)
    refs[-1][...] = total


def make_body(nr, nc):
    cores = 2 if nr % 2 == 0 else 1
    lines = nr // cores
    outer = min(nc, 4)
    inner = nc // outer

    def body(rhs, coupling, pattern, inverse, trail_coupling, trail_rhs):
        rhs = pltpu.with_memory_space_constraint(rhs, pltpu.HBM)
        coupling = pltpu.with_memory_space_constraint(coupling, pltpu.HBM)
        inverse = pltpu.with_memory_space_constraint(inverse, pltpu.HBM)
        row_index = lax.axis_index("prow")
        col_index = lax.axis_index("pcol")
        core, line = row_index % cores, row_index // cores
        inner_own = jnp.reshape(col_index % inner, (1,))
        outer_own = jnp.reshape(col_index // inner, (1,))
        panels, row_count, _, col_count = inverse.shape[:4]
        tile, width = rhs.shape[2:]
        part = width // SPLITS
        rows = col_count * tile // nc
        reduced_rows = row_count * tile
        solved_dims = (col_count * tile, part)
        trail_tiles = trail_coupling.shape[0]
        group = trail_tiles // nr
        step_tiles = min(4, group)
        pattern_flat = pattern.reshape(pattern.shape[0], pattern.shape[2])
        last = [None]

        def call(kernel, operands, specs, outs, name, flops=0, size=0, scratch=(), limit=12):
            operands, specs = list(operands), list(specs)
            extra = 0
            if last[0] is not None:
                operands.append(last[0])
                specs.append(ANY)
                extra = 1
            count = len(operands)

            def run(*refs):
                kernel(refs[: count - extra] + refs[count:])

            result = pl.pallas_call(
                run,
                in_specs=specs,
                out_specs=[VMEM] * len(outs),
                out_shape=outs,
                scratch_shapes=list(scratch),
                compiler_params=pltpu.CompilerParams(vmem_limit_bytes=limit * MIB),
                cost_estimate=cost(1, 1),
                name=name,
            )(*operands)
            last[0] = result[0]
            return result

        def couple(k, h, older, pieces):
            outs = [shape((reduced_rows, part), F32), shape((outer, inner, rows, part), BF16)]
            return call(
                functools.partial(coupling_kernel, k, inner),
                [inner_own, pattern_flat, coupling] + older + pieces,
                [SMEM, SMEM, HBM] + [VMEM] * len(older + pieces),
                outs,
                "coupling",
                2 * reduced_rows * k * col_count * tile * part,
                2 * k * reduced_rows * col_count * tile,
                scratch=[
                    pltpu.VMEM((k, row_count, col_count, tile, tile), BF16),
                    pltpu.SemaphoreType.DMA((k,)),
                ],
                limit=24,
            )

        def merge(value, arrived, coded):
            outs = [shape(value.shape, F32), shape((value.shape[0] + EXTRA, part), CODE)]
            return call(
                functools.partial(merge_kernel, coded),
                [value] + arrived,
                [VMEM] * (1 + len(arrived)),
                outs,
                "merge",
                size=10 * value.size,
            )

        def invert(k, h, update):
            outs = [shape((outer, rows, part), F32)]
            outs += [shape((outer * rows + EXTRA, part), CODE)] * (inner - 1)
            return call(
                functools.partial(inverse_kernel, k, h, len(update), inner),
                [inner_own, rhs, inverse] + update,
                [SMEM, HBM, HBM] + [VMEM] * len(update),
                outs,
                "inverse",
                4 * reduced_rows * col_count * tile * part,
                2 * reduced_rows * col_count * tile,
                scratch=[
                    pltpu.VMEM((outer, inner, rows, part), F32),
                    pltpu.VMEM((row_count, tile, part), F32),
                    pltpu.VMEM((row_count, col_count, tile, tile), BF16),
                    pltpu.SemaphoreType.DMA((2,)),
                ],
                limit=24,
            )

        def fold(kept, arrived):
            return call(
                functools.partial(fold_kernel, inner, outer),
                [outer_own, kept] + arrived,
                [SMEM] + [VMEM] * inner,
                [shape((rows, part), F32)] + [shape((rows + EXTRA, part), CODE)] * (outer - 1),
                "fold",
                size=8 * outer * rows * part,
                scratch=[pltpu.VMEM((outer, rows, part), F32)],
            )

        def finish(kept, arrived):
            return call(
                finish_kernel, [kept] + arrived, [VMEM] * outer, [shape((rows, part), BF16)], "finish", size=4 * outer * rows * part
            )[0]

        def order(pieces):
            return call(
                order_kernel,
                [outer_own] + pieces,
                [SMEM] + [VMEM] * outer,
                [shape((outer, rows, part), BF16)],
                "order",
                size=4 * outer * rows * part,
            )[0]

        def order_last(pieces):
            return call(
                order_last_kernel,
                [inner_own] + pieces,
                [SMEM] + [VMEM] * inner,
                [shape((outer, inner, rows, part), BF16)],
                "order_last",
                size=4 * nc * rows * part,
            )[0]

        def trail_product(first, count, xs, added, rank, columns, dtype, chain=False):
            steps = (trail_tiles if rank is None else group) // step_tiles
            base = jnp.reshape(0 if rank is None else rank * steps, (1,)).astype(jnp.int32)
            wide = width if columns is None else part
            column = 0 if columns is None else columns
            operands = [trail_coupling] * count + xs + ([] if added is None else [added])
            specs = [
                pl.BlockSpec(
                    (step_tiles, None, col_count, None, tile, tile),
                    functools.partial(lambda g, i, b: (b[0] + i, 0, g, 0, 0, 0), first + g),
                )
                for g in range(count)
            ] + [whole(v) for v in xs]
            if added is not None:
                specs.append(pl.BlockSpec((step_tiles, tile, wide), lambda i, b: (b[0] + i, 0, column)))
            extra = int(chain)
            if chain:
                operands.append(last[0])
                specs.append(ANY)
            total = 1 + len(operands)

            def run(*refs):
                trail_kernel(count, added is not None, refs[: total - extra] + refs[total:])

            result = pl.pallas_call(
                run,
                grid_spec=pltpu.PrefetchScalarGridSpec(
                    num_scalar_prefetch=1,
                    grid=(steps,),
                    in_specs=specs,
                    out_specs=pl.BlockSpec((step_tiles, tile, wide), lambda i, b: (i, 0, 0)),
                ),
                out_shape=shape((steps * step_tiles, tile, wide), dtype),
                compiler_params=pltpu.CompilerParams(vmem_limit_bytes=36 * MIB),
                cost_estimate=cost(
                    2 * steps * step_tiles * tile * count * col_count * tile * wide,
                    steps * step_tiles * tile * (2 * count * col_count * tile + 4 * wide),
                ),
                name="trail",
            )(base, *operands)
            if chain:
                last[0] = result
            return result

        def add(values, dtype, name):
            return call(
                add_kernel, values, [VMEM] * len(values), [shape(values[0].shape, dtype)], name, size=10 * values[0].size
            )[0]

        def join(known, first, count):
            operands, specs = [], []
            for h in range(SPLITS):
                if count > 1:
                    operands.append(jnp.stack([solved[h][first + i] for i in range(count)]))
                else:
                    operands.append(solved[h][first][None])
                specs.append(pl.BlockSpec((None,) + solved_dims, lambda i: (i, 0, 0)))
            aliases = {}
            if known is not None:
                operands.append(known)
                specs.append(ANY)
                aliases = {SPLITS: 0}
            return pl.pallas_call(
                lambda *refs: join_kernel(SPLITS, refs),
                grid=(count,),
                in_specs=specs,
                out_specs=pl.BlockSpec((None, solved_dims[0], width), lambda i: (first + i, 0, 0)),
                out_shape=shape((panels, solved_dims[0], width), BF16),
                input_output_aliases=aliases,
                compiler_params=pltpu.CompilerParams(vmem_limit_bytes=36 * MIB),
                cost_estimate=cost(0, 4 * count * solved_dims[0] * width),
                name="join",
            )(*operands)

        def subtract(out, h, values):
            operands = [trail_rhs] + values
            half = pl.BlockSpec((group, None, tile, part), lambda *_: (0, 0, 0, h))
            specs = [half] + [whole(v) for v in values]
            aliases = {}
            if out is not None:
                aliases = {len(operands): 0}
                operands.append(out)
                specs.append(ANY)
            count = 1 + len(values)
            return pl.pallas_call(
                lambda *refs: subtract_kernel(count, refs),
                grid=(1,),
                in_specs=specs,
                out_specs=half,
                out_shape=shape(trail_rhs.shape, F32),
                input_output_aliases=aliases,
                compiler_params=pltpu.CompilerParams(vmem_limit_bytes=36 * MIB),
                cost_estimate=cost(0, 12 * group * tile * part),
                name="subtract",
            )(*operands)

        solved = [[] for _ in range(SPLITS)]
        trail_sums = [None] * SPLITS
        trail = [None]

        def chain_of(h):
            pieces = None
            for k in range(panels):
                update = []
                if k > 0:
                    u, newest = couple(k, h, solved[h], pieces)
                    solved[h].append(newest.reshape(solved_dims))
                    arrived = [swap(u, "prow", nr, d) for d in range(1, cores)]
                    yield
                    update, message = merge(u, arrived, False)
                    d = 1
                    while d < lines:
                        arrived = swap(message, "prow", nr, d * cores)
                        yield
                        d *= 2
                        if d < lines:
                            update, message = merge(update, [arrived], True)
                    update = [update] + ([arrived] if lines > 1 else [])
                kept, *sent = invert(k, h, update)
                arrived = [swap(v, "pcol", nc, d + 1) for d, v in enumerate(sent)]
                yield
                kept, *sent = fold(kept, arrived)
                arrived = [swap(v, "pcol", nc, (d + 1) * inner) for d, v in enumerate(sent)]
                yield
                mine = finish(kept, arrived)
                arrived = [swap(mine, "pcol", nc, d * inner) for d in range(1, outer)]
                yield
                column = order([mine] + arrived)
                pieces = [column] + [swap(column, "pcol", nc, d) for d in range(1, inner)]
                yield
            solved[h].append(order_last(pieces).reshape(solved_dims))

            def rows_of(rank, dtype):
                return trail_product(panels - 1, 1, [solved[h][-1]], trail[0], rank, h, dtype, True)

            received = []
            for e in list(range(1, lines)) + [0]:
                there = line ^ e
                sent = [rows_of(there * cores + (core ^ d), BF16) for d in range(1, cores)]
                total = rows_of(there * cores + core, F32)
                arrived = [swap(v, "prow", nr, d + 1) for d, v in enumerate(sent)]
                if e == 0:
                    trail_sums[h] = [total] + arrived + received
                else:
                    received.append(swap(add([total] + arrived, BF16, "add"), "prow", nr, e * cores))
                yield

        chains = [chain_of(h) for h in range(SPLITS)]
        alive = [True] * SPLITS
        step = 0
        while any(alive):
            for h in range(SPLITS):
                if alive[h] and step >= h * LAG:
                    alive[h] = next(chains[h], "end") != "end"
            step += 1
            if trail[0] is None and all(len(s) == panels - 1 for s in solved):
                done = panels - 1
                xs = [solved[h][e] for e in range(done) for h in range(SPLITS)]
                trail[0] = trail_product(0, done, xs, None, None, None, F32)

        known = join(None, 0, panels - 1)
        known = join(known, panels - 1, 1)
        trail_out = None
        for h in range(SPLITS):
            trail_out = subtract(trail_out, h, trail_sums[h])
        return known.reshape(panels * col_count, 1, tile, width), trail_out

    return body


def solution(mesh):
    placed = (
        P(None, "pcol", None, None),
        P(None, "pcol", None, "prow", None, None),
        P(None, "pcol", None, "prow"),
        P(None, None, "pcol", None, "prow", None, None),
        P(None, "pcol", None, "prow", None, None),
        P("prow", "pcol", None, None),
    )
    return jax.shard_map(
        make_body(mesh.shape["prow"], mesh.shape["pcol"]),
        mesh=mesh,
        in_specs=placed,
        out_specs=(P(None, "prow", None, None), P("prow", "pcol", None, None)),
        check_vma=False,
    )
```

time: 703 us -> 313 us (0.45)
  waiting for transfers between devices: 592 us -> 96.7 us
  starting transfers between devices: 0.68 us -> 118 us
  Pallas kernels: 0 us -> 87 us
  matrix products: 54.7 us -> 0 us
  local copies, waits for them, and re-layouts: 26.7 us -> 8.47 us
  other arithmetic: 13.4 us -> 0.35 us
  between operations: 14.3 us -> 1.39 us
    reduce_scatter x5 -> x0, waiting for transfers between devices: 333 us -> none  [the longest x4 275 us: body(): lax.psum_scatter(flat_terms, 'pcol', scatter_dimension=0, tiled=True)]
    all_gather x4 -> x0, waiting for transfers between devices: 157 us -> none  [body(): lax.all_gather(share, 'pcol', axis=0, tiled=True)]
    ppermute x0 -> x82, starting transfers between devices: none -> 118 us  [swap(): return lax.ppermute(value, axis, [(s, s ^ mask) for s in range(count)])]
    psum x3 -> x0, waiting for transfers between devices: 102 us -> none  [body(): reduced = reduced - lax.psum(partial_value, 'prow')]
    ppermute x0 -> x82, waiting for transfers between devices: none -> 96.7 us  [swap(): return lax.ppermute(value, axis, [(s, s ^ mask) for s in range(count)])]
    pallas_call x0 -> x61, Pallas kernels: none -> 87 us  [the longest x48 45.7 us: call(): pl.pallas_call(run, in_specs=specs, out_specs=[VMEM] * len(outs), out_sha...]
    dot_general x8 -> x0, matrix products: 54.7 us -> none  [the longest x4 36.1 us: tile_product(): jnp.einsum('acrs,csn->arn', factor, solved_rows, preferred_element_type=j...]
    unnamed x17 -> x26, local copies, waits for them, and re-layouts: 14.6 us -> 8.47 us
  transfers between devices with their start and end apart: 12 -> 82, of which waited for: 12 -> 44; matrix products, arithmetic and copies ran while one was open for 3% -> 0% of each run, Pallas kernels for 0% -> 22%
where the time goes in v1:
time: 313 us; the launch traced here: 312 us
  starting transfers between devices  118 us (38%)
  waiting for transfers between devices  96.7 us (31%)
  Pallas kernels  87 us (28%)
  local copies, waits for them, and re-layouts  8.47 us (3%)
    ppermute x82, starting transfers between devices, swap(): return lax.ppermute(value, axis, [(s, s ^ mask) for s in range(count)])  118 us
    ppermute x82, waiting for transfers between devices, swap(): return lax.ppermute(value, axis, [(s, s ^ mask) for s in range(count)])  96.7 us
    pallas_call x48, Pallas kernels, call(): pl.pallas_call(run, in_specs=specs, out_specs=[VMEM] * len(outs), out_sha...  45.7 us
    pallas_call x9, Pallas kernels, trail_product(): pl.pallas_call(run, grid_spec=pltpu.PrefetchScalarGridSpec(num_scalar_pre...  35.7 us
    unnamed x26, local copies, waits for them, and re-layouts  8.47 us
  transfers between devices with their start and end apart: 82, of which 44 were waited for; matrix products, arithmetic and copies ran while one was open for 0% of the time, Pallas kernels for 22%

profile of v1, /device:TPU:0, one launch (start us, length us, event | category | flops | bytes accessed | tf_op | source)
XLA Modules:
  0.0 311.9 jit_solution(9656106997215760325)
XLA Ops:
  0.6 2.3 inverse.8
  3.0 3.0 collective-permute-start
  6.0 6.5 %collective-permute-done.refs_2_ = s16[528,256]{1,0:T(8,128)(2,1)S(1)} collective-permute-done((s16[528,256]{1,0:T(8,128)(2,1)S(1)}, s16[528,256]{1,0:T(8,128)(2,1)S(1)}, u32[]{:S(2)}, u32[]{:S(2)}) %collective-permute-start) | collective-permute-done | bytes 270368 | tf_op jit(solution)/shard_map/ppermute | solution.py:25
  14.6 2.6 collective-permute-start.2
  17.8 3.7 %collective-permute-done.2.refs_2_ = s16[144,256]{1,0:T(8,128)(2,1)S(1)} collective-permute-done((s16[144,256]{1,0:T(8,128)(2,1)S(1)}, s16[144,256]{1,0:T(8,128)(2,1)S(1)}, u32[]{:S(2)}, u32[]{:S(2)}) %collective-permute-start.2) | collective-permute-done | bytes 73760 | tf_op jit(solution)/shard_map/ppermute | solution.py:25
  25.5 2.5 collective-permute-start.6
  28.9 2.7 collective-permute-done.6.refs_4_
  33.2 4.9 %collective-permute-done.7.refs_4_ = bf16[4,128,256]{2,1,0:T(8,128)(2,1)S(1)} collective-permute-done((bf16[4,128,256]{2,1,0:T(8,128)(2,1)S(1)}, bf16[4,128,256]{2,1,0:T(8,128)(2,1)S(1)}, u32[]{:S(2)}, u32[]{:S(2)}) %collective-permute-start.7) | collective-permute-done | bytes 262176 | tf_op jit(solution)/shard_map/ppermute | solution.py:25
  38.1 2.4 coupling.6
  44.2 2.3 inverse.9
  48.1 3.1 %collective-permute-done.9.refs_4_ = s16[528,256]{1,0:T(8,128)(2,1)S(1)} collective-permute-done((s16[528,256]{1,0:T(8,128)(2,1)S(1)}, s16[528,256]{1,0:T(8,128)(2,1)S(1)}, u32[]{:S(2)}, u32[]{:S(2)}) %collective-permute-start.9) | collective-permute-done | bytes 270368 | tf_op jit(solution)/shard_map/ppermute | solution.py:25
  51.2 2.3 inverse.10
  55.4 3.0 collective-permute-start.16
  61.6 3.0 collective-permute-start.13
  66.3 2.8 collective-permute-start.22
  71.5 3.2 %collective-permute-start.18 = (bf16[128,256]{1,0:T(8,128)(2,1)S(1)}, bf16[128,256]{1,0:T(8,128)(2,1)S(1)}, u32[]{:S(2)}, u32[]{:S(2)}) collective-permute-start(bf16[128,256]{1,0:T(8,128)(2,1)S(1)} %finish.10.refs_5_.refs_1_), channel_id=1, source_target_pairs={{0,2},{1,3},{2,0},{3,1},{4,6},{5,7},{6,4},{7,5},{8,10},{9,11},{10,... | collective-permute-start | bytes 196616 | tf_op jit(solution)/shard_map/ppermute | solution.py:25
  77.8 3.0 collective-permute-start.25
  82.6 3.0 collective-permute-start.24
  86.8 2.4 coupling.7
  89.9 2.9 coupling.8
  96.4 6.2 %collective-permute-done.29.refs_4_ = s16[528,256]{1,0:T(8,128)(2,1)S(1)} collective-permute-done((s16[528,256]{1,0:T(8,128)(2,1)S(1)}, s16[528,256]{1,0:T(8,128)(2,1)S(1)}, u32[]{:S(2)}, u32[]{:S(2)}) %collective-permute-start.29) | collective-permute-done | bytes 270368 | tf_op jit(solution)/shard_map/ppermute | solution.py:25
  102.6 2.3 inverse.11
  104.9 2.1 collective-permute-start.31
  107.9 2.3 inverse.12
  110.3 2.1 collective-permute-start.30
  115.2 2.4 collective-permute-start.37
  121.0 2.4 collective-permute-start.34
  125.5 2.4 collective-permute-start.43
  129.5 4.4 %collective-permute-start.38 = (bf16[128,256]{1,0:T(8,128)(2,1)S(1)}, bf16[128,256]{1,0:T(8,128)(2,1)S(1)}, u32[]{:S(2)}, u32[]{:S(2)}) collective-permute-start(bf16[128,256]{1,0:T(8,128)(2,1)S(1)} %finish.12.refs_5_.refs_1_), channel_id=1, source_target_pairs={{0,2},{1,3},{2,0},{3,1},{4,6},{5,7},{6,4},{7,5},{8,10},{9,11},{10,... | collective-permute-start | bytes 196616 | tf_op jit(solution)/shard_map/ppermute | solution.py:25
  136.4 2.3 collective-permute-start.45
  140.5 2.6 collective-permute-start.44
  144.2 3.1 coupling.9
  147.5 3.9 %coupling.10 = (f32[512,256]{1,0:T(8,128)S(1)}, bf16[4,2,128,256]{3,2,1,0:T(8,128)(2,1)S(1)}) custom-call(s32[1]{0:T(128)} %bitcast.refs_0_, s32[16,32]{1,0:T(8,128)S(1)} %bitcast.60, bf16[16,1,32,1,128,128]{5,4,3,2,1,0:T(8,128)(2,1)} %refs_2_.27, bf16[1024,256]{1,0:T(8,128)(2,1)S(1)} %bitcast.39, bf16[1024,256]{1,0:T(8,128)(2,1)S(1)} %bitcast.46, ...), custom_call_target="tpu_custom_call" | custom-call | flops 1 | bytes 1 | tf_op jit(solution)/shard_map/coupling/pallas_call | solution.py:260
  154.8 6.8 %collective-permute-done.49.refs_4_ = s16[528,256]{1,0:T(8,128)(2,1)S(1)} collective-permute-done((s16[528,256]{1,0:T(8,128)(2,1)S(1)}, s16[528,256]{1,0:T(8,128)(2,1)S(1)}, u32[]{:S(2)}, u32[]{:S(2)}) %collective-permute-start.49) | collective-permute-done | bytes 270368 | tf_op jit(solution)/shard_map/ppermute | solution.py:25
  161.5 2.3 inverse.13
  166.4 2.3 inverse.14
  168.7 2.1 collective-permute-start.50
  174.0 2.1 collective-permute-start.57
  179.8 2.1 collective-permute-start.54
  182.2 2.1 collective-permute-start.62
  186.4 2.6 collective-permute-done.53.refs_2_
  189.1 3.0 collective-permute-done.62.refs_3_
  202.9 4.7 %coupling.11 = (f32[512,256]{1,0:T(8,128)}, bf16[4,2,128,256]{3,2,1,0:T(8,128)(2,1)S(1)}) custom-call(s32[1]{0:T(128)} %bitcast.refs_0_, s32[16,32]{1,0:T(8,128)S(1)} %bitcast.61, bf16[16,1,32,1,128,128]{5,4,3,2,1,0:T(8,128)(2,1)} %refs_2_.27, bf16[1024,256]{1,0:T(8,128)(2,1)S(1)} %bitcast.43, bf16[1024,256]{1,0:T(8,128)(2,1)S(1)} %bitcast.49, ...), custom_call_target="tpu_custom_call" | custom-call | flops 1 | bytes 1 | tf_op jit(solution)/shard_map/coupling/pallas_call | solution.py:260
  207.6 16.8 %trail.9.refs_3_ = f32[32,128,512]{2,1,0:T(8,128)S(1)} custom-call(s32[1]{0:T(128)} %constant.45.clone.1.refs_0_, bf16[32,1,32,1,128,128]{5,4,3,2,1,0:T(8,128)(2,1)} %refs_1_.33, bf16[32,1,32,1,128,128]{5,4,3,2,1,0:T(8,128)(2,1)} %refs_1_.33, bf16[32,1,32,1,128,128]{5,4,3,2,1,0:T(8,128)(2,1)} %refs_1_.33, bf16[1024,256]{1,0:T(8,128)(2,1)S(1)} %bitcast.40, ...), custom_call_target="tpu_custom_call" | custom-call | flops 12884901888 | bytes 33554432 | tf_op jit(solution)/shard_map/trail/pallas_call | solution.py:381
  224.5 3.6 %trail.10.refs_4_ = bf16[8,128,256]{2,1,0:T(8,128)(2,1)S(1)} custom-call(s32[1]{0:T(128)} %bitcast.12.refs_0_, bf16[32,1,32,1,128,128]{5,4,3,2,1,0:T(8,128)(2,1)} %refs_1_.33, bf16[1024,256]{1,0:T(8,128)(2,1)S(1)} %bitcast.28, f32[32,128,512]{2,1,0:T(8,128)S(1)} %trail.9.refs_3_, bf16[4,2,128,256]{3,2,1,0:T(8,128)(2,1)S(1)} %order_last.2.refs_4_), custom_call_target="tpu_custom_call" | custom-call | flops 536870912 | bytes 3145728 | tf_op jit(solution)/shard_map/trail/pallas_call | solution.py:381
  228.7 3.4 %copy-done.1 = f32[32,128,512]{2,1,0:T(8,128)S(1)} copy-done((f32[32,128,512]{2,1,0:T(8,128)S(1)}, f32[32,128,512]{2,1,0:T(8,128)}, u32[]{:S(2)}) %copy-start.1) | copy-done | bytes 8388632
  232.1 2.1 trail.11.refs_0_.refs_2_
  235.4 2.1 merge.11
  239.2 3.4 %copy-done.2 = f32[32,128,512]{2,1,0:T(8,128)S(1)} copy-done((f32[32,128,512]{2,1,0:T(8,128)S(1)}, f32[32,128,512]{2,1,0:T(8,128)}, u32[]{:S(2)}) %copy-start.2) | copy-done | bytes 8388632
  242.6 2.1 trail.12.refs_4_
  244.8 2.3 trail.13.refs_5_.refs_1_
  247.1 3.0 inverse.15
  251.5 6.9 %collective-permute-done.69.refs_2_ = s16[528,256]{1,0:T(8,128)(2,1)S(1)} collective-permute-done((s16[528,256]{1,0:T(8,128)(2,1)S(1)}, s16[528,256]{1,0:T(8,128)(2,1)S(1)}, u32[]{:S(2)}, u32[]{:S(2)}) %collective-permute-start.69) | collective-permute-done | bytes 270368 | tf_op jit(solution)/shard_map/ppermute | solution.py:25
  258.7 2.5 collective-permute-start.71
  263.1 2.8 collective-permute-done.71.refs_2_
  273.4 2.7 collective-permute-done.75.refs_4_
  277.5 5.1 %collective-permute-done.76.refs_2_ = bf16[4,128,256]{2,1,0:T(8,128)(2,1)S(1)} collective-permute-done((bf16[4,128,256]{2,1,0:T(8,128)(2,1)S(1)}, bf16[4,128,256]{2,1,0:T(8,128)(2,1)S(1)}, u32[]{:S(2)}, u32[]{:S(2)}) %collective-permute-start.76) | collective-permute-done | bytes 262176 | tf_op jit(solution)/shard_map/ppermute | solution.py:25
  282.7 2.2 trail.14.refs_4_
  286.6 2.1 trail.15.refs_0_.refs_2_
  288.9 2.2 trail.16.refs_4_
  293.4 2.1 join.2.refs_2_
  295.5 4.7 %collective-permute-done.81.refs_3_ = bf16[8,128,256]{2,1,0:T(8,128)(2,1)S(1)} collective-permute-done((bf16[8,128,256]{2,1,0:T(8,128)(2,1)S(1)}, bf16[8,128,256]{2,1,0:T(8,128)(2,1)S(1)}, u32[]{:S(2)}, u32[]{:S(2)}) %collective-permute-start.81) | collective-permute-done | bytes 524320 | tf_op jit(solution)/shard_map/ppermute | solution.py:25
  302.5 2.1 trail.17.refs_1_
  304.7 5.9 %collective-permute-done.79.refs_3_ = bf16[8,128,256]{2,1,0:T(8,128)(2,1)S(1)} collective-permute-done((bf16[8,128,256]{2,1,0:T(8,128)(2,1)S(1)}, bf16[8,128,256]{2,1,0:T(8,128)(2,1)S(1)}, u32[]{:S(2)}, u32[]{:S(2)}) %collective-permute-start.79) | collective-permute-done | bytes 524320 | tf_op jit(solution)/shard_map/ppermute | solution.py:25
  (190 shorter events, 100.1 us)
Async XLA Ops:
  3.0 9.5 %collective-permute-start = (s16[528,256]{1,0:T(8,128)(2,1)S(1)}, s16[528,256]{1,0:T(8,128)(2,1)S(1)}, u32[]{:S(2)}, u32[]{:S(2)}) collective-permute-start(s16[528,256]{1,0:T(8,128)(2,1)S(1)} %get-tuple-element.75), channel_id=1, source_target_pairs={{0,1},{1,0},{2,3},{3,2},{4,5},{5,4},{6,7},{7,6},{8,9},{9,8},{10,11... | collective-permute-start | bytes 811016 | tf_op jit(solution)/shard_map/ppermute | solution.py:25
  14.6 6.9 %collective-permute-start.2 = (s16[144,256]{1,0:T(8,128)(2,1)S(1)}, s16[144,256]{1,0:T(8,128)(2,1)S(1)}, u32[]{:S(2)}, u32[]{:S(2)}) collective-permute-start(s16[144,256]{1,0:T(8,128)(2,1)S(1)} %get-tuple-element.78), channel_id=1, source_target_pairs={{0,4},{1,5},{2,6},{3,7},{4,0},{5,1},{6,2},{7,3},{8,12},{9,13},{10,... | collective-permute-start | bytes 221192 | tf_op jit(solution)/shard_map/ppermute | solution.py:25
  17.2 6.3 %collective-permute-start.3 = (s16[144,256]{1,0:T(8,128)(2,1)S(1)}, s16[144,256]{1,0:T(8,128)(2,1)S(1)}, u32[]{:S(2)}, u32[]{:S(2)}) collective-permute-start(s16[144,256]{1,0:T(8,128)(2,1)S(1)} %get-tuple-element.79), channel_id=1, source_target_pairs={{0,6},{1,7},{2,4},{3,5},{4,2},{5,3},{6,0},{7,1},{8,14},{9,15},{10,... | collective-permute-start | bytes 221192 | tf_op jit(solution)/shard_map/ppermute | solution.py:25
  25.5 6.1 %collective-permute-start.6 = (bf16[128,256]{1,0:T(8,128)(2,1)S(1)}, bf16[128,256]{1,0:T(8,128)(2,1)S(1)}, u32[]{:S(2)}, u32[]{:S(2)}) collective-permute-start(bf16[128,256]{1,0:T(8,128)(2,1)S(1)} %finish.8.refs_1_.refs_5_), channel_id=1, source_target_pairs={{0,6},{1,7},{2,4},{3,5},{4,2},{5,3},{6,0},{7,1},{8,14},{9,15},{10,... | collective-permute-start | bytes 196616 | tf_op jit(solution)/shard_map/ppermute | solution.py:25
  31.6 6.4 %collective-permute-start.7 = (bf16[4,128,256]{2,1,0:T(8,128)(2,1)S(1)}, bf16[4,128,256]{2,1,0:T(8,128)(2,1)S(1)}, u32[]{:S(2)}, u32[]{:S(2)}) collective-permute-start(bf16[4,128,256]{2,1,0:T(8,128)(2,1)S(1)} %order.8.refs_3_.refs_5_), channel_id=1, source_target_pairs={{0,1},{1,0},{2,3},{3,2},{4,5},{5,4},{6,7},{7,6},{8,9},{9,8},{10,11... | collective-permute-start | bytes 786440 | tf_op jit(solution)/shard_map/ppermute | solution.py:25
  42.7 8.6 %collective-permute-start.9 = (s16[528,256]{1,0:T(8,128)(2,1)S(1)}, s16[528,256]{1,0:T(8,128)(2,1)S(1)}, u32[]{:S(2)}, u32[]{:S(2)}) collective-permute-start(s16[528,256]{1,0:T(8,128)(2,1)S(1)} %get-tuple-element.83), channel_id=1, source_target_pairs={{0,16},{8,24},{16,0},{24,8},{1,17},{9,25},{17,1},{25,9},{2,18},{10... | collective-permute-start | bytes 811016 | tf_op jit(solution)/shard_map/ppermute | solution.py:25
  46.5 8.6 %collective-permute-start.11 = (s16[528,256]{1,0:T(8,128)(2,1)S(1)}, s16[528,256]{1,0:T(8,128)(2,1)S(1)}, u32[]{:S(2)}, u32[]{:S(2)}) collective-permute-start(s16[528,256]{1,0:T(8,128)(2,1)S(1)} %get-tuple-element.87), channel_id=1, source_target_pairs={{0,1},{1,0},{2,3},{3,2},{4,5},{5,4},{6,7},{7,6},{8,9},{9,8},{10,11... | collective-permute-start | bytes 811016 | tf_op jit(solution)/shard_map/ppermute | solution.py:25
  53.5 7.8 %collective-permute-start.10 = (s16[528,256]{1,0:T(8,128)(2,1)S(1)}, s16[528,256]{1,0:T(8,128)(2,1)S(1)}, u32[]{:S(2)}, u32[]{:S(2)}) collective-permute-start(s16[528,256]{1,0:T(8,128)(2,1)S(1)} %get-tuple-element.86), channel_id=1, source_target_pairs={{0,1},{1,0},{2,3},{3,2},{4,5},{5,4},{6,7},{7,6},{8,9},{9,8},{10,11... | collective-permute-start | bytes 811016 | tf_op jit(solution)/shard_map/ppermute | solution.py:25
  55.4 9.3 %collective-permute-start.15 = (s16[144,256]{1,0:T(8,128)(2,1)S(1)}, s16[144,256]{1,0:T(8,128)(2,1)S(1)}, u32[]{:S(2)}, u32[]{:S(2)}) collective-permute-start(s16[144,256]{1,0:T(8,128)(2,1)S(1)} %get-tuple-element.93), channel_id=1, source_target_pairs={{0,2},{1,3},{2,0},{3,1},{4,6},{5,7},{6,4},{7,5},{8,10},{9,11},{10,... | collective-permute-start | bytes 221192 | tf_op jit(solution)/shard_map/ppermute | solution.py:25
  55.4 10.6 %collective-permute-start.16 = (s16[144,256]{1,0:T(8,128)(2,1)S(1)}, s16[144,256]{1,0:T(8,128)(2,1)S(1)}, u32[]{:S(2)}, u32[]{:S(2)}) collective-permute-start(s16[144,256]{1,0:T(8,128)(2,1)S(1)} %get-tuple-element.94), channel_id=1, source_target_pairs={{0,4},{1,5},{2,6},{3,7},{4,0},{5,1},{6,2},{7,3},{8,12},{9,13},{10,... | collective-permute-start | bytes 221192 | tf_op jit(solution)/shard_map/ppermute | solution.py:25
  58.4 7.6 %collective-permute-start.17 = (s16[144,256]{1,0:T(8,128)(2,1)S(1)}, s16[144,256]{1,0:T(8,128)(2,1)S(1)}, u32[]{:S(2)}, u32[]{:S(2)}) collective-permute-start(s16[144,256]{1,0:T(8,128)(2,1)S(1)} %get-tuple-element.95), channel_id=1, source_target_pairs={{0,6},{1,7},{2,4},{3,5},{4,2},{5,3},{6,0},{7,1},{8,14},{9,15},{10,... | collective-permute-start | bytes 221192 | tf_op jit(solution)/shard_map/ppermute | solution.py:25
  61.5 7.6 %collective-permute-start.12 = (s16[144,256]{1,0:T(8,128)(2,1)S(1)}, s16[144,256]{1,0:T(8,128)(2,1)S(1)}, u32[]{:S(2)}, u32[]{:S(2)}) collective-permute-start(s16[144,256]{1,0:T(8,128)(2,1)S(1)} %get-tuple-element.90), channel_id=1, source_target_pairs={{0,2},{1,3},{2,0},{3,1},{4,6},{5,7},{6,4},{7,5},{8,10},{9,11},{10,... | collective-permute-start | bytes 221192 | tf_op jit(solution)/shard_map/ppermute | solution.py:25
  61.6 9.7 %collective-permute-start.13 = (s16[144,256]{1,0:T(8,128)(2,1)S(1)}, s16[144,256]{1,0:T(8,128)(2,1)S(1)}, u32[]{:S(2)}, u32[]{:S(2)}) collective-permute-start(s16[144,256]{1,0:T(8,128)(2,1)S(1)} %get-tuple-element.91), channel_id=1, source_target_pairs={{0,4},{1,5},{2,6},{3,7},{4,0},{5,1},{6,2},{7,3},{8,12},{9,13},{10,... | collective-permute-start | bytes 221192 | tf_op jit(solution)/shard_map/ppermute | solution.py:25
  64.6 6.8 %collective-permute-start.14 = (s16[144,256]{1,0:T(8,128)(2,1)S(1)}, s16[144,256]{1,0:T(8,128)(2,1)S(1)}, u32[]{:S(2)}, u32[]{:S(2)}) collective-permute-start(s16[144,256]{1,0:T(8,128)(2,1)S(1)} %get-tuple-element.92), channel_id=1, source_target_pairs={{0,6},{1,7},{2,4},{3,5},{4,2},{5,3},{6,0},{7,1},{8,14},{9,15},{10,... | collective-permute-start | bytes 221192 | tf_op jit(solution)/shard_map/ppermute | solution.py:25
  66.1 10.3 %collective-permute-start.21 = (bf16[128,256]{1,0:T(8,128)(2,1)S(1)}, bf16[128,256]{1,0:T(8,128)(2,1)S(1)}, u32[]{:S(2)}, u32[]{:S(2)}) collective-permute-start(bf16[128,256]{1,0:T(8,128)(2,1)S(1)} %finish.9.refs_4_.refs_1_), channel_id=1, source_target_pairs={{0,2},{1,3},{2,0},{3,1},{4,6},{5,7},{6,4},{7,5},{8,10},{9,11},{10,... | collective-permute-start | bytes 196616 | tf_op jit(solution)/shard_map/ppermute | solution.py:25
  66.3 11.5 %collective-permute-start.22 = (bf16[128,256]{1,0:T(8,128)(2,1)S(1)}, bf16[128,256]{1,0:T(8,128)(2,1)S(1)}, u32[]{:S(2)}, u32[]{:S(2)}) collective-permute-start(bf16[128,256]{1,0:T(8,128)(2,1)S(1)} %finish.9.refs_4_.refs_1_), channel_id=1, source_target_pairs={{0,4},{1,5},{2,6},{3,7},{4,0},{5,1},{6,2},{7,3},{8,12},{9,13},{10,... | collective-permute-start | bytes 196616 | tf_op jit(solution)/shard_map/ppermute | solution.py:25
  69.2 8.6 %collective-permute-start.23 = (bf16[128,256]{1,0:T(8,128)(2,1)S(1)}, bf16[128,256]{1,0:T(8,128)(2,1)S(1)}, u32[]{:S(2)}, u32[]{:S(2)}) collective-permute-start(bf16[128,256]{1,0:T(8,128)(2,1)S(1)} %finish.9.refs_4_.refs_1_), channel_id=1, source_target_pairs={{0,6},{1,7},{2,4},{3,5},{4,2},{5,3},{6,0},{7,1},{8,14},{9,15},{10,... | collective-permute-start | bytes 196616 | tf_op jit(solution)/shard_map/ppermute | solution.py:25
  71.5 9.4 %collective-permute-start.18 = (bf16[128,256]{1,0:T(8,128)(2,1)S(1)}, bf16[128,256]{1,0:T(8,128)(2,1)S(1)}, u32[]{:S(2)}, u32[]{:S(2)}) collective-permute-start(bf16[128,256]{1,0:T(8,128)(2,1)S(1)} %finish.10.refs_5_.refs_1_), channel_id=1, source_target_pairs={{0,2},{1,3},{2,0},{3,1},{4,6},{5,7},{6,4},{7,5},{8,10},{9,11},{10,... | collective-permute-start | bytes 196616 | tf_op jit(solution)/shard_map/ppermute | solution.py:25
  74.6 6.2 %collective-permute-start.19 = (bf16[128,256]{1,0:T(8,128)(2,1)S(1)}, bf16[128,256]{1,0:T(8,128)(2,1)S(1)}, u32[]{:S(2)}, u32[]{:S(2)}) collective-permute-start(bf16[128,256]{1,0:T(8,128)(2,1)S(1)} %finish.10.refs_5_.refs_1_), channel_id=1, source_target_pairs={{0,4},{1,5},{2,6},{3,7},{4,0},{5,1},{6,2},{7,3},{8,12},{9,13},{10,... | collective-permute-start | bytes 196616 | tf_op jit(solution)/shard_map/ppermute | solution.py:25
  76.4 6.2 %collective-permute-start.20 = (bf16[128,256]{1,0:T(8,128)(2,1)S(1)}, bf16[128,256]{1,0:T(8,128)(2,1)S(1)}, u32[]{:S(2)}, u32[]{:S(2)}) collective-permute-start(bf16[128,256]{1,0:T(8,128)(2,1)S(1)} %finish.10.refs_5_.refs_1_), channel_id=1, source_target_pairs={{0,6},{1,7},{2,4},{3,5},{4,2},{5,3},{6,0},{7,1},{8,14},{9,15},{10,... | collective-permute-start | bytes 196616 | tf_op jit(solution)/shard_map/ppermute | solution.py:25
  77.8 9.0 %collective-permute-start.25 = (bf16[4,128,256]{2,1,0:T(8,128)(2,1)S(1)}, bf16[4,128,256]{2,1,0:T(8,128)(2,1)S(1)}, u32[]{:S(2)}, u32[]{:S(2)}) collective-permute-start(bf16[4,128,256]{2,1,0:T(8,128)(2,1)S(1)} %order.9.refs_5_.refs_3_), channel_id=1, source_target_pairs={{0,1},{1,0},{2,3},{3,2},{4,5},{5,4},{6,7},{7,6},{8,9},{9,8},{10,11... | collective-permute-start | bytes 786440 | tf_op jit(solution)/shard_map/ppermute | solution.py:25
  82.6 7.4 %collective-permute-start.24 = (bf16[4,128,256]{2,1,0:T(8,128)(2,1)S(1)}, bf16[4,128,256]{2,1,0:T(8,128)(2,1)S(1)}, u32[]{:S(2)}, u32[]{:S(2)}) collective-permute-start(bf16[4,128,256]{2,1,0:T(8,128)(2,1)S(1)} %order.10.refs_5_.refs_4_), channel_id=1, source_target_pairs={{0,1},{1,0},{2,3},{3,2},{4,5},{5,4},{6,7},{7,6},{8,9},{9,8},{10,11... | collective-permute-start | bytes 786440 | tf_op jit(solution)/shard_map/ppermute | solution.py:25
  93.2 9.3 %collective-permute-start.29 = (s16[528,256]{1,0:T(8,128)(2,1)S(1)}, s16[528,256]{1,0:T(8,128)(2,1)S(1)}, u32[]{:S(2)}, u32[]{:S(2)}) collective-permute-start(s16[528,256]{1,0:T(8,128)(2,1)S(1)} %get-tuple-element.102), channel_id=1, source_target_pairs={{0,16},{8,24},{16,0},{24,8},{1,17},{9,25},{17,1},{25,9},{2,18},{10... | collective-permute-start | bytes 811016 | tf_op jit(solution)/shard_map/ppermute | solution.py:25
  95.1 12.8 %collective-permute-start.28 = (s16[528,256]{1,0:T(8,128)(2,1)S(1)}, s16[528,256]{1,0:T(8,128)(2,1)S(1)}, u32[]{:S(2)}, u32[]{:S(2)}) collective-permute-start(s16[528,256]{1,0:T(8,128)(2,1)S(1)} %get-tuple-element.101), channel_id=1, source_target_pairs={{0,16},{8,24},{16,0},{24,8},{1,17},{9,25},{17,1},{25,9},{2,18},{10... | collective-permute-start | bytes 811016 | tf_op jit(solution)/shard_map/ppermute | solution.py:25
  104.9 8.0 %collective-permute-start.31 = (s16[528,256]{1,0:T(8,128)(2,1)S(1)}, s16[528,256]{1,0:T(8,128)(2,1)S(1)}, u32[]{:S(2)}, u32[]{:S(2)}) collective-permute-start(s16[528,256]{1,0:T(8,128)(2,1)S(1)} %get-tuple-element.106), channel_id=1, source_target_pairs={{0,1},{1,0},{2,3},{3,2},{4,5},{5,4},{6,7},{7,6},{8,9},{9,8},{10,11... | collective-permute-start | bytes 811016 | tf_op jit(solution)/shard_map/ppermute | solution.py:25
  110.3 8.4 %collective-permute-start.30 = (s16[528,256]{1,0:T(8,128)(2,1)S(1)}, s16[528,256]{1,0:T(8,128)(2,1)S(1)}, u32[]{:S(2)}, u32[]{:S(2)}) collective-permute-start(s16[528,256]{1,0:T(8,128)(2,1)S(1)} %get-tuple-element.105), channel_id=1, source_target_pairs={{0,1},{1,0},{2,3},{3,2},{4,5},{5,4},{6,7},{7,6},{8,9},{9,8},{10,11... | collective-permute-start | bytes 811016 | tf_op jit(solution)/shard_map/ppermute | solution.py:25
  113.1 7.8 %collective-permute-start.35 = (s16[144,256]{1,0:T(8,128)(2,1)S(1)}, s16[144,256]{1,0:T(8,128)(2,1)S(1)}, u32[]{:S(2)}, u32[]{:S(2)}) collective-permute-start(s16[144,256]{1,0:T(8,128)(2,1)S(1)} %get-tuple-element.112), channel_id=1, source_target_pairs={{0,2},{1,3},{2,0},{3,1},{4,6},{5,7},{6,4},{7,5},{8,10},{9,11},{10,... | collective-permute-start | bytes 221192 | tf_op jit(solution)/shard_map/ppermute | solution.py:25
  114.1 9.3 %collective-permute-start.36 = (s16[144,256]{1,0:T(8,128)(2,1)S(1)}, s16[144,256]{1,0:T(8,128)(2,1)S(1)}, u32[]{:S(2)}, u32[]{:S(2)}) collective-permute-start(s16[144,256]{1,0:T(8,128)(2,1)S(1)} %get-tuple-element.113), channel_id=1, source_target_pairs={{0,4},{1,5},{2,6},{3,7},{4,0},{5,1},{6,2},{7,3},{8,12},{9,13},{10,... | collective-permute-start | bytes 221192 | tf_op jit(solution)/shard_map/ppermute | solution.py:25
  115.2 8.2 %collective-permute-start.37 = (s16[144,256]{1,0:T(8,128)(2,1)S(1)}, s16[144,256]{1,0:T(8,128)(2,1)S(1)}, u32[]{:S(2)}, u32[]{:S(2)}) collective-permute-start(s16[144,256]{1,0:T(8,128)(2,1)S(1)} %get-tuple-element.114), channel_id=1, source_target_pairs={{0,6},{1,7},{2,4},{3,5},{4,2},{5,3},{6,0},{7,1},{8,14},{9,15},{10,... | collective-permute-start | bytes 221192 | tf_op jit(solution)/shard_map/ppermute | solution.py:25
  118.9 6.6 %collective-permute-start.32 = (s16[144,256]{1,0:T(8,128)(2,1)S(1)}, s16[144,256]{1,0:T(8,128)(2,1)S(1)}, u32[]{:S(2)}, u32[]{:S(2)}) collective-permute-start(s16[144,256]{1,0:T(8,128)(2,1)S(1)} %get-tuple-element.109), channel_id=1, source_target_pairs={{0,2},{1,3},{2,0},{3,1},{4,6},{5,7},{6,4},{7,5},{8,10},{9,11},{10,... | collective-permute-start | bytes 221192 | tf_op jit(solution)/shard_map/ppermute | solution.py:25
  119.8 9.6 %collective-permute-start.33 = (s16[144,256]{1,0:T(8,128)(2,1)S(1)}, s16[144,256]{1,0:T(8,128)(2,1)S(1)}, u32[]{:S(2)}, u32[]{:S(2)}) collective-permute-start(s16[144,256]{1,0:T(8,128)(2,1)S(1)} %get-tuple-element.110), channel_id=1, source_target_pairs={{0,4},{1,5},{2,6},{3,7},{4,0},{5,1},{6,2},{7,3},{8,12},{9,13},{10,... | collective-permute-start | bytes 221192 | tf_op jit(solution)/shard_map/ppermute | solution.py:25
  121.0 8.5 %collective-permute-start.34 = (s16[144,256]{1,0:T(8,128)(2,1)S(1)}, s16[144,256]{1,0:T(8,128)(2,1)S(1)}, u32[]{:S(2)}, u32[]{:S(2)}) collective-permute-start(s16[144,256]{1,0:T(8,128)(2,1)S(1)} %get-tuple-element.111), channel_id=1, source_target_pairs={{0,6},{1,7},{2,4},{3,5},{4,2},{5,3},{6,0},{7,1},{8,14},{9,15},{10,... | collective-permute-start | bytes 221192 | tf_op jit(solution)/shard_map/ppermute | solution.py:25
  123.5 10.8 %collective-permute-start.41 = (bf16[128,256]{1,0:T(8,128)(2,1)S(1)}, bf16[128,256]{1,0:T(8,128)(2,1)S(1)}, u32[]{:S(2)}, u32[]{:S(2)}) collective-permute-start(bf16[128,256]{1,0:T(8,128)(2,1)S(1)} %finish.11.refs_4_.refs_1_), channel_id=1, source_target_pairs={{0,2},{1,3},{2,0},{3,1},{4,6},{5,7},{6,4},{7,5},{8,10},{9,11},{10,... | collective-permute-start | bytes 196616 | tf_op jit(solution)/shard_map/ppermute | solution.py:25
  124.3 12.1 %collective-permute-start.42 = (bf16[128,256]{1,0:T(8,128)(2,1)S(1)}, bf16[128,256]{1,0:T(8,128)(2,1)S(1)}, u32[]{:S(2)}, u32[]{:S(2)}) collective-permute-start(bf16[128,256]{1,0:T(8,128)(2,1)S(1)} %finish.11.refs_4_.refs_1_), channel_id=1, source_target_pairs={{0,4},{1,5},{2,6},{3,7},{4,0},{5,1},{6,2},{7,3},{8,12},{9,13},{10,... | collective-permute-start | bytes 196616 | tf_op jit(solution)/shard_map/ppermute | solution.py:25
  125.5 10.9 %collective-permute-start.43 = (bf16[128,256]{1,0:T(8,128)(2,1)S(1)}, bf16[128,256]{1,0:T(8,128)(2,1)S(1)}, u32[]{:S(2)}, u32[]{:S(2)}) collective-permute-start(bf16[128,256]{1,0:T(8,128)(2,1)S(1)} %finish.11.refs_4_.refs_1_), channel_id=1, source_target_pairs={{0,6},{1,7},{2,4},{3,5},{4,2},{5,3},{6,0},{7,1},{8,14},{9,15},{10,... | collective-permute-start | bytes 196616 | tf_op jit(solution)/shard_map/ppermute | solution.py:25
  129.5 9.2 %collective-permute-start.38 = (bf16[128,256]{1,0:T(8,128)(2,1)S(1)}, bf16[128,256]{1,0:T(8,128)(2,1)S(1)}, u32[]{:S(2)}, u32[]{:S(2)}) collective-permute-start(bf16[128,256]{1,0:T(8,128)(2,1)S(1)} %finish.12.refs_5_.refs_1_), channel_id=1, source_target_pairs={{0,2},{1,3},{2,0},{3,1},{4,6},{5,7},{6,4},{7,5},{8,10},{9,11},{10,... | collective-permute-start | bytes 196616 | tf_op jit(solution)/shard_map/ppermute | solution.py:25
  134.3 6.2 %collective-permute-start.40 = (bf16[128,256]{1,0:T(8,128)(2,1)S(1)}, bf16[128,256]{1,0:T(8,128)(2,1)S(1)}, u32[]{:S(2)}, u32[]{:S(2)}) collective-permute-start(bf16[128,256]{1,0:T(8,128)(2,1)S(1)} %finish.12.refs_5_.refs_1_), channel_id=1, source_target_pairs={{0,6},{1,7},{2,4},{3,5},{4,2},{5,3},{6,0},{7,1},{8,14},{9,15},{10,... | collective-permute-start | bytes 196616 | tf_op jit(solution)/shard_map/ppermute | solution.py:25
  136.4 7.8 %collective-permute-start.45 = (bf16[4,128,256]{2,1,0:T(8,128)(2,1)S(1)}, bf16[4,128,256]{2,1,0:T(8,128)(2,1)S(1)}, u32[]{:S(2)}, u32[]{:S(2)}) collective-permute-start(bf16[4,128,256]{2,1,0:T(8,128)(2,1)S(1)} %order.11.refs_5_.refs_4_), channel_id=1, source_target_pairs={{0,1},{1,0},{2,3},{3,2},{4,5},{5,4},{6,7},{7,6},{8,9},{9,8},{10,11... | collective-permute-start | bytes 786440 | tf_op jit(solution)/shard_map/ppermute | solution.py:25
  140.5 6.9 %collective-permute-start.44 = (bf16[4,128,256]{2,1,0:T(8,128)(2,1)S(1)}, bf16[4,128,256]{2,1,0:T(8,128)(2,1)S(1)}, u32[]{:S(2)}, u32[]{:S(2)}) collective-permute-start(bf16[4,128,256]{2,1,0:T(8,128)(2,1)S(1)} %order.12.refs_6_.refs_5_), channel_id=1, source_target_pairs={{0,1},{1,0},{2,3},{3,2},{4,5},{5,4},{6,7},{7,6},{8,9},{9,8},{10,11... | collective-permute-start | bytes 786440 | tf_op jit(solution)/shard_map/ppermute | solution.py:25
  152.1 9.4 %collective-permute-start.49 = (s16[528,256]{1,0:T(8,128)(2,1)S(1)}, s16[528,256]{1,0:T(8,128)(2,1)S(1)}, u32[]{:S(2)}, u32[]{:S(2)}) collective-permute-start(s16[528,256]{1,0:T(8,128)(2,1)S(1)} %get-tuple-element.121), channel_id=1, source_target_pairs={{0,16},{8,24},{16,0},{24,8},{1,17},{9,25},{17,1},{25,9},{2,18},{10... | collective-permute-start | bytes 811016 | tf_op jit(solution)/shard_map/ppermute | solution.py:25
  153.6 12.8 %collective-permute-start.48 = (s16[528,256]{1,0:T(8,128)(2,1)S(1)}, s16[528,256]{1,0:T(8,128)(2,1)S(1)}, u32[]{:S(2)}, u32[]{:S(2)}) collective-permute-start(s16[528,256]{1,0:T(8,128)(2,1)S(1)} %get-tuple-element.120), channel_id=1, source_target_pairs={{0,16},{8,24},{16,0},{24,8},{1,17},{9,25},{17,1},{25,9},{2,18},{10... | collective-permute-start | bytes 811016 | tf_op jit(solution)/shard_map/ppermute | solution.py:25
  163.8 7.6 %collective-permute-start.51 = (s16[528,256]{1,0:T(8,128)(2,1)S(1)}, s16[528,256]{1,0:T(8,128)(2,1)S(1)}, u32[]{:S(2)}, u32[]{:S(2)}) collective-permute-start(s16[528,256]{1,0:T(8,128)(2,1)S(1)} %get-tuple-element.125), channel_id=1, source_target_pairs={{0,1},{1,0},{2,3},{3,2},{4,5},{5,4},{6,7},{7,6},{8,9},{9,8},{10,11... | collective-permute-start | bytes 811016 | tf_op jit(solution)/shard_map/ppermute | solution.py:25
  168.7 8.4 %collective-permute-start.50 = (s16[528,256]{1,0:T(8,128)(2,1)S(1)}, s16[528,256]{1,0:T(8,128)(2,1)S(1)}, u32[]{:S(2)}, u32[]{:S(2)}) collective-permute-start(s16[528,256]{1,0:T(8,128)(2,1)S(1)} %get-tuple-element.124), channel_id=1, source_target_pairs={{0,1},{1,0},{2,3},{3,2},{4,5},{5,4},{6,7},{7,6},{8,9},{9,8},{10,11... | collective-permute-start | bytes 811016 | tf_op jit(solution)/shard_map/ppermute | solution.py:25
  171.6 8.2 %collective-permute-start.55 = (s16[144,256]{1,0:T(8,128)(2,1)S(1)}, s16[144,256]{1,0:T(8,128)(2,1)S(1)}, u32[]{:S(2)}, u32[]{:S(2)}) collective-permute-start(s16[144,256]{1,0:T(8,128)(2,1)S(1)} %get-tuple-element.131), channel_id=1, source_target_pairs={{0,2},{1,3},{2,0},{3,1},{4,6},{5,7},{6,4},{7,5},{8,10},{9,11},{10,... | collective-permute-start | bytes 221192 | tf_op jit(solution)/shard_map/ppermute | solution.py:25
  172.8 9.1 %collective-permute-start.56 = (s16[144,256]{1,0:T(8,128)(2,1)S(1)}, s16[144,256]{1,0:T(8,128)(2,1)S(1)}, u32[]{:S(2)}, u32[]{:S(2)}) collective-permute-start(s16[144,256]{1,0:T(8,128)(2,1)S(1)} %get-tuple-element.132), channel_id=1, source_target_pairs={{0,4},{1,5},{2,6},{3,7},{4,0},{5,1},{6,2},{7,3},{8,12},{9,13},{10,... | collective-permute-start | bytes 221192 | tf_op jit(solution)/shard_map/ppermute | solution.py:25
  174.0 7.9 %collective-permute-start.57 = (s16[144,256]{1,0:T(8,128)(2,1)S(1)}, s16[144,256]{1,0:T(8,128)(2,1)S(1)}, u32[]{:S(2)}, u32[]{:S(2)}) collective-permute-start(s16[144,256]{1,0:T(8,128)(2,1)S(1)} %get-tuple-element.133), channel_id=1, source_target_pairs={{0,6},{1,7},{2,4},{3,5},{4,2},{5,3},{6,0},{7,1},{8,14},{9,15},{10,... | collective-permute-start | bytes 221192 | tf_op jit(solution)/shard_map/ppermute | solution.py:25
  177.4 6.9 %collective-permute-start.52 = (s16[144,256]{1,0:T(8,128)(2,1)S(1)}, s16[144,256]{1,0:T(8,128)(2,1)S(1)}, u32[]{:S(2)}, u32[]{:S(2)}) collective-permute-start(s16[144,256]{1,0:T(8,128)(2,1)S(1)} %get-tuple-element.128), channel_id=1, source_target_pairs={{0,2},{1,3},{2,0},{3,1},{4,6},{5,7},{6,4},{7,5},{8,10},{9,11},{10,... | collective-permute-start | bytes 221192 | tf_op jit(solution)/shard_map/ppermute | solution.py:25
  178.6 10.4 %collective-permute-start.53 = (s16[144,256]{1,0:T(8,128)(2,1)S(1)}, s16[144,256]{1,0:T(8,128)(2,1)S(1)}, u32[]{:S(2)}, u32[]{:S(2)}) collective-permute-start(s16[144,256]{1,0:T(8,128)(2,1)S(1)} %get-tuple-element.129), channel_id=1, source_target_pairs={{0,4},{1,5},{2,6},{3,7},{4,0},{5,1},{6,2},{7,3},{8,12},{9,13},{10,... | collective-permute-start | bytes 221192 | tf_op jit(solution)/shard_map/ppermute | solution.py:25
  179.8 9.2 %collective-permute-start.54 = (s16[144,256]{1,0:T(8,128)(2,1)S(1)}, s16[144,256]{1,0:T(8,128)(2,1)S(1)}, u32[]{:S(2)}, u32[]{:S(2)}) collective-permute-start(s16[144,256]{1,0:T(8,128)(2,1)S(1)} %get-tuple-element.130), channel_id=1, source_target_pairs={{0,6},{1,7},{2,4},{3,5},{4,2},{5,3},{6,0},{7,1},{8,14},{9,15},{10,... | collective-permute-start | bytes 221192 | tf_op jit(solution)/shard_map/ppermute | solution.py:25
  182.0 7.1 %collective-permute-start.61 = (bf16[128,256]{1,0:T(8,128)(2,1)S(1)}, bf16[128,256]{1,0:T(8,128)(2,1)S(1)}, u32[]{:S(2)}, u32[]{:S(2)}) collective-permute-start(bf16[128,256]{1,0:T(8,128)(2,1)S(1)} %finish.13.refs_4_.refs_1_), channel_id=1, source_target_pairs={{0,2},{1,3},{2,0},{3,1},{4,6},{5,7},{6,4},{7,5},{8,10},{9,11},{10,... | collective-permute-start | bytes 196616 | tf_op jit(solution)/shard_map/ppermute | solution.py:25
  182.2 9.9 %collective-permute-start.62 = (bf16[128,256]{1,0:T(8,128)(2,1)S(1)}, bf16[128,256]{1,0:T(8,128)(2,1)S(1)}, u32[]{:S(2)}, u32[]{:S(2)}) collective-permute-start(bf16[128,256]{1,0:T(8,128)(2,1)S(1)} %finish.13.refs_4_.refs_1_), channel_id=1, source_target_pairs={{0,4},{1,5},{2,6},{3,7},{4,0},{5,1},{6,2},{7,3},{8,12},{9,13},{10,... | collective-permute-start | bytes 196616 | tf_op jit(solution)/shard_map/ppermute | solution.py:25
  184.4 7.8 %collective-permute-start.63 = (bf16[128,256]{1,0:T(8,128)(2,1)S(1)}, bf16[128,256]{1,0:T(8,128)(2,1)S(1)}, u32[]{:S(2)}, u32[]{:S(2)}) collective-permute-start(bf16[128,256]{1,0:T(8,128)(2,1)S(1)} %finish.13.refs_4_.refs_1_), channel_id=1, source_target_pairs={{0,6},{1,7},{2,4},{3,5},{4,2},{5,3},{6,0},{7,1},{8,14},{9,15},{10,... | collective-permute-start | bytes 196616 | tf_op jit(solution)/shard_map/ppermute | solution.py:25
  192.1 10.8 %collective-permute-start.65 = (bf16[4,128,256]{2,1,0:T(8,128)(2,1)S(1)}, bf16[4,128,256]{2,1,0:T(8,128)(2,1)S(1)}, u32[]{:S(2)}, u32[]{:S(2)}) collective-permute-start(bf16[4,128,256]{2,1,0:T(8,128)(2,1)S(1)} %order.13.refs_5_), channel_id=1, source_target_pairs={{0,1},{1,0},{2,3},{3,2},{4,5},{5,4},{6,7},{7,6},{8,9},{9,8},{10,11... | collective-permute-start | bytes 786440 | tf_op jit(solution)/shard_map/ppermute | solution.py:25
  202.0 22.4 %collective-permute-start.64 = (bf16[4,128,256]{2,1,0:T(8,128)(2,1)S(1)}, bf16[4,128,256]{2,1,0:T(8,128)(2,1)S(1)}, u32[]{:S(2)}, u32[]{:S(2)}) collective-permute-start(bf16[4,128,256]{2,1,0:T(8,128)(2,1)S(1)} %order.14.refs_7_.refs_1_), channel_id=1, source_target_pairs={{0,1},{1,0},{2,3},{3,2},{4,5},{5,4},{6,7},{7,6},{8,9},{9,8},{10,11... | collective-permute-start | bytes 786440 | tf_op jit(solution)/shard_map/ppermute | solution.py:25
  228.2 7.2 %collective-permute-start.66 = (f32[512,256]{1,0:T(8,128)}, f32[512,256]{1,0:T(8,128)}, u32[]{:S(2)}, u32[]{:S(2)}) collective-permute-start(f32[512,256]{1,0:T(8,128)} %get-tuple-element.135.refs_3_.refs_0_), channel_id=1, source_target_pairs={{0,8},{8,0},{16,24},{24,16},{1,9},{9,1},{17,25},{25,17},{2,10},{10... | collective-permute-start | bytes 1572872 | tf_op jit(solution)/shard_map/ppermute | solution.py:25
  238.3 8.8 %collective-permute-start.68 = (s16[528,256]{1,0:T(8,128)(2,1)}, s16[528,256]{1,0:T(8,128)(2,1)S(1)}, u32[]{:S(2)}, u32[]{:S(2)}) collective-permute-start(s16[528,256]{1,0:T(8,128)(2,1)} %get-tuple-element.139), channel_id=1, source_target_pairs={{0,16},{8,24},{16,0},{24,8},{1,17},{9,25},{17,1},{25,9},{2,18},{10... | collective-permute-start | bytes 811016 | tf_op jit(solution)/shard_map/ppermute | solution.py:25
  250.2 8.3 %collective-permute-start.69 = (s16[528,256]{1,0:T(8,128)(2,1)S(1)}, s16[528,256]{1,0:T(8,128)(2,1)S(1)}, u32[]{:S(2)}, u32[]{:S(2)}) collective-permute-start(s16[528,256]{1,0:T(8,128)(2,1)S(1)} %get-tuple-element.141), channel_id=1, source_target_pairs={{0,1},{1,0},{2,3},{3,2},{4,5},{5,4},{6,7},{7,6},{8,9},{9,8},{10,11... | collective-permute-start | bytes 811016 | tf_op jit(solution)/shard_map/ppermute | solution.py:25
  258.7 7.2 %collective-permute-start.71 = (s16[144,256]{1,0:T(8,128)(2,1)S(1)}, s16[144,256]{1,0:T(8,128)(2,1)S(1)}, u32[]{:S(2)}, u32[]{:S(2)}) collective-permute-start(s16[144,256]{1,0:T(8,128)(2,1)S(1)} %get-tuple-element.144), channel_id=1, source_target_pairs={{0,4},{1,5},{2,6},{3,7},{4,0},{5,1},{6,2},{7,3},{8,12},{9,13},{10,... | collective-permute-start | bytes 221192 | tf_op jit(solution)/shard_map/ppermute | solution.py:25
  261.2 6.3 %collective-permute-start.72 = (s16[144,256]{1,0:T(8,128)(2,1)S(1)}, s16[144,256]{1,0:T(8,128)(2,1)S(1)}, u32[]{:S(2)}, u32[]{:S(2)}) collective-permute-start(s16[144,256]{1,0:T(8,128)(2,1)S(1)} %get-tuple-element.145), channel_id=1, source_target_pairs={{0,6},{1,7},{2,4},{3,5},{4,2},{5,3},{6,0},{7,1},{8,14},{9,15},{10,... | collective-permute-start | bytes 221192 | tf_op jit(solution)/shard_map/ppermute | solution.py:25
  276.2 6.4 %collective-permute-start.76 = (bf16[4,128,256]{2,1,0:T(8,128)(2,1)S(1)}, bf16[4,128,256]{2,1,0:T(8,128)(2,1)S(1)}, u32[]{:S(2)}, u32[]{:S(2)}) collective-permute-start(bf16[4,128,256]{2,1,0:T(8,128)(2,1)S(1)} %order.15.refs_1_.refs_3_), channel_id=1, source_target_pairs={{0,1},{1,0},{2,3},{3,2},{4,5},{5,4},{6,7},{7,6},{8,9},{9,8},{10,11... | collective-permute-start | bytes 786440 | tf_op jit(solution)/shard_map/ppermute | solution.py:25
  285.0 10.5 %collective-permute-start.80 = (bf16[8,128,256]{2,1,0:T(8,128)(2,1)S(1)}, bf16[8,128,256]{2,1,0:T(8,128)(2,1)S(1)}, u32[]{:S(2)}, u32[]{:S(2)}) collective-permute-start(bf16[8,128,256]{2,1,0:T(8,128)(2,1)S(1)} %trail.12.refs_4_), channel_id=1, source_target_pairs={{0,8},{8,0},{16,24},{24,16},{1,9},{9,1},{17,25},{25,17},{2,10},{10... | collective-permute-start | bytes 1572872 | tf_op jit(solution)/shard_map/ppermute | solution.py:25
  285.5 14.8 %collective-permute-start.81 = (bf16[8,128,256]{2,1,0:T(8,128)(2,1)S(1)}, bf16[8,128,256]{2,1,0:T(8,128)(2,1)S(1)}, u32[]{:S(2)}, u32[]{:S(2)}) collective-permute-start(bf16[8,128,256]{2,1,0:T(8,128)(2,1)S(1)} %copy-done.9), channel_id=1, source_target_pairs={{0,16},{8,24},{16,0},{24,8},{1,17},{9,25},{17,1},{25,9},{2,18},{10... | collective-permute-start | bytes 1572872 | tf_op jit(solution)/shard_map/ppermute | solution.py:25
  291.1 13.6 %collective-permute-start.78 = (bf16[8,128,256]{2,1,0:T(8,128)(2,1)S(1)}, bf16[8,128,256]{2,1,0:T(8,128)(2,1)S(1)}, u32[]{:S(2)}, u32[]{:S(2)}) collective-permute-start(bf16[8,128,256]{2,1,0:T(8,128)(2,1)S(1)} %trail.16.refs_4_), channel_id=1, source_target_pairs={{0,8},{8,0},{16,24},{24,16},{1,9},{9,1},{17,25},{25,17},{2,10},{10... | collective-permute-start | bytes 1572872 | tf_op jit(solution)/shard_map/ppermute | solution.py:25
  291.2 19.5 %collective-permute-start.79 = (bf16[8,128,256]{2,1,0:T(8,128)(2,1)S(1)}, bf16[8,128,256]{2,1,0:T(8,128)(2,1)S(1)}, u32[]{:S(2)}, u32[]{:S(2)}) collective-permute-start(bf16[8,128,256]{2,1,0:T(8,128)(2,1)S(1)} %add.34.refs_4_), channel_id=1, source_target_pairs={{0,16},{8,24},{16,0},{24,8},{1,17},{9,25},{17,1},{25,9},{2,18},{10... | collective-permute-start | bytes 1572872 | tf_op jit(solution)/shard_map/ppermute | solution.py:25
  (31 other events, 292.3 us)

commit v2 on v1

--- a/solution.py
+++ b/solution.py
@@ -8,7 +8,9 @@
 from jax.sharding import PartitionSpec as P
 
 SPLITS = 2
-LAG = 5
+LAG = 2
+MERGED = False
+PAUSE = 1
 F32 = jnp.float32
 BF16 = jnp.bfloat16
 CODE = jnp.int16
@@ -185,7 +187,8 @@
 
 
 def trail_kernel(groups, add, refs):
-    blocks, rest, out_ref = refs[1 : 1 + groups], refs[1 + groups : -1], refs[-1]
+    blocks, rest, out_ref, token_ref = refs[1 : 1 + groups], refs[1 + groups : -2], refs[-2], refs[-1]
+    token_ref[...] = jnp.zeros(token_ref.shape, F32)
     count = (len(rest) - int(add)) // groups
     total = flat_rows(rest[-1][...]) if add else None
     for g in range(groups):
@@ -225,9 +228,7 @@
     inner = nc // outer
 
     def body(rhs, coupling, pattern, inverse, trail_coupling, trail_rhs):
-        rhs = pltpu.with_memory_space_constraint(rhs, pltpu.HBM)
-        coupling = pltpu.with_memory_space_constraint(coupling, pltpu.HBM)
-        inverse = pltpu.with_memory_space_constraint(inverse, pltpu.HBM)
+        trail_rhs = pltpu.with_memory_space_constraint(trail_rhs, pltpu.HBM)
         row_index = lax.axis_index("prow")
         col_index = lax.axis_index("pcol")
         core, line = row_index % cores, row_index // cores
@@ -241,7 +242,6 @@
         solved_dims = (col_count * tile, part)
         trail_tiles = trail_coupling.shape[0]
         group = trail_tiles // nr
-        step_tiles = min(4, group)
         pattern_flat = pattern.reshape(pattern.shape[0], pattern.shape[2])
         last = [None]
 
@@ -264,7 +264,7 @@
                 out_shape=outs,
                 scratch_shapes=list(scratch),
                 compiler_params=pltpu.CompilerParams(vmem_limit_bytes=limit * MIB),
-                cost_estimate=cost(1, 1),
+                cost_estimate=cost(10e9, 1),
                 name=name,
             )(*operands)
             last[0] = result[0]
@@ -354,12 +354,12 @@
                 size=4 * nc * rows * part,
             )[0]
 
-        def trail_product(first, count, xs, added, rank, columns, dtype, chain=False):
-            steps = (trail_tiles if rank is None else group) // step_tiles
-            base = jnp.reshape(0 if rank is None else rank * steps, (1,)).astype(jnp.int32)
-            wide = width if columns is None else part
-            column = 0 if columns is None else columns
-            operands = [trail_coupling] * count + xs + ([] if added is None else [added])
+        def trail_product(first, xs, added, rank, column, dtype):
+            count = len(xs)
+            step_tiles = min(4, group)
+            steps = group // step_tiles
+            base = jnp.reshape(rank * steps, (1,)).astype(jnp.int32)
+            operands = [trail_coupling] * count + xs + ([] if added is None else [added]) + [last[0]]
             specs = [
                 pl.BlockSpec(
                     (step_tiles, None, col_count, None, tile, tile),
@@ -368,35 +368,32 @@
                 for g in range(count)
             ] + [whole(v) for v in xs]
             if added is not None:
-                specs.append(pl.BlockSpec((step_tiles, tile, wide), lambda i, b: (b[0] + i, 0, column)))
-            extra = int(chain)
-            if chain:
-                operands.append(last[0])
-                specs.append(ANY)
+                specs.append(pl.BlockSpec((step_tiles, tile, part), lambda i, b: (i, 0, 0)))
+            specs.append(ANY)
             total = 1 + len(operands)
 
             def run(*refs):
-                trail_kernel(count, added is not None, refs[: total - extra] + refs[total:])
-
+                trail_kernel(count, added is not None, refs[: total - 1] + refs[total:])
+
+            token = shape((8, 128), F32)
             result = pl.pallas_call(
                 run,
                 grid_spec=pltpu.PrefetchScalarGridSpec(
                     num_scalar_prefetch=1,
                     grid=(steps,),
                     in_specs=specs,
-                    out_specs=pl.BlockSpec((step_tiles, tile, wide), lambda i, b: (i, 0, 0)),
+                    out_specs=[
+                        pl.BlockSpec((step_tiles, tile, part), lambda i, b: (i, 0, 0)),
+                        whole(token),
+                    ],
                 ),
-                out_shape=shape((steps * step_tiles, tile, wide), dtype),
+                out_shape=[shape((group, tile, part), dtype), token],
                 compiler_params=pltpu.CompilerParams(vmem_limit_bytes=36 * MIB),
-                cost_estimate=cost(
-                    2 * steps * step_tiles * tile * count * col_count * tile * wide,
-                    steps * step_tiles * tile * (2 * count * col_count * tile + 4 * wide),
-                ),
+                cost_estimate=cost(10e9, 1),
                 name="trail",
             )(base, *operands)
-            if chain:
-                last[0] = result
-            return result
+            last[0] = result[1]
+            return result[0]
 
         def add(values, dtype, name):
             return call(
@@ -452,21 +449,30 @@
 
         solved = [[] for _ in range(SPLITS)]
         trail_sums = [None] * SPLITS
-        trail = [None]
 
         def chain_of(h):
             pieces = None
+            early = {}
+            wanted = [(e, d) for e in range(1, lines) for d in list(range(1, cores)) + [0]]
+
+            def begin():
+                if h == SPLITS - 1 and k == panels - 1 and wanted:
+                    e, d = wanted.pop(0)
+                    early[e, d] = trail_product(0, solved[h], None, (line ^ e) * cores + (core ^ d), h, F32)
+
             for k in range(panels):
                 update = []
                 if k > 0:
                     u, newest = couple(k, h, solved[h], pieces)
                     solved[h].append(newest.reshape(solved_dims))
                     arrived = [swap(u, "prow", nr, d) for d in range(1, cores)]
-                    yield
+                    if not MERGED:
+                        yield
                     update, message = merge(u, arrived, False)
                     d = 1
                     while d < lines:
                         arrived = swap(message, "prow", nr, d * cores)
+                        begin()
                         yield
                         d *= 2
                         if d < lines:
@@ -474,6 +480,7 @@
                     update = [update] + ([arrived] if lines > 1 else [])
                 kept, *sent = invert(k, h, update)
                 arrived = [swap(v, "pcol", nc, d + 1) for d, v in enumerate(sent)]
+                begin()
                 yield
                 kept, *sent = fold(kept, arrived)
                 arrived = [swap(v, "pcol", nc, (d + 1) * inner) for d, v in enumerate(sent)]
@@ -485,21 +492,29 @@
                 pieces = [column] + [swap(column, "pcol", nc, d) for d in range(1, inner)]
                 yield
             solved[h].append(order_last(pieces).reshape(solved_dims))
-
-            def rows_of(rank, dtype):
-                return trail_product(panels - 1, 1, [solved[h][-1]], trail[0], rank, h, dtype, True)
-
             received = []
             for e in list(range(1, lines)) + [0]:
                 there = line ^ e
-                sent = [rows_of(there * cores + (core ^ d), BF16) for d in range(1, cores)]
-                total = rows_of(there * cores + core, F32)
-                arrived = [swap(v, "prow", nr, d + 1) for d, v in enumerate(sent)]
+
+                def rows_of(d, dtype):
+                    rank = there * cores + (core ^ d)
+                    if (e, d) in early:
+                        return trail_product(panels - 1, solved[h][-1:], early[e, d], rank, h, dtype)
+                    return trail_product(0, solved[h], None, rank, h, dtype)
+
+                arrived = []
+                for d in range(1, cores):
+                    arrived.append(swap(rows_of(d, BF16), "prow", nr, d))
+                    yield
+                total = rows_of(0, F32)
                 if e == 0:
                     trail_sums[h] = [total] + arrived + received
                 else:
                     received.append(swap(add([total] + arrived, BF16, "add"), "prow", nr, e * cores))
                 yield
+                if e == lines - 1 and h < SPLITS - 1:
+                    for _ in range(PAUSE):
+                        yield
 
         chains = [chain_of(h) for h in range(SPLITS)]
         alive = [True] * SPLITS
@@ -509,11 +524,6 @@
                 if alive[h] and step >= h * LAG:
                     alive[h] = next(chains[h], "end") != "end"
             step += 1
-            if trail[0] is None and all(len(s) == panels - 1 for s in solved):
-                done = panels - 1
-                xs = [solved[h][e] for e in range(done) for h in range(SPLITS)]
-                trail[0] = trail_product(0, done, xs, None, None, None, F32)
-
         known = join(None, 0, panels - 1)
         known = join(known, panels - 1, 1)
         trail_out = None

time: 313 us -> 258 us (0.82)
  waiting for transfers between devices: 96.7 us -> 64.1 us
  Pallas kernels: 87 us -> 76.2 us
  starting transfers between devices: 118 us -> 110 us
    ppermute x82, waiting for transfers between devices: 96.7 us -> 64.1 us  [swap(): return lax.ppermute(value, axis, [(s, s ^ mask) for s in range(count)])]
    pallas_call x48, Pallas kernels: 45.7 us -> 26.9 us  [call(): pl.pallas_call(run, in_specs=specs, out_specs=[VMEM] * len(outs), out_sha...]
    ppermute x82, starting transfers between devices: 118 us -> 110 us  [swap(): return lax.ppermute(value, axis, [(s, s ^ mask) for s in range(count)])]
    pallas_call x9 -> x10, Pallas kernels: 35.7 us -> 41.1 us  [trail_product(): pl.pallas_call(run, grid_spec=pltpu.PrefetchScalarGridSpec(num_scalar_pre...]
    unnamed x26 -> x40, local copies, waits for them, and re-layouts: 8.47 us -> 5.61 us
  transfers between devices with their start and end apart: 82 -> 82, of which waited for: 44 -> 33; matrix products, arithmetic and copies ran while one was open for 0% -> 0% of each run, Pallas kernels for 22% -> 28%
where the time goes in v2:
time: 258 us
  starting transfers between devices  110 us (43%)
  Pallas kernels  76.2 us (30%)
  waiting for transfers between devices  64.1 us (25%)
  local copies, waits for them, and re-layouts  5.61 us (2%)
    ppermute x82, starting transfers between devices, swap(): return lax.ppermute(value, axis, [(s, s ^ mask) for s in range(count)])  110 us
    ppermute x82, waiting for transfers between devices, swap(): return lax.ppermute(value, axis, [(s, s ^ mask) for s in range(count)])  64.1 us
    pallas_call x10, Pallas kernels, trail_product(): pl.pallas_call(run, grid_spec=pltpu.PrefetchScalarGridSpec(num_scalar_pre...  41.1 us
    pallas_call x48, Pallas kernels, call(): pl.pallas_call(run, in_specs=specs, out_specs=[VMEM] * len(outs), out_sha...  26.9 us
    unnamed x40, local copies, waits for them, and re-layouts  5.61 us
  transfers between devices with their start and end apart: 82, of which 33 were waited for; matrix products, arithmetic and copies ran while one was open for 0% of the time, Pallas kernels for 28%

profile of v2, /device:TPU:0, one launch (start us, length us, event | category | flops | bytes accessed | tf_op | source)
XLA Modules:
  0.0 257.9 jit_solution(3613238724072943767)
XLA Ops:
  0.7 2.2 copy-done.4
  2.8 2.2 copy-done.7
  6.1 3.0 %collective-permute-start = (s16[528,256]{1,0:T(8,128)(2,1)S(1)}, s16[528,256]{1,0:T(8,128)(2,1)S(1)}, u32[]{:S(2)}, u32[]{:S(2)}) collective-permute-start(s16[528,256]{1,0:T(8,128)(2,1)S(1)} %get-tuple-element.94), channel_id=1, source_target_pairs={{0,1},{1,0},{2,3},{3,2},{4,5},{5,4},{6,7},{7,6},{8,9},{9,8},{10,11... | collective-permute-start | bytes 811016 | tf_op jit(solution)/shard_map/ppermute | solution.py:27
  9.2 6.5 %collective-permute-done.refs_2_ = s16[528,256]{1,0:T(8,128)(2,1)S(1)} collective-permute-done((s16[528,256]{1,0:T(8,128)(2,1)S(1)}, s16[528,256]{1,0:T(8,128)(2,1)S(1)}, u32[]{:S(2)}, u32[]{:S(2)}) %collective-permute-start) | collective-permute-done | bytes 270368 | tf_op jit(solution)/shard_map/ppermute | solution.py:27
  15.9 1.9 collective-permute-start.1
  17.8 2.6 %collective-permute-start.2 = (s16[144,256]{1,0:T(8,128)(2,1)S(1)}, s16[144,256]{1,0:T(8,128)(2,1)S(1)}, u32[]{:S(2)}, u32[]{:S(2)}) collective-permute-start(s16[144,256]{1,0:T(8,128)(2,1)S(1)} %get-tuple-element.97), channel_id=1, source_target_pairs={{0,4},{1,5},{2,6},{3,7},{4,0},{5,1},{6,2},{7,3},{8,12},{9,13},{10,... | collective-permute-start | bytes 221192 | tf_op jit(solution)/shard_map/ppermute | solution.py:27
  21.0 3.7 %collective-permute-done.2.refs_2_ = s16[144,256]{1,0:T(8,128)(2,1)S(1)} collective-permute-done((s16[144,256]{1,0:T(8,128)(2,1)S(1)}, s16[144,256]{1,0:T(8,128)(2,1)S(1)}, u32[]{:S(2)}, u32[]{:S(2)}) %collective-permute-start.2) | collective-permute-done | bytes 73760 | tf_op jit(solution)/shard_map/ppermute | solution.py:27
  24.7 1.9 collective-permute-done.3.refs_3_
  26.7 2.0 collective-permute-start.6
  28.9 2.2 collective-permute-start.4
  36.2 4.0 %collective-permute-done.8.refs_2_ = s16[528,256]{1,0:T(8,128)(2,1)S(1)} collective-permute-done((s16[528,256]{1,0:T(8,128)(2,1)S(1)}, s16[528,256]{1,0:T(8,128)(2,1)S(1)}, u32[]{:S(2)}, u32[]{:S(2)}) %collective-permute-start.8) | collective-permute-done | bytes 270368 | tf_op jit(solution)/shard_map/ppermute | solution.py:27
  42.4 2.5 collective-permute-start.12
  46.3 2.3 collective-permute-done.12.refs_3_
  48.6 2.6 %collective-permute-start.16 = (bf16[128,256]{1,0:T(8,128)(2,1)S(1)}, bf16[128,256]{1,0:T(8,128)(2,1)S(1)}, u32[]{:S(2)}, u32[]{:S(2)}) collective-permute-start(bf16[128,256]{1,0:T(8,128)(2,1)S(1)} %finish.9.refs_2_.refs_1_), channel_id=1, source_target_pairs={{0,6},{1,7},{2,4},{3,5},{4,2},{5,3},{6,0},{7,1},{8,14},{9,15},{10,... | collective-permute-start | bytes 196616 | tf_op jit(solution)/shard_map/ppermute | solution.py:27
  51.3 1.8 collective-permute-start.14
  58.0 1.8 collective-permute-done.13.refs_4_
  62.7 2.7 %collective-permute-done.18.refs_4_ = bf16[4,128,256]{2,1,0:T(8,128)(2,1)S(1)} collective-permute-done((bf16[4,128,256]{2,1,0:T(8,128)(2,1)S(1)}, bf16[4,128,256]{2,1,0:T(8,128)(2,1)S(1)}, u32[]{:S(2)}, u32[]{:S(2)}) %collective-permute-start.18) | collective-permute-done | bytes 262176 | tf_op jit(solution)/shard_map/ppermute | solution.py:27
  66.7 2.0 collective-permute-done.17.refs_2_
  69.3 1.9 collective-permute-start.20
  71.2 2.2 collective-permute-start.21
  77.5 2.3 collective-permute-start.25
  86.9 4.0 %collective-permute-done.28.refs_2_ = s16[528,256]{1,0:T(8,128)(2,1)S(1)} collective-permute-done((s16[528,256]{1,0:T(8,128)(2,1)S(1)}, s16[528,256]{1,0:T(8,128)(2,1)S(1)}, u32[]{:S(2)}, u32[]{:S(2)}) %collective-permute-start.28) | collective-permute-done | bytes 270368 | tf_op jit(solution)/shard_map/ppermute | solution.py:27
  91.5 2.1 collective-permute-start.31
  93.6 2.0 collective-permute-start.32
  95.6 1.8 coupling.8
  97.5 2.3 collective-permute-done.32.refs_3_
  99.9 2.1 collective-permute-start.36
  102.0 2.4 collective-permute-start.34
  109.0 2.1 collective-permute-done.33.refs_4_
  114.0 2.3 collective-permute-done.38.refs_5_
  116.3 1.9 coupling.9
  120.5 2.1 collective-permute-start.40
  122.6 1.8 collective-permute-start.41
  126.2 2.7 %collective-permute-done.40.refs_2_ = s16[144,256]{1,0:T(8,128)(2,1)S(1)} collective-permute-done((s16[144,256]{1,0:T(8,128)(2,1)S(1)}, s16[144,256]{1,0:T(8,128)(2,1)S(1)}, u32[]{:S(2)}, u32[]{:S(2)}) %collective-permute-start.40) | collective-permute-done | bytes 73760 | tf_op jit(solution)/shard_map/ppermute | solution.py:27
  129.0 1.9 collective-permute-start.45
  138.4 4.7 %collective-permute-done.48.refs_2_ = s16[528,256]{1,0:T(8,128)(2,1)S(1)} collective-permute-done((s16[528,256]{1,0:T(8,128)(2,1)S(1)}, s16[528,256]{1,0:T(8,128)(2,1)S(1)}, u32[]{:S(2)}, u32[]{:S(2)}) %collective-permute-start.48) | collective-permute-done | bytes 270368 | tf_op jit(solution)/shard_map/ppermute | solution.py:27
  145.6 2.2 collective-permute-start.52
  147.8 2.8 %coupling.10 = (f32[512,256]{1,0:T(8,128)S(1)}, bf16[4,2,128,256]{3,2,1,0:T(8,128)(2,1)S(1)}) custom-call(s32[1]{0:T(128)} %bitcast.refs_0_, s32[16,32]{1,0:T(8,128)S(1)} %bitcast.78, bf16[16,1,32,1,128,128]{5,4,3,2,1,0:T(8,128)(2,1)S(1)} %bitcast.73, bf16[1024,256]{1,0:T(8,128)(2,1)S(1)} %bitcast.32, bf16[1024,256]{1,0:T(8,128)(2,1)S(1)} %bitcast.45, ...), custom_call_target="tpu_custom_call" | custom-call | flops 10000000000 | bytes 1 | tf_op jit(solution)/shard_map/coupling/pallas_call | solution.py:260
  151.8 2.2 collective-permute-start.56
  154.0 2.3 collective-permute-start.54
  161.5 2.0 collective-permute-done.53.refs_4_
  166.4 1.9 collective-permute-done.58.refs_6_
  168.3 2.8 %coupling.11 = (f32[512,256]{1,0:T(8,128)S(1)}, bf16[4,2,128,256]{3,2,1,0:T(8,128)(2,1)S(1)}) custom-call(s32[1]{0:T(128)} %bitcast.refs_0_, s32[16,32]{1,0:T(8,128)S(1)} %bitcast.79, bf16[16,1,32,1,128,128]{5,4,3,2,1,0:T(8,128)(2,1)S(1)} %bitcast.73, bf16[1024,256]{1,0:T(8,128)(2,1)S(1)} %bitcast.39, bf16[1024,256]{1,0:T(8,128)(2,1)S(1)} %bitcast.51, ...), custom_call_target="tpu_custom_call" | custom-call | flops 10000000000 | bytes 1 | tf_op jit(solution)/shard_map/coupling/pallas_call | solution.py:260
  175.0 2.2 collective-permute-start.61
  178.7 3.9 %trail.10 = (f32[8,128,256]{2,1,0:T(8,128)S(1)}, f32[8,128]{1,0:T(8,128)S(1)}) custom-call(s32[1]{0:T(128)} %bitcast.7.refs_0_, bf16[32,1,32,1,128,128]{5,4,3,2,1,0:T(8,128)(2,1)} %refs_4_.11, bf16[32,1,32,1,128,128]{5,4,3,2,1,0:T(8,128)(2,1)} %refs_4_.11, bf16[32,1,32,1,128,128]{5,4,3,2,1,0:T(8,128)(2,1)} %refs_4_.11, bf16[1024,256]{1,0:T(8,128)(2,1)S(1)} %bitcast.40, ...), custom_call_target="tpu_custom_call" | custom-call | flops 10000000000 | bytes 1 | tf_op jit(solution)/shard_map/trail/pallas_call | solution.py:379
  182.7 2.1 collective-permute-start.65
  184.9 2.3 collective-permute-start.63
  190.1 3.9 %trail.11 = (f32[8,128,256]{2,1,0:T(8,128)S(1)}, f32[8,128]{1,0:T(8,128)S(1)}) custom-call(s32[1]{0:T(128)} %bitcast.9.refs_0_, bf16[32,1,32,1,128,128]{5,4,3,2,1,0:T(8,128)(2,1)} %refs_4_.11, bf16[32,1,32,1,128,128]{5,4,3,2,1,0:T(8,128)(2,1)} %refs_4_.11, bf16[32,1,32,1,128,128]{5,4,3,2,1,0:T(8,128)(2,1)} %refs_4_.11, bf16[1024,256]{1,0:T(8,128)(2,1)S(1)} %bitcast.41, ...), custom_call_target="tpu_custom_call" | custom-call | flops 10000000000 | bytes 1 | tf_op jit(solution)/shard_map/trail/pallas_call | solution.py:379
  196.7 2.7 %collective-permute-start.70 = (s16[144,256]{1,0:T(8,128)(2,1)S(1)}, s16[144,256]{1,0:T(8,128)(2,1)S(1)}, u32[]{:S(2)}, u32[]{:S(2)}) collective-permute-start(s16[144,256]{1,0:T(8,128)(2,1)S(1)} %get-tuple-element.164), channel_id=1, source_target_pairs={{0,4},{1,5},{2,6},{3,7},{4,0},{5,1},{6,2},{7,3},{8,12},{9,13},{10,... | collective-permute-start | bytes 221192 | tf_op jit(solution)/shard_map/ppermute | solution.py:27
  202.2 4.7 %trail.12 = (bf16[8,128,256]{2,1,0:T(8,128)(2,1)S(1)}, f32[8,128]{1,0:T(8,128)S(1)}) custom-call(s32[1]{0:T(128)} %bitcast.7.refs_0_, bf16[32,1,32,1,128,128]{5,4,3,2,1,0:T(8,128)(2,1)} %refs_4_.11, bf16[32,1,32,1,128,128]{5,4,3,2,1,0:T(8,128)(2,1)} %refs_4_.11, bf16[32,1,32,1,128,128]{5,4,3,2,1,0:T(8,128)(2,1)} %refs_4_.11, ...), custom_call_target="tpu_custom_call" | custom-call | flops 10000000000 | bytes 1 | tf_op jit(solution)/shard_map/trail/pallas_call | solution.py:379
  207.2 2.3 collective-permute-start.74
  209.4 2.2 collective-permute-start.72
  211.6 4.8 %trail.13 = (f32[8,128,256]{2,1,0:T(8,128)S(1)}, f32[8,128]{1,0:T(8,128)S(1)}) custom-call(s32[1]{0:T(128)} %bitcast.9.refs_0_, bf16[32,1,32,1,128,128]{5,4,3,2,1,0:T(8,128)(2,1)} %refs_4_.11, bf16[32,1,32,1,128,128]{5,4,3,2,1,0:T(8,128)(2,1)} %refs_4_.11, bf16[32,1,32,1,128,128]{5,4,3,2,1,0:T(8,128)(2,1)} %refs_4_.11, ...), custom_call_target="tpu_custom_call" | custom-call | flops 10000000000 | bytes 1 | tf_op jit(solution)/shard_map/trail/pallas_call | solution.py:379
  217.3 2.6 collective-permute-start.76
  220.3 2.1 join.2.refs_2_
  223.4 2.6 collective-permute-done.76.refs_2_
  226.0 2.2 trail.14
  228.2 4.8 %trail.15 = (bf16[8,128,256]{2,1,0:T(8,128)(2,1)S(1)}, f32[8,128]{1,0:T(8,128)S(1)}) custom-call(s32[1]{0:T(128)} %bitcast.24.refs_0_, bf16[32,1,32,1,128,128]{5,4,3,2,1,0:T(8,128)(2,1)} %refs_4_.11, bf16[32,1,32,1,128,128]{5,4,3,2,1,0:T(8,128)(2,1)} %refs_4_.11, bf16[32,1,32,1,128,128]{5,4,3,2,1,0:T(8,128)(2,1)} %refs_4_.11, ...), custom_call_target="tpu_custom_call" | custom-call | flops 10000000000 | bytes 1 | tf_op jit(solution)/shard_map/trail/pallas_call | solution.py:379
  234.6 2.1 trail.16
  238.0 4.8 %trail.17 = (f32[8,128,256]{2,1,0:T(8,128)S(1)}, f32[8,128]{1,0:T(8,128)S(1)}) custom-call(s32[1]{0:T(128)} %bitcast.22.refs_0_, bf16[32,1,32,1,128,128]{5,4,3,2,1,0:T(8,128)(2,1)} %refs_4_.11, bf16[32,1,32,1,128,128]{5,4,3,2,1,0:T(8,128)(2,1)} %refs_4_.11, bf16[32,1,32,1,128,128]{5,4,3,2,1,0:T(8,128)(2,1)} %refs_4_.11, ...), custom_call_target="tpu_custom_call" | custom-call | flops 10000000000 | bytes 1 | tf_op jit(solution)/shard_map/trail/pallas_call | solution.py:379
  242.8 4.8 %trail.18 = (bf16[8,128,256]{2,1,0:T(8,128)(2,1)S(1)}, f32[8,128]{1,0:T(8,128)S(1)}) custom-call(s32[1]{0:T(128)} %bitcast.24.refs_0_, bf16[32,1,32,1,128,128]{5,4,3,2,1,0:T(8,128)(2,1)} %refs_4_.11, bf16[32,1,32,1,128,128]{5,4,3,2,1,0:T(8,128)(2,1)} %refs_4_.11, bf16[32,1,32,1,128,128]{5,4,3,2,1,0:T(8,128)(2,1)} %refs_4_.11, ...), custom_call_target="tpu_custom_call" | custom-call | flops 10000000000 | bytes 1 | tf_op jit(solution)/shard_map/trail/pallas_call | solution.py:379
  247.7 2.5 subtract.2.refs_4_
  250.2 5.2 %trail.19 = (f32[8,128,256]{2,1,0:T(8,128)S(1)}, f32[8,128]{1,0:T(8,128)}) custom-call(s32[1]{0:T(128)} %bitcast.22.refs_0_, bf16[32,1,32,1,128,128]{5,4,3,2,1,0:T(8,128)(2,1)} %refs_4_.11, bf16[32,1,32,1,128,128]{5,4,3,2,1,0:T(8,128)(2,1)} %refs_4_.11, bf16[32,1,32,1,128,128]{5,4,3,2,1,0:T(8,128)(2,1)} %refs_4_.11, ...), custom_call_target="tpu_custom_call" | custom-call | flops 10000000000 | bytes 1 | tf_op jit(solution)/shard_map/trail/pallas_call | solution.py:379
  255.5 2.5 subtract.3
  (205 shorter events, 82.8 us)
Async XLA Ops:
  6.1 9.5 %collective-permute-start = (s16[528,256]{1,0:T(8,128)(2,1)S(1)}, s16[528,256]{1,0:T(8,128)(2,1)S(1)}, u32[]{:S(2)}, u32[]{:S(2)}) collective-permute-start(s16[528,256]{1,0:T(8,128)(2,1)S(1)} %get-tuple-element.94), channel_id=1, source_target_pairs={{0,1},{1,0},{2,3},{3,2},{4,5},{5,4},{6,7},{7,6},{8,9},{9,8},{10,11... | collective-permute-start | bytes 811016 | tf_op jit(solution)/shard_map/ppermute | solution.py:27
  17.8 6.9 %collective-permute-start.2 = (s16[144,256]{1,0:T(8,128)(2,1)S(1)}, s16[144,256]{1,0:T(8,128)(2,1)S(1)}, u32[]{:S(2)}, u32[]{:S(2)}) collective-permute-start(s16[144,256]{1,0:T(8,128)(2,1)S(1)} %get-tuple-element.97), channel_id=1, source_target_pairs={{0,4},{1,5},{2,6},{3,7},{4,0},{5,1},{6,2},{7,3},{8,12},{9,13},{10,... | collective-permute-start | bytes 221192 | tf_op jit(solution)/shard_map/ppermute | solution.py:27
  20.3 6.3 %collective-permute-start.3 = (s16[144,256]{1,0:T(8,128)(2,1)S(1)}, s16[144,256]{1,0:T(8,128)(2,1)S(1)}, u32[]{:S(2)}, u32[]{:S(2)}) collective-permute-start(s16[144,256]{1,0:T(8,128)(2,1)S(1)} %get-tuple-element.98), channel_id=1, source_target_pairs={{0,6},{1,7},{2,4},{3,5},{4,2},{5,3},{6,0},{7,1},{8,14},{9,15},{10,... | collective-permute-start | bytes 221192 | tf_op jit(solution)/shard_map/ppermute | solution.py:27
  26.7 7.2 %collective-permute-start.6 = (bf16[128,256]{1,0:T(8,128)(2,1)S(1)}, bf16[128,256]{1,0:T(8,128)(2,1)S(1)}, u32[]{:S(2)}, u32[]{:S(2)}) collective-permute-start(bf16[128,256]{1,0:T(8,128)(2,1)S(1)} %finish.8.refs_3_.refs_1_), channel_id=1, source_target_pairs={{0,6},{1,7},{2,4},{3,5},{4,2},{5,3},{6,0},{7,1},{8,14},{9,15},{10,... | collective-permute-start | bytes 196616 | tf_op jit(solution)/shard_map/ppermute | solution.py:27
  32.3 7.9 %collective-permute-start.8 = (s16[528,256]{1,0:T(8,128)(2,1)S(1)}, s16[528,256]{1,0:T(8,128)(2,1)S(1)}, u32[]{:S(2)}, u32[]{:S(2)}) collective-permute-start(s16[528,256]{1,0:T(8,128)(2,1)S(1)} %get-tuple-element.100), channel_id=1, source_target_pairs={{0,1},{1,0},{2,3},{3,2},{4,5},{5,4},{6,7},{7,6},{8,9},{9,8},{10,11... | collective-permute-start | bytes 811016 | tf_op jit(solution)/shard_map/ppermute | solution.py:27
  34.6 10.3 %collective-permute-start.7 = (bf16[4,128,256]{2,1,0:T(8,128)(2,1)S(1)}, bf16[4,128,256]{2,1,0:T(8,128)(2,1)S(1)}, u32[]{:S(2)}, u32[]{:S(2)}) collective-permute-start(bf16[4,128,256]{2,1,0:T(8,128)(2,1)S(1)} %order.8.refs_3_), channel_id=1, source_target_pairs={{0,1},{1,0},{2,3},{3,2},{4,5},{5,4},{6,7},{7,6},{8,9},{9,8},{10,11... | collective-permute-start | bytes 786440 | tf_op jit(solution)/shard_map/ppermute | solution.py:27
  42.4 6.2 %collective-permute-start.12 = (s16[144,256]{1,0:T(8,128)(2,1)S(1)}, s16[144,256]{1,0:T(8,128)(2,1)S(1)}, u32[]{:S(2)}, u32[]{:S(2)}) collective-permute-start(s16[144,256]{1,0:T(8,128)(2,1)S(1)} %get-tuple-element.106), channel_id=1, source_target_pairs={{0,6},{1,7},{2,4},{3,5},{4,2},{5,3},{6,0},{7,1},{8,14},{9,15},{10,... | collective-permute-start | bytes 221192 | tf_op jit(solution)/shard_map/ppermute | solution.py:27
  46.2 6.9 %collective-permute-start.9 = (f32[512,256]{1,0:T(8,128)S(1)}, f32[512,256]{1,0:T(8,128)S(1)}, u32[]{:S(2)}, u32[]{:S(2)}) collective-permute-start(f32[512,256]{1,0:T(8,128)S(1)} %get-tuple-element.103.refs_4_.refs_0_), channel_id=1, source_target_pairs={{0,8},{8,0},{16,24},{24,16},{1,9},{9,1},{17,25},{25,17},{2,10},{10... | collective-permute-start | bytes 1572872 | tf_op jit(solution)/shard_map/ppermute | solution.py:27
  48.6 6.3 %collective-permute-start.16 = (bf16[128,256]{1,0:T(8,128)(2,1)S(1)}, bf16[128,256]{1,0:T(8,128)(2,1)S(1)}, u32[]{:S(2)}, u32[]{:S(2)}) collective-permute-start(bf16[128,256]{1,0:T(8,128)(2,1)S(1)} %finish.9.refs_2_.refs_1_), channel_id=1, source_target_pairs={{0,6},{1,7},{2,4},{3,5},{4,2},{5,3},{6,0},{7,1},{8,14},{9,15},{10,... | collective-permute-start | bytes 196616 | tf_op jit(solution)/shard_map/ppermute | solution.py:27
  53.3 6.5 %collective-permute-start.13 = (s16[528,256]{1,0:T(8,128)(2,1)S(1)}, s16[528,256]{1,0:T(8,128)(2,1)S(1)}, u32[]{:S(2)}, u32[]{:S(2)}) collective-permute-start(s16[528,256]{1,0:T(8,128)(2,1)S(1)} %get-tuple-element.108), channel_id=1, source_target_pairs={{0,16},{8,24},{16,0},{24,8},{1,17},{9,25},{17,1},{25,9},{2,18},{10... | collective-permute-start | bytes 811016 | tf_op jit(solution)/shard_map/ppermute | solution.py:27
  56.5 8.9 %collective-permute-start.18 = (bf16[4,128,256]{2,1,0:T(8,128)(2,1)S(1)}, bf16[4,128,256]{2,1,0:T(8,128)(2,1)S(1)}, u32[]{:S(2)}, u32[]{:S(2)}) collective-permute-start(bf16[4,128,256]{2,1,0:T(8,128)(2,1)S(1)} %order.9.refs_5_.refs_3_), channel_id=1, source_target_pairs={{0,1},{1,0},{2,3},{3,2},{4,5},{5,4},{6,7},{7,6},{8,9},{9,8},{10,11... | collective-permute-start | bytes 786440 | tf_op jit(solution)/shard_map/ppermute | solution.py:27
  61.2 7.5 %collective-permute-start.17 = (s16[528,256]{1,0:T(8,128)(2,1)S(1)}, s16[528,256]{1,0:T(8,128)(2,1)S(1)}, u32[]{:S(2)}, u32[]{:S(2)}) collective-permute-start(s16[528,256]{1,0:T(8,128)(2,1)S(1)} %get-tuple-element.110), channel_id=1, source_target_pairs={{0,1},{1,0},{2,3},{3,2},{4,5},{5,4},{6,7},{7,6},{8,9},{9,8},{10,11... | collective-permute-start | bytes 811016 | tf_op jit(solution)/shard_map/ppermute | solution.py:27
  66.6 6.8 %collective-permute-start.22 = (f32[512,256]{1,0:T(8,128)S(1)}, f32[512,256]{1,0:T(8,128)S(1)}, u32[]{:S(2)}, u32[]{:S(2)}) collective-permute-start(f32[512,256]{1,0:T(8,128)S(1)} %get-tuple-element.111.refs_3_.refs_0_), channel_id=1, source_target_pairs={{0,8},{8,0},{16,24},{24,16},{1,9},{9,1},{17,25},{25,17},{2,10},{10... | collective-permute-start | bytes 1572872 | tf_op jit(solution)/shard_map/ppermute | solution.py:27
  69.0 6.3 %collective-permute-start.19 = (s16[144,256]{1,0:T(8,128)(2,1)S(1)}, s16[144,256]{1,0:T(8,128)(2,1)S(1)}, u32[]{:S(2)}, u32[]{:S(2)}) collective-permute-start(s16[144,256]{1,0:T(8,128)(2,1)S(1)} %get-tuple-element.113), channel_id=1, source_target_pairs={{0,2},{1,3},{2,0},{3,1},{4,6},{5,7},{6,4},{7,5},{8,10},{9,11},{10,... | collective-permute-start | bytes 221192 | tf_op jit(solution)/shard_map/ppermute | solution.py:27
  69.3 6.9 %collective-permute-start.20 = (s16[144,256]{1,0:T(8,128)(2,1)S(1)}, s16[144,256]{1,0:T(8,128)(2,1)S(1)}, u32[]{:S(2)}, u32[]{:S(2)}) collective-permute-start(s16[144,256]{1,0:T(8,128)(2,1)S(1)} %get-tuple-element.114), channel_id=1, source_target_pairs={{0,4},{1,5},{2,6},{3,7},{4,0},{5,1},{6,2},{7,3},{8,12},{9,13},{10,... | collective-permute-start | bytes 221192 | tf_op jit(solution)/shard_map/ppermute | solution.py:27
  71.2 6.3 %collective-permute-start.21 = (s16[144,256]{1,0:T(8,128)(2,1)S(1)}, s16[144,256]{1,0:T(8,128)(2,1)S(1)}, u32[]{:S(2)}, u32[]{:S(2)}) collective-permute-start(s16[144,256]{1,0:T(8,128)(2,1)S(1)} %get-tuple-element.115), channel_id=1, source_target_pairs={{0,6},{1,7},{2,4},{3,5},{4,2},{5,3},{6,0},{7,1},{8,14},{9,15},{10,... | collective-permute-start | bytes 221192 | tf_op jit(solution)/shard_map/ppermute | solution.py:27
  73.6 8.3 %collective-permute-start.26 = (s16[528,256]{1,0:T(8,128)(2,1)S(1)}, s16[528,256]{1,0:T(8,128)(2,1)S(1)}, u32[]{:S(2)}, u32[]{:S(2)}) collective-permute-start(s16[528,256]{1,0:T(8,128)(2,1)S(1)} %get-tuple-element.117), channel_id=1, source_target_pairs={{0,16},{8,24},{16,0},{24,8},{1,17},{9,25},{17,1},{25,9},{2,18},{10... | collective-permute-start | bytes 811016 | tf_op jit(solution)/shard_map/ppermute | solution.py:27
  77.5 7.3 %collective-permute-start.25 = (bf16[128,256]{1,0:T(8,128)(2,1)S(1)}, bf16[128,256]{1,0:T(8,128)(2,1)S(1)}, u32[]{:S(2)}, u32[]{:S(2)}) collective-permute-start(bf16[128,256]{1,0:T(8,128)(2,1)S(1)} %finish.10.refs_5_.refs_1_), channel_id=1, source_target_pairs={{0,6},{1,7},{2,4},{3,5},{4,2},{5,3},{6,0},{7,1},{8,14},{9,15},{10,... | collective-permute-start | bytes 196616 | tf_op jit(solution)/shard_map/ppermute | solution.py:27
  83.3 7.6 %collective-permute-start.28 = (s16[528,256]{1,0:T(8,128)(2,1)S(1)}, s16[528,256]{1,0:T(8,128)(2,1)S(1)}, u32[]{:S(2)}, u32[]{:S(2)}) collective-permute-start(s16[528,256]{1,0:T(8,128)(2,1)S(1)} %get-tuple-element.119), channel_id=1, source_target_pairs={{0,1},{1,0},{2,3},{3,2},{4,5},{5,4},{6,7},{7,6},{8,9},{9,8},{10,11... | collective-permute-start | bytes 811016 | tf_op jit(solution)/shard_map/ppermute | solution.py:27
  85.4 10.2 %collective-permute-start.27 = (bf16[4,128,256]{2,1,0:T(8,128)(2,1)S(1)}, bf16[4,128,256]{2,1,0:T(8,128)(2,1)S(1)}, u32[]{:S(2)}, u32[]{:S(2)}) collective-permute-start(bf16[4,128,256]{2,1,0:T(8,128)(2,1)S(1)} %order.10.refs_3_.refs_4_), channel_id=1, source_target_pairs={{0,1},{1,0},{2,3},{3,2},{4,5},{5,4},{6,7},{7,6},{8,9},{9,8},{10,11... | collective-permute-start | bytes 786440 | tf_op jit(solution)/shard_map/ppermute | solution.py:27
  91.2 6.3 %collective-permute-start.30 = (s16[144,256]{1,0:T(8,128)(2,1)S(1)}, s16[144,256]{1,0:T(8,128)(2,1)S(1)}, u32[]{:S(2)}, u32[]{:S(2)}) collective-permute-start(s16[144,256]{1,0:T(8,128)(2,1)S(1)} %get-tuple-element.123), channel_id=1, source_target_pairs={{0,2},{1,3},{2,0},{3,1},{4,6},{5,7},{6,4},{7,5},{8,10},{9,11},{10,... | collective-permute-start | bytes 221192 | tf_op jit(solution)/shard_map/ppermute | solution.py:27
  93.6 6.2 %collective-permute-start.32 = (s16[144,256]{1,0:T(8,128)(2,1)S(1)}, s16[144,256]{1,0:T(8,128)(2,1)S(1)}, u32[]{:S(2)}, u32[]{:S(2)}) collective-permute-start(s16[144,256]{1,0:T(8,128)(2,1)S(1)} %get-tuple-element.125), channel_id=1, source_target_pairs={{0,6},{1,7},{2,4},{3,5},{4,2},{5,3},{6,0},{7,1},{8,14},{9,15},{10,... | collective-permute-start | bytes 221192 | tf_op jit(solution)/shard_map/ppermute | solution.py:27
  97.4 6.9 %collective-permute-start.29 = (f32[512,256]{1,0:T(8,128)S(1)}, f32[512,256]{1,0:T(8,128)S(1)}, u32[]{:S(2)}, u32[]{:S(2)}) collective-permute-start(f32[512,256]{1,0:T(8,128)S(1)} %get-tuple-element.122.refs_4_.refs_0_), channel_id=1, source_target_pairs={{0,8},{8,0},{16,24},{24,16},{1,9},{9,1},{17,25},{25,17},{2,10},{10... | collective-permute-start | bytes 1572872 | tf_op jit(solution)/shard_map/ppermute | solution.py:27
  99.9 6.3 %collective-permute-start.36 = (bf16[128,256]{1,0:T(8,128)(2,1)S(1)}, bf16[128,256]{1,0:T(8,128)(2,1)S(1)}, u32[]{:S(2)}, u32[]{:S(2)}) collective-permute-start(bf16[128,256]{1,0:T(8,128)(2,1)S(1)} %finish.11.refs_2_.refs_1_), channel_id=1, source_target_pairs={{0,6},{1,7},{2,4},{3,5},{4,2},{5,3},{6,0},{7,1},{8,14},{9,15},{10,... | collective-permute-start | bytes 196616 | tf_op jit(solution)/shard_map/ppermute | solution.py:27
  104.6 6.5 %collective-permute-start.33 = (s16[528,256]{1,0:T(8,128)(2,1)S(1)}, s16[528,256]{1,0:T(8,128)(2,1)S(1)}, u32[]{:S(2)}, u32[]{:S(2)}) collective-permute-start(s16[528,256]{1,0:T(8,128)(2,1)S(1)} %get-tuple-element.127), channel_id=1, source_target_pairs={{0,16},{8,24},{16,0},{24,8},{1,17},{9,25},{17,1},{25,9},{2,18},{10... | collective-permute-start | bytes 811016 | tf_op jit(solution)/shard_map/ppermute | solution.py:27
  107.5 8.9 %collective-permute-start.38 = (bf16[4,128,256]{2,1,0:T(8,128)(2,1)S(1)}, bf16[4,128,256]{2,1,0:T(8,128)(2,1)S(1)}, u32[]{:S(2)}, u32[]{:S(2)}) collective-permute-start(bf16[4,128,256]{2,1,0:T(8,128)(2,1)S(1)} %order.11.refs_5_.refs_4_), channel_id=1, source_target_pairs={{0,1},{1,0},{2,3},{3,2},{4,5},{5,4},{6,7},{7,6},{8,9},{9,8},{10,11... | collective-permute-start | bytes 786440 | tf_op jit(solution)/shard_map/ppermute | solution.py:27
  112.4 7.3 %collective-permute-start.37 = (s16[528,256]{1,0:T(8,128)(2,1)S(1)}, s16[528,256]{1,0:T(8,128)(2,1)S(1)}, u32[]{:S(2)}, u32[]{:S(2)}) collective-permute-start(s16[528,256]{1,0:T(8,128)(2,1)S(1)} %get-tuple-element.129), channel_id=1, source_target_pairs={{0,1},{1,0},{2,3},{3,2},{4,5},{5,4},{6,7},{7,6},{8,9},{9,8},{10,11... | collective-permute-start | bytes 811016 | tf_op jit(solution)/shard_map/ppermute | solution.py:27
  118.3 6.1 %collective-permute-start.42 = (f32[512,256]{1,0:T(8,128)S(1)}, f32[512,256]{1,0:T(8,128)S(1)}, u32[]{:S(2)}, u32[]{:S(2)}) collective-permute-start(f32[512,256]{1,0:T(8,128)S(1)} %get-tuple-element.131.refs_3_.refs_0_), channel_id=1, source_target_pairs={{0,8},{8,0},{16,24},{24,16},{1,9},{9,1},{17,25},{25,17},{2,10},{10... | collective-permute-start | bytes 1572872 | tf_op jit(solution)/shard_map/ppermute | solution.py:27
  119.9 6.3 %collective-permute-start.39 = (s16[144,256]{1,0:T(8,128)(2,1)S(1)}, s16[144,256]{1,0:T(8,128)(2,1)S(1)}, u32[]{:S(2)}, u32[]{:S(2)}) collective-permute-start(s16[144,256]{1,0:T(8,128)(2,1)S(1)} %get-tuple-element.133), channel_id=1, source_target_pairs={{0,2},{1,3},{2,0},{3,1},{4,6},{5,7},{6,4},{7,5},{8,10},{9,11},{10,... | collective-permute-start | bytes 221192 | tf_op jit(solution)/shard_map/ppermute | solution.py:27
  120.5 8.4 %collective-permute-start.40 = (s16[144,256]{1,0:T(8,128)(2,1)S(1)}, s16[144,256]{1,0:T(8,128)(2,1)S(1)}, u32[]{:S(2)}, u32[]{:S(2)}) collective-permute-start(s16[144,256]{1,0:T(8,128)(2,1)S(1)} %get-tuple-element.134), channel_id=1, source_target_pairs={{0,4},{1,5},{2,6},{3,7},{4,0},{5,1},{6,2},{7,3},{8,12},{9,13},{10,... | collective-permute-start | bytes 221192 | tf_op jit(solution)/shard_map/ppermute | solution.py:27
  122.6 6.3 %collective-permute-start.41 = (s16[144,256]{1,0:T(8,128)(2,1)S(1)}, s16[144,256]{1,0:T(8,128)(2,1)S(1)}, u32[]{:S(2)}, u32[]{:S(2)}) collective-permute-start(s16[144,256]{1,0:T(8,128)(2,1)S(1)} %get-tuple-element.135), channel_id=1, source_target_pairs={{0,6},{1,7},{2,4},{3,5},{4,2},{5,3},{6,0},{7,1},{8,14},{9,15},{10,... | collective-permute-start | bytes 221192 | tf_op jit(solution)/shard_map/ppermute | solution.py:27
  124.6 8.8 %collective-permute-start.46 = (s16[528,256]{1,0:T(8,128)(2,1)S(1)}, s16[528,256]{1,0:T(8,128)(2,1)S(1)}, u32[]{:S(2)}, u32[]{:S(2)}) collective-permute-start(s16[528,256]{1,0:T(8,128)(2,1)S(1)} %get-tuple-element.137), channel_id=1, source_target_pairs={{0,16},{8,24},{16,0},{24,8},{1,17},{9,25},{17,1},{25,9},{2,18},{10... | collective-permute-start | bytes 811016 | tf_op jit(solution)/shard_map/ppermute | solution.py:27
  129.0 7.3 %collective-permute-start.45 = (bf16[128,256]{1,0:T(8,128)(2,1)S(1)}, bf16[128,256]{1,0:T(8,128)(2,1)S(1)}, u32[]{:S(2)}, u32[]{:S(2)}) collective-permute-start(bf16[128,256]{1,0:T(8,128)(2,1)S(1)} %finish.12.refs_5_.refs_1_), channel_id=1, source_target_pairs={{0,6},{1,7},{2,4},{3,5},{4,2},{5,3},{6,0},{7,1},{8,14},{9,15},{10,... | collective-permute-start | bytes 196616 | tf_op jit(solution)/shard_map/ppermute | solution.py:27
  134.7 8.3 %collective-permute-start.48 = (s16[528,256]{1,0:T(8,128)(2,1)S(1)}, s16[528,256]{1,0:T(8,128)(2,1)S(1)}, u32[]{:S(2)}, u32[]{:S(2)}) collective-permute-start(s16[528,256]{1,0:T(8,128)(2,1)S(1)} %get-tuple-element.139), channel_id=1, source_target_pairs={{0,1},{1,0},{2,3},{3,2},{4,5},{5,4},{6,7},{7,6},{8,9},{9,8},{10,11... | collective-permute-start | bytes 811016 | tf_op jit(solution)/shard_map/ppermute | solution.py:27
  136.8 10.9 %collective-permute-start.47 = (bf16[4,128,256]{2,1,0:T(8,128)(2,1)S(1)}, bf16[4,128,256]{2,1,0:T(8,128)(2,1)S(1)}, u32[]{:S(2)}, u32[]{:S(2)}) collective-permute-start(bf16[4,128,256]{2,1,0:T(8,128)(2,1)S(1)} %order.12.refs_3_.refs_5_), channel_id=1, source_target_pairs={{0,1},{1,0},{2,3},{3,2},{4,5},{5,4},{6,7},{7,6},{8,9},{9,8},{10,11... | collective-permute-start | bytes 786440 | tf_op jit(solution)/shard_map/ppermute | solution.py:27
  143.3 7.3 %collective-permute-start.50 = (s16[144,256]{1,0:T(8,128)(2,1)S(1)}, s16[144,256]{1,0:T(8,128)(2,1)S(1)}, u32[]{:S(2)}, u32[]{:S(2)}) collective-permute-start(s16[144,256]{1,0:T(8,128)(2,1)S(1)} %get-tuple-element.142), channel_id=1, source_target_pairs={{0,2},{1,3},{2,0},{3,1},{4,6},{5,7},{6,4},{7,5},{8,10},{9,11},{10,... | collective-permute-start | bytes 221192 | tf_op jit(solution)/shard_map/ppermute | solution.py:27
  144.1 6.5 %collective-permute-start.51 = (s16[144,256]{1,0:T(8,128)(2,1)S(1)}, s16[144,256]{1,0:T(8,128)(2,1)S(1)}, u32[]{:S(2)}, u32[]{:S(2)}) collective-permute-start(s16[144,256]{1,0:T(8,128)(2,1)S(1)} %get-tuple-element.143), channel_id=1, source_target_pairs={{0,4},{1,5},{2,6},{3,7},{4,0},{5,1},{6,2},{7,3},{8,12},{9,13},{10,... | collective-permute-start | bytes 221192 | tf_op jit(solution)/shard_map/ppermute | solution.py:27
  145.6 6.2 %collective-permute-start.52 = (s16[144,256]{1,0:T(8,128)(2,1)S(1)}, s16[144,256]{1,0:T(8,128)(2,1)S(1)}, u32[]{:S(2)}, u32[]{:S(2)}) collective-permute-start(s16[144,256]{1,0:T(8,128)(2,1)S(1)} %get-tuple-element.144), channel_id=1, source_target_pairs={{0,6},{1,7},{2,4},{3,5},{4,2},{5,3},{6,0},{7,1},{8,14},{9,15},{10,... | collective-permute-start | bytes 221192 | tf_op jit(solution)/shard_map/ppermute | solution.py:27
  151.8 6.8 %collective-permute-start.56 = (bf16[128,256]{1,0:T(8,128)(2,1)S(1)}, bf16[128,256]{1,0:T(8,128)(2,1)S(1)}, u32[]{:S(2)}, u32[]{:S(2)}) collective-permute-start(bf16[128,256]{1,0:T(8,128)(2,1)S(1)} %finish.13.refs_2_.refs_1_), channel_id=1, source_target_pairs={{0,6},{1,7},{2,4},{3,5},{4,2},{5,3},{6,0},{7,1},{8,14},{9,15},{10,... | collective-permute-start | bytes 196616 | tf_op jit(solution)/shard_map/ppermute | solution.py:27
  156.5 7.0 %collective-permute-start.53 = (s16[528,256]{1,0:T(8,128)(2,1)S(1)}, s16[528,256]{1,0:T(8,128)(2,1)S(1)}, u32[]{:S(2)}, u32[]{:S(2)}) collective-permute-start(s16[528,256]{1,0:T(8,128)(2,1)S(1)} %get-tuple-element.146), channel_id=1, source_target_pairs={{0,16},{8,24},{16,0},{24,8},{1,17},{9,25},{17,1},{25,9},{2,18},{10... | collective-permute-start | bytes 811016 | tf_op jit(solution)/shard_map/ppermute | solution.py:27
  160.0 8.3 %collective-permute-start.58 = (bf16[4,128,256]{2,1,0:T(8,128)(2,1)S(1)}, bf16[4,128,256]{2,1,0:T(8,128)(2,1)S(1)}, u32[]{:S(2)}, u32[]{:S(2)}) collective-permute-start(bf16[4,128,256]{2,1,0:T(8,128)(2,1)S(1)} %order.13.refs_5_), channel_id=1, source_target_pairs={{0,1},{1,0},{2,3},{3,2},{4,5},{5,4},{6,7},{7,6},{8,9},{9,8},{10,11... | collective-permute-start | bytes 786440 | tf_op jit(solution)/shard_map/ppermute | solution.py:27
  164.8 7.7 %collective-permute-start.57 = (s16[528,256]{1,0:T(8,128)(2,1)S(1)}, s16[528,256]{1,0:T(8,128)(2,1)S(1)}, u32[]{:S(2)}, u32[]{:S(2)}) collective-permute-start(s16[528,256]{1,0:T(8,128)(2,1)S(1)} %get-tuple-element.148), channel_id=1, source_target_pairs={{0,1},{1,0},{2,3},{3,2},{4,5},{5,4},{6,7},{7,6},{8,9},{9,8},{10,11... | collective-permute-start | bytes 811016 | tf_op jit(solution)/shard_map/ppermute | solution.py:27
  171.1 6.2 %collective-permute-start.62 = (f32[512,256]{1,0:T(8,128)S(1)}, f32[512,256]{1,0:T(8,128)S(1)}, u32[]{:S(2)}, u32[]{:S(2)}) collective-permute-start(f32[512,256]{1,0:T(8,128)S(1)} %get-tuple-element.150.refs_3_.refs_0_), channel_id=1, source_target_pairs={{0,8},{8,0},{16,24},{24,16},{1,9},{9,1},{17,25},{25,17},{2,10},{10... | collective-permute-start | bytes 1572872 | tf_op jit(solution)/shard_map/ppermute | solution.py:27
  172.8 9.8 %collective-permute-start.59 = (s16[144,256]{1,0:T(8,128)(2,1)S(1)}, s16[144,256]{1,0:T(8,128)(2,1)S(1)}, u32[]{:S(2)}, u32[]{:S(2)}) collective-permute-start(s16[144,256]{1,0:T(8,128)(2,1)S(1)} %get-tuple-element.152), channel_id=1, source_target_pairs={{0,2},{1,3},{2,0},{3,1},{4,6},{5,7},{6,4},{7,5},{8,10},{9,11},{10,... | collective-permute-start | bytes 221192 | tf_op jit(solution)/shard_map/ppermute | solution.py:27
  173.3 9.3 %collective-permute-start.60 = (s16[144,256]{1,0:T(8,128)(2,1)S(1)}, s16[144,256]{1,0:T(8,128)(2,1)S(1)}, u32[]{:S(2)}, u32[]{:S(2)}) collective-permute-start(s16[144,256]{1,0:T(8,128)(2,1)S(1)} %get-tuple-element.153), channel_id=1, source_target_pairs={{0,4},{1,5},{2,6},{3,7},{4,0},{5,1},{6,2},{7,3},{8,12},{9,13},{10,... | collective-permute-start | bytes 221192 | tf_op jit(solution)/shard_map/ppermute | solution.py:27
  175.0 7.6 %collective-permute-start.61 = (s16[144,256]{1,0:T(8,128)(2,1)S(1)}, s16[144,256]{1,0:T(8,128)(2,1)S(1)}, u32[]{:S(2)}, u32[]{:S(2)}) collective-permute-start(s16[144,256]{1,0:T(8,128)(2,1)S(1)} %get-tuple-element.154), channel_id=1, source_target_pairs={{0,6},{1,7},{2,4},{3,5},{4,2},{5,3},{6,0},{7,1},{8,14},{9,15},{10,... | collective-permute-start | bytes 221192 | tf_op jit(solution)/shard_map/ppermute | solution.py:27
  177.4 9.7 %collective-permute-start.66 = (s16[528,256]{1,0:T(8,128)(2,1)S(1)}, s16[528,256]{1,0:T(8,128)(2,1)S(1)}, u32[]{:S(2)}, u32[]{:S(2)}) collective-permute-start(s16[528,256]{1,0:T(8,128)(2,1)S(1)} %get-tuple-element.158), channel_id=1, source_target_pairs={{0,16},{8,24},{16,0},{24,8},{1,17},{9,25},{17,1},{25,9},{2,18},{10... | collective-permute-start | bytes 811016 | tf_op jit(solution)/shard_map/ppermute | solution.py:27
  182.7 11.2 %collective-permute-start.65 = (bf16[128,256]{1,0:T(8,128)(2,1)S(1)}, bf16[128,256]{1,0:T(8,128)(2,1)S(1)}, u32[]{:S(2)}, u32[]{:S(2)}) collective-permute-start(bf16[128,256]{1,0:T(8,128)(2,1)S(1)} %finish.14.refs_5_.refs_1_), channel_id=1, source_target_pairs={{0,6},{1,7},{2,4},{3,5},{4,2},{5,3},{6,0},{7,1},{8,14},{9,15},{10,... | collective-permute-start | bytes 196616 | tf_op jit(solution)/shard_map/ppermute | solution.py:27
  184.9 9.1 %collective-permute-start.64 = (bf16[128,256]{1,0:T(8,128)(2,1)S(1)}, bf16[128,256]{1,0:T(8,128)(2,1)S(1)}, u32[]{:S(2)}, u32[]{:S(2)}) collective-permute-start(bf16[128,256]{1,0:T(8,128)(2,1)S(1)} %finish.14.refs_5_.refs_1_), channel_id=1, source_target_pairs={{0,4},{1,5},{2,6},{3,7},{4,0},{5,1},{6,2},{7,3},{8,12},{9,13},{10,... | collective-permute-start | bytes 196616 | tf_op jit(solution)/shard_map/ppermute | solution.py:27
  184.9 9.1 %collective-permute-start.63 = (bf16[128,256]{1,0:T(8,128)(2,1)S(1)}, bf16[128,256]{1,0:T(8,128)(2,1)S(1)}, u32[]{:S(2)}, u32[]{:S(2)}) collective-permute-start(bf16[128,256]{1,0:T(8,128)(2,1)S(1)} %finish.14.refs_5_.refs_1_), channel_id=1, source_target_pairs={{0,2},{1,3},{2,0},{3,1},{4,6},{5,7},{6,4},{7,5},{8,10},{9,11},{10,... | collective-permute-start | bytes 196616 | tf_op jit(solution)/shard_map/ppermute | solution.py:27
  188.5 7.8 %collective-permute-start.68 = (s16[528,256]{1,0:T(8,128)(2,1)S(1)}, s16[528,256]{1,0:T(8,128)(2,1)S(1)}, u32[]{:S(2)}, u32[]{:S(2)}) collective-permute-start(s16[528,256]{1,0:T(8,128)(2,1)S(1)} %get-tuple-element.161), channel_id=1, source_target_pairs={{0,1},{1,0},{2,3},{3,2},{4,5},{5,4},{6,7},{7,6},{8,9},{9,8},{10,11... | collective-permute-start | bytes 811016 | tf_op jit(solution)/shard_map/ppermute | solution.py:27
  194.0 7.0 %collective-permute-start.67 = (bf16[4,128,256]{2,1,0:T(8,128)(2,1)S(1)}, bf16[4,128,256]{2,1,0:T(8,128)(2,1)S(1)}, u32[]{:S(2)}, u32[]{:S(2)}) collective-permute-start(bf16[4,128,256]{2,1,0:T(8,128)(2,1)S(1)} %order.14.refs_3_.refs_1_), channel_id=1, source_target_pairs={{0,1},{1,0},{2,3},{3,2},{4,5},{5,4},{6,7},{7,6},{8,9},{9,8},{10,11... | collective-permute-start | bytes 786440 | tf_op jit(solution)/shard_map/ppermute | solution.py:27
  196.6 10.5 %collective-permute-start.69 = (s16[144,256]{1,0:T(8,128)(2,1)S(1)}, s16[144,256]{1,0:T(8,128)(2,1)S(1)}, u32[]{:S(2)}, u32[]{:S(2)}) collective-permute-start(s16[144,256]{1,0:T(8,128)(2,1)S(1)} %get-tuple-element.163), channel_id=1, source_target_pairs={{0,2},{1,3},{2,0},{3,1},{4,6},{5,7},{6,4},{7,5},{8,10},{9,11},{10,... | collective-permute-start | bytes 221192 | tf_op jit(solution)/shard_map/ppermute | solution.py:27
  196.7 10.4 %collective-permute-start.70 = (s16[144,256]{1,0:T(8,128)(2,1)S(1)}, s16[144,256]{1,0:T(8,128)(2,1)S(1)}, u32[]{:S(2)}, u32[]{:S(2)}) collective-permute-start(s16[144,256]{1,0:T(8,128)(2,1)S(1)} %get-tuple-element.164), channel_id=1, source_target_pairs={{0,4},{1,5},{2,6},{3,7},{4,0},{5,1},{6,2},{7,3},{8,12},{9,13},{10,... | collective-permute-start | bytes 221192 | tf_op jit(solution)/shard_map/ppermute | solution.py:27
  199.4 7.7 %collective-permute-start.71 = (s16[144,256]{1,0:T(8,128)(2,1)S(1)}, s16[144,256]{1,0:T(8,128)(2,1)S(1)}, u32[]{:S(2)}, u32[]{:S(2)}) collective-permute-start(s16[144,256]{1,0:T(8,128)(2,1)S(1)} %get-tuple-element.165), channel_id=1, source_target_pairs={{0,6},{1,7},{2,4},{3,5},{4,2},{5,3},{6,0},{7,1},{8,14},{9,15},{10,... | collective-permute-start | bytes 221192 | tf_op jit(solution)/shard_map/ppermute | solution.py:27
  207.0 9.4 %collective-permute-start.75 = (bf16[8,128,256]{2,1,0:T(8,128)(2,1)S(1)}, bf16[8,128,256]{2,1,0:T(8,128)(2,1)S(1)}, u32[]{:S(2)}, u32[]{:S(2)}) collective-permute-start(bf16[8,128,256]{2,1,0:T(8,128)(2,1)S(1)} %get-tuple-element.169), channel_id=1, source_target_pairs={{0,8},{8,0},{16,24},{24,16},{1,9},{9,1},{17,25},{25,17},{2,10},{10... | collective-permute-start | bytes 1572872 | tf_op jit(solution)/shard_map/ppermute | solution.py:27
  207.2 10.1 %collective-permute-start.74 = (bf16[128,256]{1,0:T(8,128)(2,1)S(1)}, bf16[128,256]{1,0:T(8,128)(2,1)S(1)}, u32[]{:S(2)}, u32[]{:S(2)}) collective-permute-start(bf16[128,256]{1,0:T(8,128)(2,1)S(1)} %finish.15.refs_9_.refs_1_), channel_id=1, source_target_pairs={{0,6},{1,7},{2,4},{3,5},{4,2},{5,3},{6,0},{7,1},{8,14},{9,15},{10,... | collective-permute-start | bytes 196616 | tf_op jit(solution)/shard_map/ppermute | solution.py:27
  209.4 7.9 %collective-permute-start.73 = (bf16[128,256]{1,0:T(8,128)(2,1)S(1)}, bf16[128,256]{1,0:T(8,128)(2,1)S(1)}, u32[]{:S(2)}, u32[]{:S(2)}) collective-permute-start(bf16[128,256]{1,0:T(8,128)(2,1)S(1)} %finish.15.refs_9_.refs_1_), channel_id=1, source_target_pairs={{0,4},{1,5},{2,6},{3,7},{4,0},{5,1},{6,2},{7,3},{8,12},{9,13},{10,... | collective-permute-start | bytes 196616 | tf_op jit(solution)/shard_map/ppermute | solution.py:27
  209.4 7.9 %collective-permute-start.72 = (bf16[128,256]{1,0:T(8,128)(2,1)S(1)}, bf16[128,256]{1,0:T(8,128)(2,1)S(1)}, u32[]{:S(2)}, u32[]{:S(2)}) collective-permute-start(bf16[128,256]{1,0:T(8,128)(2,1)S(1)} %finish.15.refs_9_.refs_1_), channel_id=1, source_target_pairs={{0,2},{1,3},{2,0},{3,1},{4,6},{5,7},{6,4},{7,5},{8,10},{9,11},{10,... | collective-permute-start | bytes 196616 | tf_op jit(solution)/shard_map/ppermute | solution.py:27
  217.3 8.7 %collective-permute-start.76 = (bf16[4,128,256]{2,1,0:T(8,128)(2,1)S(1)}, bf16[4,128,256]{2,1,0:T(8,128)(2,1)S(1)}, u32[]{:S(2)}, u32[]{:S(2)}) collective-permute-start(bf16[4,128,256]{2,1,0:T(8,128)(2,1)S(1)} %order.15.refs_1_.refs_3_), channel_id=1, source_target_pairs={{0,1},{1,0},{2,3},{3,2},{4,5},{5,4},{6,7},{7,6},{8,9},{9,8},{10,11... | collective-permute-start | bytes 786440 | tf_op jit(solution)/shard_map/ppermute | solution.py:27
  222.4 25.3 %collective-permute-start.81 = (bf16[8,128,256]{2,1,0:T(8,128)(2,1)}, bf16[8,128,256]{2,1,0:T(8,128)(2,1)}, u32[]{:S(2)}, u32[]{:S(2)}) collective-permute-start(bf16[8,128,256]{2,1,0:T(8,128)(2,1)} %add.35.refs_5_), channel_id=1, source_target_pairs={{0,16},{8,24},{16,0},{24,8},{1,17},{9,25},{17,1},{25,9},{2,18},{10... | collective-permute-start | bytes 1572872 | tf_op jit(solution)/shard_map/ppermute | solution.py:27
  233.0 14.7 %collective-permute-start.80 = (bf16[8,128,256]{2,1,0:T(8,128)(2,1)S(1)}, bf16[8,128,256]{2,1,0:T(8,128)(2,1)S(1)}, u32[]{:S(2)}, u32[]{:S(2)}) collective-permute-start(bf16[8,128,256]{2,1,0:T(8,128)(2,1)S(1)} %get-tuple-element.183), channel_id=1, source_target_pairs={{0,8},{8,0},{16,24},{24,16},{1,9},{9,1},{17,25},{25,17},{2,10},{10... | collective-permute-start | bytes 1572872 | tf_op jit(solution)/shard_map/ppermute | solution.py:27
  236.9 18.5 %collective-permute-start.79 = (bf16[8,128,256]{2,1,0:T(8,128)(2,1)S(1)}, bf16[8,128,256]{2,1,0:T(8,128)(2,1)S(1)}, u32[]{:S(2)}, u32[]{:S(2)}) collective-permute-start(bf16[8,128,256]{2,1,0:T(8,128)(2,1)S(1)} %add.36.refs_9_), channel_id=1, source_target_pairs={{0,16},{8,24},{16,0},{24,8},{1,17},{9,25},{17,1},{25,9},{2,18},{10... | collective-permute-start | bytes 1572872 | tf_op jit(solution)/shard_map/ppermute | solution.py:27
  247.6 7.9 %collective-permute-start.78 = (bf16[8,128,256]{2,1,0:T(8,128)(2,1)S(1)}, bf16[8,128,256]{2,1,0:T(8,128)(2,1)S(1)}, u32[]{:S(2)}, u32[]{:S(2)}) collective-permute-start(bf16[8,128,256]{2,1,0:T(8,128)(2,1)S(1)} %get-tuple-element.181), channel_id=1, source_target_pairs={{0,8},{8,0},{16,24},{24,16},{1,9},{9,1},{17,25},{25,17},{2,10},{10... | collective-permute-start | bytes 1572872 | tf_op jit(solution)/shard_map/ppermute | solution.py:27
  (38 other events, 345.7 us)

commit v3 on v2

--- a/solution.py
+++ b/solution.py
@@ -299,11 +299,15 @@
             )
 
         def invert(k, h, update):
+            b_all, d_all = rhs, inverse
+            if k == 0 and h == 0:
+                b_all = pltpu.with_memory_space_constraint(rhs, pltpu.HBM)
+                d_all = pltpu.with_memory_space_constraint(inverse, pltpu.HBM)
             outs = [shape((outer, rows, part), F32)]
             outs += [shape((outer * rows + EXTRA, part), CODE)] * (inner - 1)
             return call(
                 functools.partial(inverse_kernel, k, h, len(update), inner),
-                [inner_own, rhs, inverse] + update,
+                [inner_own, b_all, d_all] + update,
                 [SMEM, HBM, HBM] + [VMEM] * len(update),
                 outs,
                 "inverse",
@@ -506,15 +510,15 @@
                 for d in range(1, cores):
                     arrived.append(swap(rows_of(d, BF16), "prow", nr, d))
                     yield
+                if e == 0 and h < SPLITS - 1:
+                    for _ in range(PAUSE):
+                        yield
                 total = rows_of(0, F32)
                 if e == 0:
                     trail_sums[h] = [total] + arrived + received
                 else:
                     received.append(swap(add([total] + arrived, BF16, "add"), "prow", nr, e * cores))
                 yield
-                if e == lines - 1 and h < SPLITS - 1:
-                    for _ in range(PAUSE):
-                        yield
 
         chains = [chain_of(h) for h in range(SPLITS)]
         alive = [True] * SPLITS

time: 258 us -> 253 us (0.981)
  local copies, waits for them, and re-layouts: 5.61 us -> 1.91 us
    unnamed x40, local copies, waits for them, and re-layouts: 5.61 us -> 1.91 us
  transfers between devices with their start and end apart: 82 -> 82, of which waited for: 33 -> 32; matrix products, arithmetic and copies ran while one was open for 0% -> 0% of each run, Pallas kernels for 28% -> 29%
where the time goes in v3:
time: 253 us
  starting transfers between devices  109 us (43%)
  Pallas kernels  77.4 us (31%)
  waiting for transfers between devices  62.4 us (25%)
    ppermute x82, starting transfers between devices, swap(): return lax.ppermute(value, axis, [(s, s ^ mask) for s in range(count)])  109 us
    ppermute x82, waiting for transfers between devices, swap(): return lax.ppermute(value, axis, [(s, s ^ mask) for s in range(count)])  62.4 us
    pallas_call x10, Pallas kernels, trail_product(): pl.pallas_call(run, grid_spec=pltpu.PrefetchScalarGridSpec(num_scalar_pre...  41.1 us
    pallas_call x48, Pallas kernels, call(): pl.pallas_call(run, in_specs=specs, out_specs=[VMEM] * len(outs), out_sha...  28.1 us
  transfers between devices with their start and end apart: 82, of which 32 were waited for; matrix products, arithmetic and copies ran while one was open for 0% of the time, Pallas kernels for 29%

profile of v3, /device:TPU:0, one launch (start us, length us, event | category | flops | bytes accessed | tf_op | source)
XLA Modules:
  0.0 252.7 jit_solution(14233019865286925563)
XLA Ops:
  0.6 2.3 inverse.8
  3.0 3.0 %collective-permute-start = (s16[528,256]{1,0:T(8,128)(2,1)S(1)}, s16[528,256]{1,0:T(8,128)(2,1)S(1)}, u32[]{:S(2)}, u32[]{:S(2)}) collective-permute-start(s16[528,256]{1,0:T(8,128)(2,1)S(1)} %get-tuple-element.94), channel_id=1, source_target_pairs={{0,1},{1,0},{2,3},{3,2},{4,5},{5,4},{6,7},{7,6},{8,9},{9,8},{10,11... | collective-permute-start | bytes 811016 | tf_op jit(solution)/shard_map/ppermute | solution.py:27
  6.0 6.5 %collective-permute-done.refs_2_ = s16[528,256]{1,0:T(8,128)(2,1)S(1)} collective-permute-done((s16[528,256]{1,0:T(8,128)(2,1)S(1)}, s16[528,256]{1,0:T(8,128)(2,1)S(1)}, u32[]{:S(2)}, u32[]{:S(2)}) %collective-permute-start) | collective-permute-done | bytes 270368 | tf_op jit(solution)/shard_map/ppermute | solution.py:27
  12.7 1.9 collective-permute-start.1
  14.6 2.6 %collective-permute-start.2 = (s16[144,256]{1,0:T(8,128)(2,1)S(1)}, s16[144,256]{1,0:T(8,128)(2,1)S(1)}, u32[]{:S(2)}, u32[]{:S(2)}) collective-permute-start(s16[144,256]{1,0:T(8,128)(2,1)S(1)} %get-tuple-element.97), channel_id=1, source_target_pairs={{0,4},{1,5},{2,6},{3,7},{4,0},{5,1},{6,2},{7,3},{8,12},{9,13},{10,... | collective-permute-start | bytes 221192 | tf_op jit(solution)/shard_map/ppermute | solution.py:27
  17.8 3.7 %collective-permute-done.2.refs_2_ = s16[144,256]{1,0:T(8,128)(2,1)S(1)} collective-permute-done((s16[144,256]{1,0:T(8,128)(2,1)S(1)}, s16[144,256]{1,0:T(8,128)(2,1)S(1)}, u32[]{:S(2)}, u32[]{:S(2)}) %collective-permute-start.2) | collective-permute-done | bytes 73760 | tf_op jit(solution)/shard_map/ppermute | solution.py:27
  21.5 1.9 collective-permute-done.3.refs_3_
  23.5 2.0 collective-permute-start.6
  25.7 2.2 collective-permute-start.4
  33.0 4.0 %collective-permute-done.8.refs_2_ = s16[528,256]{1,0:T(8,128)(2,1)S(1)} collective-permute-done((s16[528,256]{1,0:T(8,128)(2,1)S(1)}, s16[528,256]{1,0:T(8,128)(2,1)S(1)}, u32[]{:S(2)}, u32[]{:S(2)}) %collective-permute-start.8) | collective-permute-done | bytes 270368 | tf_op jit(solution)/shard_map/ppermute | solution.py:27
  37.6 1.6 collective-permute-start.11
  39.2 2.5 collective-permute-start.12
  43.1 2.3 collective-permute-done.12.refs_3_
  45.4 2.6 %collective-permute-start.16 = (bf16[128,256]{1,0:T(8,128)(2,1)S(1)}, bf16[128,256]{1,0:T(8,128)(2,1)S(1)}, u32[]{:S(2)}, u32[]{:S(2)}) collective-permute-start(bf16[128,256]{1,0:T(8,128)(2,1)S(1)} %finish.9.refs_2_.refs_1_), channel_id=1, source_target_pairs={{0,6},{1,7},{2,4},{3,5},{4,2},{5,3},{6,0},{7,1},{8,14},{9,15},{10,... | collective-permute-start | bytes 196616 | tf_op jit(solution)/shard_map/ppermute | solution.py:27
  48.1 1.8 collective-permute-start.14
  54.8 1.8 collective-permute-done.13.refs_4_
  59.5 2.7 %collective-permute-done.18.refs_4_ = bf16[4,128,256]{2,1,0:T(8,128)(2,1)S(1)} collective-permute-done((bf16[4,128,256]{2,1,0:T(8,128)(2,1)S(1)}, bf16[4,128,256]{2,1,0:T(8,128)(2,1)S(1)}, u32[]{:S(2)}, u32[]{:S(2)}) %collective-permute-start.18) | collective-permute-done | bytes 262176 | tf_op jit(solution)/shard_map/ppermute | solution.py:27
  63.5 2.0 collective-permute-done.17.refs_2_
  66.1 1.9 collective-permute-start.20
  68.0 2.2 collective-permute-start.21
  74.3 2.3 collective-permute-start.25
  83.8 4.0 %collective-permute-done.28.refs_2_ = s16[528,256]{1,0:T(8,128)(2,1)S(1)} collective-permute-done((s16[528,256]{1,0:T(8,128)(2,1)S(1)}, s16[528,256]{1,0:T(8,128)(2,1)S(1)}, u32[]{:S(2)}, u32[]{:S(2)}) %collective-permute-start.28) | collective-permute-done | bytes 270368 | tf_op jit(solution)/shard_map/ppermute | solution.py:27
  88.3 2.1 collective-permute-start.31
  90.4 2.0 collective-permute-start.32
  92.4 1.8 coupling.8
  94.3 2.3 collective-permute-done.32.refs_3_
  96.7 2.1 collective-permute-start.36
  98.8 2.4 collective-permute-start.34
  105.8 2.1 collective-permute-done.33.refs_4_
  110.8 2.3 collective-permute-done.38.refs_5_
  113.1 1.8 coupling.9
  117.3 2.1 collective-permute-start.40
  119.4 1.8 collective-permute-start.41
  123.0 1.7 collective-permute-done.40.refs_2_
  125.7 1.9 collective-permute-start.45
  128.4 1.7 collective-permute-start.43
  135.0 4.7 %collective-permute-done.48.refs_2_ = s16[528,256]{1,0:T(8,128)(2,1)S(1)} collective-permute-done((s16[528,256]{1,0:T(8,128)(2,1)S(1)}, s16[528,256]{1,0:T(8,128)(2,1)S(1)}, u32[]{:S(2)}, u32[]{:S(2)}) %collective-permute-start.48) | collective-permute-done | bytes 270368 | tf_op jit(solution)/shard_map/ppermute | solution.py:27
  142.2 2.1 collective-permute-start.52
  144.4 2.8 %coupling.10 = (f32[512,256]{1,0:T(8,128)S(1)}, bf16[4,2,128,256]{3,2,1,0:T(8,128)(2,1)S(1)}) custom-call(s32[1]{0:T(128)} %bitcast.refs_0_, s32[16,32]{1,0:T(8,128)S(1)} %bitcast.78, bf16[16,1,32,1,128,128]{5,4,3,2,1,0:T(8,128)(2,1)S(1)} %bitcast.73, bf16[1024,256]{1,0:T(8,128)(2,1)S(1)} %bitcast.32, bf16[1024,256]{1,0:T(8,128)(2,1)S(1)} %bitcast.45, ...), custom_call_target="tpu_custom_call" | custom-call | flops 10000000000 | bytes 1 | tf_op jit(solution)/shard_map/coupling/pallas_call | solution.py:260
  148.6 2.1 collective-permute-start.56
  150.7 2.3 collective-permute-start.54
  155.2 1.9 collective-permute-done.55.refs_3_
  158.7 1.6 collective-permute-done.53.refs_4_
  163.3 3.2 %collective-permute-done.58.refs_6_ = bf16[4,128,256]{2,1,0:T(8,128)(2,1)S(1)} collective-permute-done((bf16[4,128,256]{2,1,0:T(8,128)(2,1)S(1)}, bf16[4,128,256]{2,1,0:T(8,128)(2,1)S(1)}, u32[]{:S(2)}, u32[]{:S(2)}) %collective-permute-start.58) | collective-permute-done | bytes 262176 | tf_op jit(solution)/shard_map/ppermute | solution.py:27
  166.5 2.8 %coupling.11 = (f32[512,256]{1,0:T(8,128)S(1)}, bf16[4,2,128,256]{3,2,1,0:T(8,128)(2,1)S(1)}) custom-call(s32[1]{0:T(128)} %bitcast.refs_0_, s32[16,32]{1,0:T(8,128)S(1)} %bitcast.79, bf16[16,1,32,1,128,128]{5,4,3,2,1,0:T(8,128)(2,1)S(1)} %bitcast.73, bf16[1024,256]{1,0:T(8,128)(2,1)S(1)} %bitcast.39, bf16[1024,256]{1,0:T(8,128)(2,1)S(1)} %bitcast.51, ...), custom_call_target="tpu_custom_call" | custom-call | flops 10000000000 | bytes 1 | tf_op jit(solution)/shard_map/coupling/pallas_call | solution.py:260
  169.5 2.1 join.2.refs_2_
  173.2 3.1 %collective-permute-start.61 = (s16[144,256]{1,0:T(8,128)(2,1)S(1)}, s16[144,256]{1,0:T(8,128)(2,1)S(1)}, u32[]{:S(2)}, u32[]{:S(2)}) collective-permute-start(s16[144,256]{1,0:T(8,128)(2,1)S(1)} %get-tuple-element.154), channel_id=1, source_target_pairs={{0,6},{1,7},{2,4},{3,5},{4,2},{5,3},{6,0},{7,1},{8,14},{9,15},{10,... | collective-permute-start | bytes 221192 | tf_op jit(solution)/shard_map/ppermute | solution.py:27
  176.6 1.6 collective-permute-start.66
  178.2 3.9 %trail.10 = (f32[8,128,256]{2,1,0:T(8,128)S(1)}, f32[8,128]{1,0:T(8,128)S(1)}) custom-call(s32[1]{0:T(128)} %bitcast.7.refs_0_, bf16[32,1,32,1,128,128]{5,4,3,2,1,0:T(8,128)(2,1)} %refs_4_.11, bf16[32,1,32,1,128,128]{5,4,3,2,1,0:T(8,128)(2,1)} %refs_4_.11, bf16[32,1,32,1,128,128]{5,4,3,2,1,0:T(8,128)(2,1)} %refs_4_.11, bf16[1024,256]{1,0:T(8,128)(2,1)S(1)} %bitcast.41, ...), custom_call_target="tpu_custom_call" | custom-call | flops 10000000000 | bytes 1 | tf_op jit(solution)/shard_map/trail/pallas_call | solution.py:383
  184.6 2.1 collective-permute-start.63
  188.9 3.9 %trail.11 = (f32[8,128,256]{2,1,0:T(8,128)S(1)}, f32[8,128]{1,0:T(8,128)S(1)}) custom-call(s32[1]{0:T(128)} %bitcast.9.refs_0_, bf16[32,1,32,1,128,128]{5,4,3,2,1,0:T(8,128)(2,1)} %refs_4_.11, bf16[32,1,32,1,128,128]{5,4,3,2,1,0:T(8,128)(2,1)} %refs_4_.11, bf16[32,1,32,1,128,128]{5,4,3,2,1,0:T(8,128)(2,1)} %refs_4_.11, bf16[1024,256]{1,0:T(8,128)(2,1)S(1)} %bitcast.42, ...), custom_call_target="tpu_custom_call" | custom-call | flops 10000000000 | bytes 1 | tf_op jit(solution)/shard_map/trail/pallas_call | solution.py:383
  194.1 2.0 collective-permute-done.68.refs_2_
  197.8 3.0 %collective-permute-start.71 = (s16[144,256]{1,0:T(8,128)(2,1)S(1)}, s16[144,256]{1,0:T(8,128)(2,1)S(1)}, u32[]{:S(2)}, u32[]{:S(2)}) collective-permute-start(s16[144,256]{1,0:T(8,128)(2,1)S(1)} %get-tuple-element.165), channel_id=1, source_target_pairs={{0,6},{1,7},{2,4},{3,5},{4,2},{5,3},{6,0},{7,1},{8,14},{9,15},{10,... | collective-permute-start | bytes 221192 | tf_op jit(solution)/shard_map/ppermute | solution.py:27
  202.2 4.8 %trail.12 = (bf16[8,128,256]{2,1,0:T(8,128)(2,1)S(1)}, f32[8,128]{1,0:T(8,128)S(1)}) custom-call(s32[1]{0:T(128)} %bitcast.7.refs_0_, bf16[32,1,32,1,128,128]{5,4,3,2,1,0:T(8,128)(2,1)} %refs_4_.11, bf16[32,1,32,1,128,128]{5,4,3,2,1,0:T(8,128)(2,1)} %refs_4_.11, bf16[32,1,32,1,128,128]{5,4,3,2,1,0:T(8,128)(2,1)} %refs_4_.11, ...), custom_call_target="tpu_custom_call" | custom-call | flops 10000000000 | bytes 1 | tf_op jit(solution)/shard_map/trail/pallas_call | solution.py:383
  209.3 2.3 collective-permute-start.72
  211.6 4.8 %trail.13 = (f32[8,128,256]{2,1,0:T(8,128)S(1)}, f32[8,128]{1,0:T(8,128)S(1)}) custom-call(s32[1]{0:T(128)} %bitcast.9.refs_0_, bf16[32,1,32,1,128,128]{5,4,3,2,1,0:T(8,128)(2,1)} %refs_4_.11, bf16[32,1,32,1,128,128]{5,4,3,2,1,0:T(8,128)(2,1)} %refs_4_.11, bf16[32,1,32,1,128,128]{5,4,3,2,1,0:T(8,128)(2,1)} %refs_4_.11, ...), custom_call_target="tpu_custom_call" | custom-call | flops 10000000000 | bytes 1 | tf_op jit(solution)/shard_map/trail/pallas_call | solution.py:383
  219.6 4.8 %trail.14 = (bf16[8,128,256]{2,1,0:T(8,128)(2,1)S(1)}, f32[8,128]{1,0:T(8,128)S(1)}) custom-call(s32[1]{0:T(128)} %bitcast.13.refs_0_, bf16[32,1,32,1,128,128]{5,4,3,2,1,0:T(8,128)(2,1)} %refs_4_.11, bf16[32,1,32,1,128,128]{5,4,3,2,1,0:T(8,128)(2,1)} %refs_4_.11, bf16[32,1,32,1,128,128]{5,4,3,2,1,0:T(8,128)(2,1)} %refs_4_.11, ...), custom_call_target="tpu_custom_call" | custom-call | flops 10000000000 | bytes 1 | tf_op jit(solution)/shard_map/trail/pallas_call | solution.py:383
  225.7 2.2 trail.15
  229.0 2.1 trail.16
  232.7 4.8 %trail.17 = (f32[8,128,256]{2,1,0:T(8,128)S(1)}, f32[8,128]{1,0:T(8,128)S(1)}) custom-call(s32[1]{0:T(128)} %bitcast.23.refs_0_, bf16[32,1,32,1,128,128]{5,4,3,2,1,0:T(8,128)(2,1)} %refs_4_.11, bf16[32,1,32,1,128,128]{5,4,3,2,1,0:T(8,128)(2,1)} %refs_4_.11, bf16[32,1,32,1,128,128]{5,4,3,2,1,0:T(8,128)(2,1)} %refs_4_.11, ...), custom_call_target="tpu_custom_call" | custom-call | flops 10000000000 | bytes 1 | tf_op jit(solution)/shard_map/trail/pallas_call | solution.py:383
  237.4 4.8 %trail.18 = (bf16[8,128,256]{2,1,0:T(8,128)(2,1)S(1)}, f32[8,128]{1,0:T(8,128)S(1)}) custom-call(s32[1]{0:T(128)} %bitcast.13.refs_0_, bf16[32,1,32,1,128,128]{5,4,3,2,1,0:T(8,128)(2,1)} %refs_4_.11, bf16[32,1,32,1,128,128]{5,4,3,2,1,0:T(8,128)(2,1)} %refs_4_.11, bf16[32,1,32,1,128,128]{5,4,3,2,1,0:T(8,128)(2,1)} %refs_4_.11, ...), custom_call_target="tpu_custom_call" | custom-call | flops 10000000000 | bytes 1 | tf_op jit(solution)/shard_map/trail/pallas_call | solution.py:383
  242.5 2.5 %subtract.2.refs_4_ = f32[8,1,128,512]{3,2,1,0:T(8,128)} custom-call(f32[8,1,128,512]{3,2,1,0:T(8,128)} %refs_0_.3, f32[8,128,256]{2,1,0:T(8,128)S(1)} %get-tuple-element.182.refs_1_, bf16[8,128,256]{2,1,0:T(8,128)(2,1)S(1)} %collective-permute-done.80.refs_2_, bf16[8,128,256]{2,1,0:T(8,128)(2,1)} %collective-permute-done.81.refs_3_), custom_call_target="tpu_custom_call" | custom-call | bytes 3145728 | tf_op jit(solution)/shard_map/subtract/pallas_call | solution.py:442
  245.1 5.2 %trail.19 = (f32[8,128,256]{2,1,0:T(8,128)S(1)}, f32[8,128]{1,0:T(8,128)}) custom-call(s32[1]{0:T(128)} %bitcast.23.refs_0_, bf16[32,1,32,1,128,128]{5,4,3,2,1,0:T(8,128)(2,1)} %refs_4_.11, bf16[32,1,32,1,128,128]{5,4,3,2,1,0:T(8,128)(2,1)} %refs_4_.11, bf16[32,1,32,1,128,128]{5,4,3,2,1,0:T(8,128)(2,1)} %refs_4_.11, ...), custom_call_target="tpu_custom_call" | custom-call | flops 10000000000 | bytes 1 | tf_op jit(solution)/shard_map/trail/pallas_call | solution.py:383
  250.3 2.4 subtract.3
  (205 shorter events, 79.6 us)
Async XLA Ops:
  3.0 9.5 %collective-permute-start = (s16[528,256]{1,0:T(8,128)(2,1)S(1)}, s16[528,256]{1,0:T(8,128)(2,1)S(1)}, u32[]{:S(2)}, u32[]{:S(2)}) collective-permute-start(s16[528,256]{1,0:T(8,128)(2,1)S(1)} %get-tuple-element.94), channel_id=1, source_target_pairs={{0,1},{1,0},{2,3},{3,2},{4,5},{5,4},{6,7},{7,6},{8,9},{9,8},{10,11... | collective-permute-start | bytes 811016 | tf_op jit(solution)/shard_map/ppermute | solution.py:27
  14.6 6.9 %collective-permute-start.2 = (s16[144,256]{1,0:T(8,128)(2,1)S(1)}, s16[144,256]{1,0:T(8,128)(2,1)S(1)}, u32[]{:S(2)}, u32[]{:S(2)}) collective-permute-start(s16[144,256]{1,0:T(8,128)(2,1)S(1)} %get-tuple-element.97), channel_id=1, source_target_pairs={{0,4},{1,5},{2,6},{3,7},{4,0},{5,1},{6,2},{7,3},{8,12},{9,13},{10,... | collective-permute-start | bytes 221192 | tf_op jit(solution)/shard_map/ppermute | solution.py:27
  17.1 6.3 %collective-permute-start.3 = (s16[144,256]{1,0:T(8,128)(2,1)S(1)}, s16[144,256]{1,0:T(8,128)(2,1)S(1)}, u32[]{:S(2)}, u32[]{:S(2)}) collective-permute-start(s16[144,256]{1,0:T(8,128)(2,1)S(1)} %get-tuple-element.98), channel_id=1, source_target_pairs={{0,6},{1,7},{2,4},{3,5},{4,2},{5,3},{6,0},{7,1},{8,14},{9,15},{10,... | collective-permute-start | bytes 221192 | tf_op jit(solution)/shard_map/ppermute | solution.py:27
  23.5 7.2 %collective-permute-start.6 = (bf16[128,256]{1,0:T(8,128)(2,1)S(1)}, bf16[128,256]{1,0:T(8,128)(2,1)S(1)}, u32[]{:S(2)}, u32[]{:S(2)}) collective-permute-start(bf16[128,256]{1,0:T(8,128)(2,1)S(1)} %finish.8.refs_3_.refs_1_), channel_id=1, source_target_pairs={{0,6},{1,7},{2,4},{3,5},{4,2},{5,3},{6,0},{7,1},{8,14},{9,15},{10,... | collective-permute-start | bytes 196616 | tf_op jit(solution)/shard_map/ppermute | solution.py:27
  29.1 7.9 %collective-permute-start.8 = (s16[528,256]{1,0:T(8,128)(2,1)S(1)}, s16[528,256]{1,0:T(8,128)(2,1)S(1)}, u32[]{:S(2)}, u32[]{:S(2)}) collective-permute-start(s16[528,256]{1,0:T(8,128)(2,1)S(1)} %get-tuple-element.100), channel_id=1, source_target_pairs={{0,1},{1,0},{2,3},{3,2},{4,5},{5,4},{6,7},{7,6},{8,9},{9,8},{10,11... | collective-permute-start | bytes 811016 | tf_op jit(solution)/shard_map/ppermute | solution.py:27
  31.4 10.3 %collective-permute-start.7 = (bf16[4,128,256]{2,1,0:T(8,128)(2,1)S(1)}, bf16[4,128,256]{2,1,0:T(8,128)(2,1)S(1)}, u32[]{:S(2)}, u32[]{:S(2)}) collective-permute-start(bf16[4,128,256]{2,1,0:T(8,128)(2,1)S(1)} %order.8.refs_3_), channel_id=1, source_target_pairs={{0,1},{1,0},{2,3},{3,2},{4,5},{5,4},{6,7},{7,6},{8,9},{9,8},{10,11... | collective-permute-start | bytes 786440 | tf_op jit(solution)/shard_map/ppermute | solution.py:27
  43.0 6.9 %collective-permute-start.9 = (f32[512,256]{1,0:T(8,128)S(1)}, f32[512,256]{1,0:T(8,128)S(1)}, u32[]{:S(2)}, u32[]{:S(2)}) collective-permute-start(f32[512,256]{1,0:T(8,128)S(1)} %get-tuple-element.103.refs_4_.refs_0_), channel_id=1, source_target_pairs={{0,8},{8,0},{16,24},{24,16},{1,9},{9,1},{17,25},{25,17},{2,10},{10... | collective-permute-start | bytes 1572872 | tf_op jit(solution)/shard_map/ppermute | solution.py:27
  45.4 6.3 %collective-permute-start.16 = (bf16[128,256]{1,0:T(8,128)(2,1)S(1)}, bf16[128,256]{1,0:T(8,128)(2,1)S(1)}, u32[]{:S(2)}, u32[]{:S(2)}) collective-permute-start(bf16[128,256]{1,0:T(8,128)(2,1)S(1)} %finish.9.refs_2_.refs_1_), channel_id=1, source_target_pairs={{0,6},{1,7},{2,4},{3,5},{4,2},{5,3},{6,0},{7,1},{8,14},{9,15},{10,... | collective-permute-start | bytes 196616 | tf_op jit(solution)/shard_map/ppermute | solution.py:27
  50.1 6.5 %collective-permute-start.13 = (s16[528,256]{1,0:T(8,128)(2,1)S(1)}, s16[528,256]{1,0:T(8,128)(2,1)S(1)}, u32[]{:S(2)}, u32[]{:S(2)}) collective-permute-start(s16[528,256]{1,0:T(8,128)(2,1)S(1)} %get-tuple-element.108), channel_id=1, source_target_pairs={{0,16},{8,24},{16,0},{24,8},{1,17},{9,25},{17,1},{25,9},{2,18},{10... | collective-permute-start | bytes 811016 | tf_op jit(solution)/shard_map/ppermute | solution.py:27
  53.3 8.9 %collective-permute-start.18 = (bf16[4,128,256]{2,1,0:T(8,128)(2,1)S(1)}, bf16[4,128,256]{2,1,0:T(8,128)(2,1)S(1)}, u32[]{:S(2)}, u32[]{:S(2)}) collective-permute-start(bf16[4,128,256]{2,1,0:T(8,128)(2,1)S(1)} %order.9.refs_5_.refs_3_), channel_id=1, source_target_pairs={{0,1},{1,0},{2,3},{3,2},{4,5},{5,4},{6,7},{7,6},{8,9},{9,8},{10,11... | collective-permute-start | bytes 786440 | tf_op jit(solution)/shard_map/ppermute | solution.py:27
  58.0 7.5 %collective-permute-start.17 = (s16[528,256]{1,0:T(8,128)(2,1)S(1)}, s16[528,256]{1,0:T(8,128)(2,1)S(1)}, u32[]{:S(2)}, u32[]{:S(2)}) collective-permute-start(s16[528,256]{1,0:T(8,128)(2,1)S(1)} %get-tuple-element.110), channel_id=1, source_target_pairs={{0,1},{1,0},{2,3},{3,2},{4,5},{5,4},{6,7},{7,6},{8,9},{9,8},{10,11... | collective-permute-start | bytes 811016 | tf_op jit(solution)/shard_map/ppermute | solution.py:27
  63.4 6.8 %collective-permute-start.22 = (f32[512,256]{1,0:T(8,128)S(1)}, f32[512,256]{1,0:T(8,128)S(1)}, u32[]{:S(2)}, u32[]{:S(2)}) collective-permute-start(f32[512,256]{1,0:T(8,128)S(1)} %get-tuple-element.111.refs_3_.refs_0_), channel_id=1, source_target_pairs={{0,8},{8,0},{16,24},{24,16},{1,9},{9,1},{17,25},{25,17},{2,10},{10... | collective-permute-start | bytes 1572872 | tf_op jit(solution)/shard_map/ppermute | solution.py:27
  65.7 6.3 %collective-permute-start.19 = (s16[144,256]{1,0:T(8,128)(2,1)S(1)}, s16[144,256]{1,0:T(8,128)(2,1)S(1)}, u32[]{:S(2)}, u32[]{:S(2)}) collective-permute-start(s16[144,256]{1,0:T(8,128)(2,1)S(1)} %get-tuple-element.113), channel_id=1, source_target_pairs={{0,2},{1,3},{2,0},{3,1},{4,6},{5,7},{6,4},{7,5},{8,10},{9,11},{10,... | collective-permute-start | bytes 221192 | tf_op jit(solution)/shard_map/ppermute | solution.py:27
  66.1 6.9 %collective-permute-start.20 = (s16[144,256]{1,0:T(8,128)(2,1)S(1)}, s16[144,256]{1,0:T(8,128)(2,1)S(1)}, u32[]{:S(2)}, u32[]{:S(2)}) collective-permute-start(s16[144,256]{1,0:T(8,128)(2,1)S(1)} %get-tuple-element.114), channel_id=1, source_target_pairs={{0,4},{1,5},{2,6},{3,7},{4,0},{5,1},{6,2},{7,3},{8,12},{9,13},{10,... | collective-permute-start | bytes 221192 | tf_op jit(solution)/shard_map/ppermute | solution.py:27
  68.0 6.3 %collective-permute-start.21 = (s16[144,256]{1,0:T(8,128)(2,1)S(1)}, s16[144,256]{1,0:T(8,128)(2,1)S(1)}, u32[]{:S(2)}, u32[]{:S(2)}) collective-permute-start(s16[144,256]{1,0:T(8,128)(2,1)S(1)} %get-tuple-element.115), channel_id=1, source_target_pairs={{0,6},{1,7},{2,4},{3,5},{4,2},{5,3},{6,0},{7,1},{8,14},{9,15},{10,... | collective-permute-start | bytes 221192 | tf_op jit(solution)/shard_map/ppermute | solution.py:27
  70.4 8.3 %collective-permute-start.26 = (s16[528,256]{1,0:T(8,128)(2,1)S(1)}, s16[528,256]{1,0:T(8,128)(2,1)S(1)}, u32[]{:S(2)}, u32[]{:S(2)}) collective-permute-start(s16[528,256]{1,0:T(8,128)(2,1)S(1)} %get-tuple-element.117), channel_id=1, source_target_pairs={{0,16},{8,24},{16,0},{24,8},{1,17},{9,25},{17,1},{25,9},{2,18},{10... | collective-permute-start | bytes 811016 | tf_op jit(solution)/shard_map/ppermute | solution.py:27
  74.3 7.3 %collective-permute-start.25 = (bf16[128,256]{1,0:T(8,128)(2,1)S(1)}, bf16[128,256]{1,0:T(8,128)(2,1)S(1)}, u32[]{:S(2)}, u32[]{:S(2)}) collective-permute-start(bf16[128,256]{1,0:T(8,128)(2,1)S(1)} %finish.10.refs_5_.refs_1_), channel_id=1, source_target_pairs={{0,6},{1,7},{2,4},{3,5},{4,2},{5,3},{6,0},{7,1},{8,14},{9,15},{10,... | collective-permute-start | bytes 196616 | tf_op jit(solution)/shard_map/ppermute | solution.py:27
  80.1 7.6 %collective-permute-start.28 = (s16[528,256]{1,0:T(8,128)(2,1)S(1)}, s16[528,256]{1,0:T(8,128)(2,1)S(1)}, u32[]{:S(2)}, u32[]{:S(2)}) collective-permute-start(s16[528,256]{1,0:T(8,128)(2,1)S(1)} %get-tuple-element.119), channel_id=1, source_target_pairs={{0,1},{1,0},{2,3},{3,2},{4,5},{5,4},{6,7},{7,6},{8,9},{9,8},{10,11... | collective-permute-start | bytes 811016 | tf_op jit(solution)/shard_map/ppermute | solution.py:27
  82.2 10.2 %collective-permute-start.27 = (bf16[4,128,256]{2,1,0:T(8,128)(2,1)S(1)}, bf16[4,128,256]{2,1,0:T(8,128)(2,1)S(1)}, u32[]{:S(2)}, u32[]{:S(2)}) collective-permute-start(bf16[4,128,256]{2,1,0:T(8,128)(2,1)S(1)} %order.10.refs_3_.refs_4_), channel_id=1, source_target_pairs={{0,1},{1,0},{2,3},{3,2},{4,5},{5,4},{6,7},{7,6},{8,9},{9,8},{10,11... | collective-permute-start | bytes 786440 | tf_op jit(solution)/shard_map/ppermute | solution.py:27
  88.0 6.3 %collective-permute-start.30 = (s16[144,256]{1,0:T(8,128)(2,1)S(1)}, s16[144,256]{1,0:T(8,128)(2,1)S(1)}, u32[]{:S(2)}, u32[]{:S(2)}) collective-permute-start(s16[144,256]{1,0:T(8,128)(2,1)S(1)} %get-tuple-element.123), channel_id=1, source_target_pairs={{0,2},{1,3},{2,0},{3,1},{4,6},{5,7},{6,4},{7,5},{8,10},{9,11},{10,... | collective-permute-start | bytes 221192 | tf_op jit(solution)/shard_map/ppermute | solution.py:27
  94.2 6.9 %collective-permute-start.29 = (f32[512,256]{1,0:T(8,128)S(1)}, f32[512,256]{1,0:T(8,128)S(1)}, u32[]{:S(2)}, u32[]{:S(2)}) collective-permute-start(f32[512,256]{1,0:T(8,128)S(1)} %get-tuple-element.122.refs_4_.refs_0_), channel_id=1, source_target_pairs={{0,8},{8,0},{16,24},{24,16},{1,9},{9,1},{17,25},{25,17},{2,10},{10... | collective-permute-start | bytes 1572872 | tf_op jit(solution)/shard_map/ppermute | solution.py:27
  96.7 6.3 %collective-permute-start.36 = (bf16[128,256]{1,0:T(8,128)(2,1)S(1)}, bf16[128,256]{1,0:T(8,128)(2,1)S(1)}, u32[]{:S(2)}, u32[]{:S(2)}) collective-permute-start(bf16[128,256]{1,0:T(8,128)(2,1)S(1)} %finish.11.refs_2_.refs_1_), channel_id=1, source_target_pairs={{0,6},{1,7},{2,4},{3,5},{4,2},{5,3},{6,0},{7,1},{8,14},{9,15},{10,... | collective-permute-start | bytes 196616 | tf_op jit(solution)/shard_map/ppermute | solution.py:27
  101.4 6.5 %collective-permute-start.33 = (s16[528,256]{1,0:T(8,128)(2,1)S(1)}, s16[528,256]{1,0:T(8,128)(2,1)S(1)}, u32[]{:S(2)}, u32[]{:S(2)}) collective-permute-start(s16[528,256]{1,0:T(8,128)(2,1)S(1)} %get-tuple-element.127), channel_id=1, source_target_pairs={{0,16},{8,24},{16,0},{24,8},{1,17},{9,25},{17,1},{25,9},{2,18},{10... | collective-permute-start | bytes 811016 | tf_op jit(solution)/shard_map/ppermute | solution.py:27
  104.3 8.9 %collective-permute-start.38 = (bf16[4,128,256]{2,1,0:T(8,128)(2,1)S(1)}, bf16[4,128,256]{2,1,0:T(8,128)(2,1)S(1)}, u32[]{:S(2)}, u32[]{:S(2)}) collective-permute-start(bf16[4,128,256]{2,1,0:T(8,128)(2,1)S(1)} %order.11.refs_5_.refs_4_), channel_id=1, source_target_pairs={{0,1},{1,0},{2,3},{3,2},{4,5},{5,4},{6,7},{7,6},{8,9},{9,8},{10,11... | collective-permute-start | bytes 786440 | tf_op jit(solution)/shard_map/ppermute | solution.py:27
  109.2 7.3 %collective-permute-start.37 = (s16[528,256]{1,0:T(8,128)(2,1)S(1)}, s16[528,256]{1,0:T(8,128)(2,1)S(1)}, u32[]{:S(2)}, u32[]{:S(2)}) collective-permute-start(s16[528,256]{1,0:T(8,128)(2,1)S(1)} %get-tuple-element.129), channel_id=1, source_target_pairs={{0,1},{1,0},{2,3},{3,2},{4,5},{5,4},{6,7},{7,6},{8,9},{9,8},{10,11... | collective-permute-start | bytes 811016 | tf_op jit(solution)/shard_map/ppermute | solution.py:27
  114.9 6.3 %collective-permute-start.42 = (f32[512,256]{1,0:T(8,128)S(1)}, f32[512,256]{1,0:T(8,128)S(1)}, u32[]{:S(2)}, u32[]{:S(2)}) collective-permute-start(f32[512,256]{1,0:T(8,128)S(1)} %get-tuple-element.131.refs_3_.refs_0_), channel_id=1, source_target_pairs={{0,8},{8,0},{16,24},{24,16},{1,9},{9,1},{17,25},{25,17},{2,10},{10... | collective-permute-start | bytes 1572872 | tf_op jit(solution)/shard_map/ppermute | solution.py:27
  116.7 6.3 %collective-permute-start.39 = (s16[144,256]{1,0:T(8,128)(2,1)S(1)}, s16[144,256]{1,0:T(8,128)(2,1)S(1)}, u32[]{:S(2)}, u32[]{:S(2)}) collective-permute-start(s16[144,256]{1,0:T(8,128)(2,1)S(1)} %get-tuple-element.133), channel_id=1, source_target_pairs={{0,2},{1,3},{2,0},{3,1},{4,6},{5,7},{6,4},{7,5},{8,10},{9,11},{10,... | collective-permute-start | bytes 221192 | tf_op jit(solution)/shard_map/ppermute | solution.py:27
  117.3 7.4 %collective-permute-start.40 = (s16[144,256]{1,0:T(8,128)(2,1)S(1)}, s16[144,256]{1,0:T(8,128)(2,1)S(1)}, u32[]{:S(2)}, u32[]{:S(2)}) collective-permute-start(s16[144,256]{1,0:T(8,128)(2,1)S(1)} %get-tuple-element.134), channel_id=1, source_target_pairs={{0,4},{1,5},{2,6},{3,7},{4,0},{5,1},{6,2},{7,3},{8,12},{9,13},{10,... | collective-permute-start | bytes 221192 | tf_op jit(solution)/shard_map/ppermute | solution.py:27
  119.4 6.3 %collective-permute-start.41 = (s16[144,256]{1,0:T(8,128)(2,1)S(1)}, s16[144,256]{1,0:T(8,128)(2,1)S(1)}, u32[]{:S(2)}, u32[]{:S(2)}) collective-permute-start(s16[144,256]{1,0:T(8,128)(2,1)S(1)} %get-tuple-element.135), channel_id=1, source_target_pairs={{0,6},{1,7},{2,4},{3,5},{4,2},{5,3},{6,0},{7,1},{8,14},{9,15},{10,... | collective-permute-start | bytes 221192 | tf_op jit(solution)/shard_map/ppermute | solution.py:27
  121.4 8.8 %collective-permute-start.46 = (s16[528,256]{1,0:T(8,128)(2,1)S(1)}, s16[528,256]{1,0:T(8,128)(2,1)S(1)}, u32[]{:S(2)}, u32[]{:S(2)}) collective-permute-start(s16[528,256]{1,0:T(8,128)(2,1)S(1)} %get-tuple-element.137), channel_id=1, source_target_pairs={{0,16},{8,24},{16,0},{24,8},{1,17},{9,25},{17,1},{25,9},{2,18},{10... | collective-permute-start | bytes 811016 | tf_op jit(solution)/shard_map/ppermute | solution.py:27
  125.7 7.5 %collective-permute-start.45 = (bf16[128,256]{1,0:T(8,128)(2,1)S(1)}, bf16[128,256]{1,0:T(8,128)(2,1)S(1)}, u32[]{:S(2)}, u32[]{:S(2)}) collective-permute-start(bf16[128,256]{1,0:T(8,128)(2,1)S(1)} %finish.12.refs_5_.refs_1_), channel_id=1, source_target_pairs={{0,6},{1,7},{2,4},{3,5},{4,2},{5,3},{6,0},{7,1},{8,14},{9,15},{10,... | collective-permute-start | bytes 196616 | tf_op jit(solution)/shard_map/ppermute | solution.py:27
  131.7 8.0 %collective-permute-start.48 = (s16[528,256]{1,0:T(8,128)(2,1)S(1)}, s16[528,256]{1,0:T(8,128)(2,1)S(1)}, u32[]{:S(2)}, u32[]{:S(2)}) collective-permute-start(s16[528,256]{1,0:T(8,128)(2,1)S(1)} %get-tuple-element.139), channel_id=1, source_target_pairs={{0,1},{1,0},{2,3},{3,2},{4,5},{5,4},{6,7},{7,6},{8,9},{9,8},{10,11... | collective-permute-start | bytes 811016 | tf_op jit(solution)/shard_map/ppermute | solution.py:27
  133.4 11.0 %collective-permute-start.47 = (bf16[4,128,256]{2,1,0:T(8,128)(2,1)S(1)}, bf16[4,128,256]{2,1,0:T(8,128)(2,1)S(1)}, u32[]{:S(2)}, u32[]{:S(2)}) collective-permute-start(bf16[4,128,256]{2,1,0:T(8,128)(2,1)S(1)} %order.12.refs_3_.refs_5_), channel_id=1, source_target_pairs={{0,1},{1,0},{2,3},{3,2},{4,5},{5,4},{6,7},{7,6},{8,9},{9,8},{10,11... | collective-permute-start | bytes 786440 | tf_op jit(solution)/shard_map/ppermute | solution.py:27
  139.9 8.1 %collective-permute-start.50 = (s16[144,256]{1,0:T(8,128)(2,1)S(1)}, s16[144,256]{1,0:T(8,128)(2,1)S(1)}, u32[]{:S(2)}, u32[]{:S(2)}) collective-permute-start(s16[144,256]{1,0:T(8,128)(2,1)S(1)} %get-tuple-element.142), channel_id=1, source_target_pairs={{0,2},{1,3},{2,0},{3,1},{4,6},{5,7},{6,4},{7,5},{8,10},{9,11},{10,... | collective-permute-start | bytes 221192 | tf_op jit(solution)/shard_map/ppermute | solution.py:27
  140.9 7.1 %collective-permute-start.51 = (s16[144,256]{1,0:T(8,128)(2,1)S(1)}, s16[144,256]{1,0:T(8,128)(2,1)S(1)}, u32[]{:S(2)}, u32[]{:S(2)}) collective-permute-start(s16[144,256]{1,0:T(8,128)(2,1)S(1)} %get-tuple-element.143), channel_id=1, source_target_pairs={{0,4},{1,5},{2,6},{3,7},{4,0},{5,1},{6,2},{7,3},{8,12},{9,13},{10,... | collective-permute-start | bytes 221192 | tf_op jit(solution)/shard_map/ppermute | solution.py:27
  142.2 6.3 %collective-permute-start.52 = (s16[144,256]{1,0:T(8,128)(2,1)S(1)}, s16[144,256]{1,0:T(8,128)(2,1)S(1)}, u32[]{:S(2)}, u32[]{:S(2)}) collective-permute-start(s16[144,256]{1,0:T(8,128)(2,1)S(1)} %get-tuple-element.144), channel_id=1, source_target_pairs={{0,6},{1,7},{2,4},{3,5},{4,2},{5,3},{6,0},{7,1},{8,14},{9,15},{10,... | collective-permute-start | bytes 221192 | tf_op jit(solution)/shard_map/ppermute | solution.py:27
  148.6 6.6 %collective-permute-start.56 = (bf16[128,256]{1,0:T(8,128)(2,1)S(1)}, bf16[128,256]{1,0:T(8,128)(2,1)S(1)}, u32[]{:S(2)}, u32[]{:S(2)}) collective-permute-start(bf16[128,256]{1,0:T(8,128)(2,1)S(1)} %finish.13.refs_2_.refs_1_), channel_id=1, source_target_pairs={{0,6},{1,7},{2,4},{3,5},{4,2},{5,3},{6,0},{7,1},{8,14},{9,15},{10,... | collective-permute-start | bytes 196616 | tf_op jit(solution)/shard_map/ppermute | solution.py:27
  150.7 6.5 %collective-permute-start.55 = (bf16[128,256]{1,0:T(8,128)(2,1)S(1)}, bf16[128,256]{1,0:T(8,128)(2,1)S(1)}, u32[]{:S(2)}, u32[]{:S(2)}) collective-permute-start(bf16[128,256]{1,0:T(8,128)(2,1)S(1)} %finish.13.refs_2_.refs_1_), channel_id=1, source_target_pairs={{0,4},{1,5},{2,6},{3,7},{4,0},{5,1},{6,2},{7,3},{8,12},{9,13},{10,... | collective-permute-start | bytes 196616 | tf_op jit(solution)/shard_map/ppermute | solution.py:27
  150.7 6.5 %collective-permute-start.54 = (bf16[128,256]{1,0:T(8,128)(2,1)S(1)}, bf16[128,256]{1,0:T(8,128)(2,1)S(1)}, u32[]{:S(2)}, u32[]{:S(2)}) collective-permute-start(bf16[128,256]{1,0:T(8,128)(2,1)S(1)} %finish.13.refs_2_.refs_1_), channel_id=1, source_target_pairs={{0,2},{1,3},{2,0},{3,1},{4,6},{5,7},{6,4},{7,5},{8,10},{9,11},{10,... | collective-permute-start | bytes 196616 | tf_op jit(solution)/shard_map/ppermute | solution.py:27
  153.3 7.1 %collective-permute-start.53 = (s16[528,256]{1,0:T(8,128)(2,1)S(1)}, s16[528,256]{1,0:T(8,128)(2,1)S(1)}, u32[]{:S(2)}, u32[]{:S(2)}) collective-permute-start(s16[528,256]{1,0:T(8,128)(2,1)S(1)} %get-tuple-element.146), channel_id=1, source_target_pairs={{0,16},{8,24},{16,0},{24,8},{1,17},{9,25},{17,1},{25,9},{2,18},{10... | collective-permute-start | bytes 811016 | tf_op jit(solution)/shard_map/ppermute | solution.py:27
  157.2 9.3 %collective-permute-start.58 = (bf16[4,128,256]{2,1,0:T(8,128)(2,1)S(1)}, bf16[4,128,256]{2,1,0:T(8,128)(2,1)S(1)}, u32[]{:S(2)}, u32[]{:S(2)}) collective-permute-start(bf16[4,128,256]{2,1,0:T(8,128)(2,1)S(1)} %order.13.refs_5_), channel_id=1, source_target_pairs={{0,1},{1,0},{2,3},{3,2},{4,5},{5,4},{6,7},{7,6},{8,9},{9,8},{10,11... | collective-permute-start | bytes 786440 | tf_op jit(solution)/shard_map/ppermute | solution.py:27
  161.7 9.9 %collective-permute-start.57 = (s16[528,256]{1,0:T(8,128)(2,1)S(1)}, s16[528,256]{1,0:T(8,128)(2,1)S(1)}, u32[]{:S(2)}, u32[]{:S(2)}) collective-permute-start(s16[528,256]{1,0:T(8,128)(2,1)S(1)} %get-tuple-element.148), channel_id=1, source_target_pairs={{0,1},{1,0},{2,3},{3,2},{4,5},{5,4},{6,7},{7,6},{8,9},{9,8},{10,11... | collective-permute-start | bytes 811016 | tf_op jit(solution)/shard_map/ppermute | solution.py:27
  169.2 7.1 %collective-permute-start.62 = (f32[512,256]{1,0:T(8,128)S(1)}, f32[512,256]{1,0:T(8,128)S(1)}, u32[]{:S(2)}, u32[]{:S(2)}) collective-permute-start(f32[512,256]{1,0:T(8,128)S(1)} %get-tuple-element.150.refs_3_.refs_0_), channel_id=1, source_target_pairs={{0,8},{8,0},{16,24},{24,16},{1,9},{9,1},{17,25},{25,17},{2,10},{10... | collective-permute-start | bytes 1572872 | tf_op jit(solution)/shard_map/ppermute | solution.py:27
  171.9 10.2 %collective-permute-start.59 = (s16[144,256]{1,0:T(8,128)(2,1)S(1)}, s16[144,256]{1,0:T(8,128)(2,1)S(1)}, u32[]{:S(2)}, u32[]{:S(2)}) collective-permute-start(s16[144,256]{1,0:T(8,128)(2,1)S(1)} %get-tuple-element.152), channel_id=1, source_target_pairs={{0,2},{1,3},{2,0},{3,1},{4,6},{5,7},{6,4},{7,5},{8,10},{9,11},{10,... | collective-permute-start | bytes 221192 | tf_op jit(solution)/shard_map/ppermute | solution.py:27
  172.0 10.1 %collective-permute-start.60 = (s16[144,256]{1,0:T(8,128)(2,1)S(1)}, s16[144,256]{1,0:T(8,128)(2,1)S(1)}, u32[]{:S(2)}, u32[]{:S(2)}) collective-permute-start(s16[144,256]{1,0:T(8,128)(2,1)S(1)} %get-tuple-element.153), channel_id=1, source_target_pairs={{0,4},{1,5},{2,6},{3,7},{4,0},{5,1},{6,2},{7,3},{8,12},{9,13},{10,... | collective-permute-start | bytes 221192 | tf_op jit(solution)/shard_map/ppermute | solution.py:27
  173.2 8.9 %collective-permute-start.61 = (s16[144,256]{1,0:T(8,128)(2,1)S(1)}, s16[144,256]{1,0:T(8,128)(2,1)S(1)}, u32[]{:S(2)}, u32[]{:S(2)}) collective-permute-start(s16[144,256]{1,0:T(8,128)(2,1)S(1)} %get-tuple-element.154), channel_id=1, source_target_pairs={{0,6},{1,7},{2,4},{3,5},{4,2},{5,3},{6,0},{7,1},{8,14},{9,15},{10,... | collective-permute-start | bytes 221192 | tf_op jit(solution)/shard_map/ppermute | solution.py:27
  176.6 10.1 %collective-permute-start.66 = (s16[528,256]{1,0:T(8,128)(2,1)S(1)}, s16[528,256]{1,0:T(8,128)(2,1)S(1)}, u32[]{:S(2)}, u32[]{:S(2)}) collective-permute-start(s16[528,256]{1,0:T(8,128)(2,1)S(1)} %get-tuple-element.158), channel_id=1, source_target_pairs={{0,16},{8,24},{16,0},{24,8},{1,17},{9,25},{17,1},{25,9},{2,18},{10... | collective-permute-start | bytes 811016 | tf_op jit(solution)/shard_map/ppermute | solution.py:27
  182.2 10.6 %collective-permute-start.65 = (bf16[128,256]{1,0:T(8,128)(2,1)S(1)}, bf16[128,256]{1,0:T(8,128)(2,1)S(1)}, u32[]{:S(2)}, u32[]{:S(2)}) collective-permute-start(bf16[128,256]{1,0:T(8,128)(2,1)S(1)} %finish.14.refs_5_.refs_1_), channel_id=1, source_target_pairs={{0,6},{1,7},{2,4},{3,5},{4,2},{5,3},{6,0},{7,1},{8,14},{9,15},{10,... | collective-permute-start | bytes 196616 | tf_op jit(solution)/shard_map/ppermute | solution.py:27
  183.4 9.3 %collective-permute-start.64 = (bf16[128,256]{1,0:T(8,128)(2,1)S(1)}, bf16[128,256]{1,0:T(8,128)(2,1)S(1)}, u32[]{:S(2)}, u32[]{:S(2)}) collective-permute-start(bf16[128,256]{1,0:T(8,128)(2,1)S(1)} %finish.14.refs_5_.refs_1_), channel_id=1, source_target_pairs={{0,4},{1,5},{2,6},{3,7},{4,0},{5,1},{6,2},{7,3},{8,12},{9,13},{10,... | collective-permute-start | bytes 196616 | tf_op jit(solution)/shard_map/ppermute | solution.py:27
  184.6 8.2 %collective-permute-start.63 = (bf16[128,256]{1,0:T(8,128)(2,1)S(1)}, bf16[128,256]{1,0:T(8,128)(2,1)S(1)}, u32[]{:S(2)}, u32[]{:S(2)}) collective-permute-start(bf16[128,256]{1,0:T(8,128)(2,1)S(1)} %finish.14.refs_5_.refs_1_), channel_id=1, source_target_pairs={{0,2},{1,3},{2,0},{3,1},{4,6},{5,7},{6,4},{7,5},{8,10},{9,11},{10,... | collective-permute-start | bytes 196616 | tf_op jit(solution)/shard_map/ppermute | solution.py:27
  188.0 8.2 %collective-permute-start.68 = (s16[528,256]{1,0:T(8,128)(2,1)S(1)}, s16[528,256]{1,0:T(8,128)(2,1)S(1)}, u32[]{:S(2)}, u32[]{:S(2)}) collective-permute-start(s16[528,256]{1,0:T(8,128)(2,1)S(1)} %get-tuple-element.161), channel_id=1, source_target_pairs={{0,1},{1,0},{2,3},{3,2},{4,5},{5,4},{6,7},{7,6},{8,9},{9,8},{10,11... | collective-permute-start | bytes 811016 | tf_op jit(solution)/shard_map/ppermute | solution.py:27
  192.8 8.0 %collective-permute-start.67 = (bf16[4,128,256]{2,1,0:T(8,128)(2,1)S(1)}, bf16[4,128,256]{2,1,0:T(8,128)(2,1)S(1)}, u32[]{:S(2)}, u32[]{:S(2)}) collective-permute-start(bf16[4,128,256]{2,1,0:T(8,128)(2,1)S(1)} %order.14.refs_3_.refs_1_), channel_id=1, source_target_pairs={{0,1},{1,0},{2,3},{3,2},{4,5},{5,4},{6,7},{7,6},{8,9},{9,8},{10,11... | collective-permute-start | bytes 786440 | tf_op jit(solution)/shard_map/ppermute | solution.py:27
  196.4 10.7 %collective-permute-start.69 = (s16[144,256]{1,0:T(8,128)(2,1)S(1)}, s16[144,256]{1,0:T(8,128)(2,1)S(1)}, u32[]{:S(2)}, u32[]{:S(2)}) collective-permute-start(s16[144,256]{1,0:T(8,128)(2,1)S(1)} %get-tuple-element.163), channel_id=1, source_target_pairs={{0,2},{1,3},{2,0},{3,1},{4,6},{5,7},{6,4},{7,5},{8,10},{9,11},{10,... | collective-permute-start | bytes 221192 | tf_op jit(solution)/shard_map/ppermute | solution.py:27
  196.7 10.3 %collective-permute-start.70 = (s16[144,256]{1,0:T(8,128)(2,1)S(1)}, s16[144,256]{1,0:T(8,128)(2,1)S(1)}, u32[]{:S(2)}, u32[]{:S(2)}) collective-permute-start(s16[144,256]{1,0:T(8,128)(2,1)S(1)} %get-tuple-element.164), channel_id=1, source_target_pairs={{0,4},{1,5},{2,6},{3,7},{4,0},{5,1},{6,2},{7,3},{8,12},{9,13},{10,... | collective-permute-start | bytes 221192 | tf_op jit(solution)/shard_map/ppermute | solution.py:27
  197.8 9.2 %collective-permute-start.71 = (s16[144,256]{1,0:T(8,128)(2,1)S(1)}, s16[144,256]{1,0:T(8,128)(2,1)S(1)}, u32[]{:S(2)}, u32[]{:S(2)}) collective-permute-start(s16[144,256]{1,0:T(8,128)(2,1)S(1)} %get-tuple-element.165), channel_id=1, source_target_pairs={{0,6},{1,7},{2,4},{3,5},{4,2},{5,3},{6,0},{7,1},{8,14},{9,15},{10,... | collective-permute-start | bytes 221192 | tf_op jit(solution)/shard_map/ppermute | solution.py:27
  206.9 9.4 %collective-permute-start.75 = (bf16[8,128,256]{2,1,0:T(8,128)(2,1)S(1)}, bf16[8,128,256]{2,1,0:T(8,128)(2,1)S(1)}, u32[]{:S(2)}, u32[]{:S(2)}) collective-permute-start(bf16[8,128,256]{2,1,0:T(8,128)(2,1)S(1)} %get-tuple-element.169), channel_id=1, source_target_pairs={{0,8},{8,0},{16,24},{24,16},{1,9},{9,1},{17,25},{25,17},{2,10},{10... | collective-permute-start | bytes 1572872 | tf_op jit(solution)/shard_map/ppermute | solution.py:27
  207.1 10.9 %collective-permute-start.74 = (bf16[128,256]{1,0:T(8,128)(2,1)S(1)}, bf16[128,256]{1,0:T(8,128)(2,1)S(1)}, u32[]{:S(2)}, u32[]{:S(2)}) collective-permute-start(bf16[128,256]{1,0:T(8,128)(2,1)S(1)} %finish.15.refs_9_.refs_1_), channel_id=1, source_target_pairs={{0,6},{1,7},{2,4},{3,5},{4,2},{5,3},{6,0},{7,1},{8,14},{9,15},{10,... | collective-permute-start | bytes 196616 | tf_op jit(solution)/shard_map/ppermute | solution.py:27
  208.2 9.9 %collective-permute-start.73 = (bf16[128,256]{1,0:T(8,128)(2,1)S(1)}, bf16[128,256]{1,0:T(8,128)(2,1)S(1)}, u32[]{:S(2)}, u32[]{:S(2)}) collective-permute-start(bf16[128,256]{1,0:T(8,128)(2,1)S(1)} %finish.15.refs_9_.refs_1_), channel_id=1, source_target_pairs={{0,4},{1,5},{2,6},{3,7},{4,0},{5,1},{6,2},{7,3},{8,12},{9,13},{10,... | collective-permute-start | bytes 196616 | tf_op jit(solution)/shard_map/ppermute | solution.py:27
  209.3 8.7 %collective-permute-start.72 = (bf16[128,256]{1,0:T(8,128)(2,1)S(1)}, bf16[128,256]{1,0:T(8,128)(2,1)S(1)}, u32[]{:S(2)}, u32[]{:S(2)}) collective-permute-start(bf16[128,256]{1,0:T(8,128)(2,1)S(1)} %finish.15.refs_9_.refs_1_), channel_id=1, source_target_pairs={{0,2},{1,3},{2,0},{3,1},{4,6},{5,7},{6,4},{7,5},{8,10},{9,11},{10,... | collective-permute-start | bytes 196616 | tf_op jit(solution)/shard_map/ppermute | solution.py:27
  217.3 25.2 %collective-permute-start.81 = (bf16[8,128,256]{2,1,0:T(8,128)(2,1)}, bf16[8,128,256]{2,1,0:T(8,128)(2,1)}, u32[]{:S(2)}, u32[]{:S(2)}) collective-permute-start(bf16[8,128,256]{2,1,0:T(8,128)(2,1)} %add.35.refs_5_), channel_id=1, source_target_pairs={{0,16},{8,24},{16,0},{24,8},{1,17},{9,25},{17,1},{25,9},{2,18},{10... | collective-permute-start | bytes 1572872 | tf_op jit(solution)/shard_map/ppermute | solution.py:27
  218.1 7.6 %collective-permute-start.76 = (bf16[4,128,256]{2,1,0:T(8,128)(2,1)S(1)}, bf16[4,128,256]{2,1,0:T(8,128)(2,1)S(1)}, u32[]{:S(2)}, u32[]{:S(2)}) collective-permute-start(bf16[4,128,256]{2,1,0:T(8,128)(2,1)S(1)} %order.15.refs_9_.refs_1_), channel_id=1, source_target_pairs={{0,1},{1,0},{2,3},{3,2},{4,5},{5,4},{6,7},{7,6},{8,9},{9,8},{10,11... | collective-permute-start | bytes 786440 | tf_op jit(solution)/shard_map/ppermute | solution.py:27
  224.4 18.2 %collective-permute-start.80 = (bf16[8,128,256]{2,1,0:T(8,128)(2,1)S(1)}, bf16[8,128,256]{2,1,0:T(8,128)(2,1)S(1)}, u32[]{:S(2)}, u32[]{:S(2)}) collective-permute-start(bf16[8,128,256]{2,1,0:T(8,128)(2,1)S(1)} %get-tuple-element.183), channel_id=1, source_target_pairs={{0,8},{8,0},{16,24},{24,16},{1,9},{9,1},{17,25},{25,17},{2,10},{10... | collective-permute-start | bytes 1572872 | tf_op jit(solution)/shard_map/ppermute | solution.py:27
  231.3 19.0 %collective-permute-start.79 = (bf16[8,128,256]{2,1,0:T(8,128)(2,1)S(1)}, bf16[8,128,256]{2,1,0:T(8,128)(2,1)S(1)}, u32[]{:S(2)}, u32[]{:S(2)}) collective-permute-start(bf16[8,128,256]{2,1,0:T(8,128)(2,1)S(1)} %add.36.refs_9_), channel_id=1, source_target_pairs={{0,16},{8,24},{16,0},{24,8},{1,17},{9,25},{17,1},{25,9},{2,18},{10... | collective-permute-start | bytes 1572872 | tf_op jit(solution)/shard_map/ppermute | solution.py:27
  242.2 8.1 %collective-permute-start.78 = (bf16[8,128,256]{2,1,0:T(8,128)(2,1)S(1)}, bf16[8,128,256]{2,1,0:T(8,128)(2,1)S(1)}, u32[]{:S(2)}, u32[]{:S(2)}) collective-permute-start(bf16[8,128,256]{2,1,0:T(8,128)(2,1)S(1)} %get-tuple-element.181), channel_id=1, source_target_pairs={{0,8},{8,0},{16,24},{24,16},{1,9},{9,1},{17,25},{25,17},{2,10},{10... | collective-permute-start | bytes 1572872 | tf_op jit(solution)/shard_map/ppermute | solution.py:27
  (38 other events, 348.8 us)
